TPU v7x, 32 devices: a whole 2x2x4 slice. The times are simulated.
32 devices in a mesh: sec: 4 (over y, x), xs: 8 (over z, core).
Axes of the slice: x: 2, y: 2, z: 4, core: 2. Of those that a mesh axis runs over, the one named last changes fastest.
Arguments:
- soot: float32 [96, 128, 1024], P('sec', 'xs'), may hold values from 0.05 to 1
- species: float32 [40, 128, 1024], P(None, 'xs'), may hold values from 0.1 to 1
- kernel: float32 [96, 96], replicated, may hold values from 0.002 to 0.02
- split: float32 [96, 96], replicated, may hold values from 0.2 to 0.8
- target: int32 [96, 96], replicated, may hold values from 0 to 94, as said below
- growth: float32 [96], replicated, may hold values from 0.05 to 0.5
- diffusivity: float32 [40], replicated, may hold values from 0.05 to 0.2
- reaction: float32 [40, 40], replicated, may hold values from -1 to 1
- stoich: float32 [40], replicated, may hold values from -1 to 1
Outputs:
- soot_out: float32 [96, 128, 1024], P('sec', 'xs')
- species_out: float32 [40, 128, 1024], P(None, 'xs')
Inputs may be any that keep to these rules, and one draw needn't show every extreme that they name: target[i, j] = min(max(i, j) + r, 94) with r of 0 to 3.
All inputs are finite; a program needn't handle non-finite values.
Results may differ from a plain program's by a relative error of at most 0.0003.
Values sent between devices are 32-bit elements; how exact they have to be, the bound alone decides.
No kernel may reach another device: no remote copies, remote signals or barrier semaphores. Data moves between devices by JAX's collectives and lax.ppermute only.
A program may use at most 128 MiB of HBM per device.

v0:
```python
import jax
import jax.numpy as jnp
from jax import lax
from jax.sharding import PartitionSpec as P

HI = lax.Precision.HIGHEST


def extended(cells, sides, width):
    for axis, dim in sides:
        count = lax.axis_size(axis)
        ends = count - 1
        head = lax.slice_in_dim(cells, 0, width, axis=dim)
        tail = lax.slice_in_dim(cells, cells.shape[dim] - width, cells.shape[dim], axis=dim)
        cells = jnp.concatenate(
            [
                lax.ppermute(tail, axis, [(i, (i + 1) % count) for i in range(ends)]),
                cells,
                lax.ppermute(head, axis, [((i + 1) % count, i) for i in range(ends)]),
            ],
            axis=dim,
        )
    return cells


def birth_rows(dense, kernel, split, target, first, count):

    def one_target(index):
        weights = (
            0.5
            * kernel
            * (
                split * (target == index).astype(kernel.dtype)
                + (1.0 - split) * (target + 1 == index).astype(kernel.dtype)
            )
        )
        product = jnp.dot(weights, dense, precision=HI)
        return jnp.sum(dense * product, axis=0)

    indices = first + jnp.arange(count)
    return lax.map(one_target, indices)


def shards(soot, species, kernel, split, target, growth, diffusivity, reaction, stoich):
    local_sec, rows, width = soot.shape
    kinds = species.shape[0]
    sections = kernel.shape[0]
    cells = rows * width
    flat = soot.reshape(local_sec, cells)
    acet = species[0].reshape(1, cells)
    whole = lax.all_gather(flat, "sec", axis=0, tiled=True)
    start = lax.axis_index("sec") * local_sec
    birth = birth_rows(whole, kernel, split, target, start, local_sec)
    kernel_rows = lax.dynamic_slice(kernel, (start, jnp.int32(0)), (local_sec, sections))
    loss = flat * jnp.dot(kernel_rows, whole, precision=HI)
    grow_own = lax.dynamic_slice_in_dim(growth, start, local_sec)
    flux = grow_own[:, None] * flat * acet
    before = jnp.maximum(start - 1, 0)
    prev_dense = lax.dynamic_slice(whole, (before, jnp.int32(0)), (1, cells))
    prev_rate = lax.dynamic_slice_in_dim(growth, before, 1)
    present = (start > 0).astype(flat.dtype)
    prev_flux = present * prev_rate[:, None] * prev_dense * acet
    inflow = jnp.concatenate([prev_flux, flux[:-1]], axis=0)
    rate = birth - loss - flux + inflow
    consumption = lax.psum(jnp.sum(flux, axis=0), "sec")
    stacked = jnp.concatenate([soot, species], axis=0)
    padded = extended(stacked, (("xs", 1),), 1)
    middle = jnp.pad(padded[:, 1:-1, :], ((0, 0), (0, 0), (1, 1)))
    beside = padded[:, 2:, :] + padded[:, :-2, :] + middle[:, :, 2:] + middle[:, :, :-2]
    lapl = beside - 4.0 * stacked
    soot_out = soot + 0.1 * lapl[:local_sec] + rate.reshape(soot.shape)
    mixed = jnp.dot(reaction, species.reshape(kinds, cells), precision=HI).reshape(species.shape)
    species_out = (
        species
        + diffusivity[:, None, None] * lapl[local_sec:]
        + mixed
        - stoich[:, None, None] * consumption.reshape(1, rows, width)
    )
    return (soot_out, species_out)


def solution(mesh):
    return jax.shard_map(
        shards,
        mesh=mesh,
        in_specs=(P("sec", "xs", None), P(None, "xs", None), P(), P(), P(), P(), P(), P(), P()),
        out_specs=(P("sec", "xs", None), P(None, "xs", None)),
        check_vma=False,
    )
```

profile of v0, /device:TPU:0, one launch (start us, length us, event | category | flops | bytes accessed | tf_op | source)
XLA Modules:
  0.0 437.6 jit_solution(4388229768553003035)
XLA Ops:
  27.8 10.6 %fusion.22 = f32[64,16,1024]{2,0,1:T(8,128)} fusion(f32[64,16,1024]{2,0,1:T(8,128)} %copy-done.4, f32[64,1,1024]{2,0,1:T(8,128)} %collective-permute-done.1, f32[64,1,1024]{2,0,1:T(8,128)} %collective-permute-done), kind=kLoop, calls=%fused_computation.27 | loop fusion | flops 7340032 | bytes 8912896 | tf_op jit(solution)/shard_map/sub | solution.py:70
  38.4 17.1 %all-reduce.3.cloned.1.call-done = f32[16,1024]{1,0:T(8,128)} async-done(((f32[16,1024]{1,0:T(8,128)}), f32[16,1024]{1,0:T(8,128)}) %all-reduce.3.cloned.1.call-update) | async-done | bytes 65552 | tf_op jit(solution)/shard_map/psum | solution.py:65
  67.3 60.5 %all-gather.2.cloned.1.call-done = f32[96,16384]{1,0:T(8,128)} async-done(((f32[24,16384]{1,0:T(8,128)}), f32[96,16384]{1,0:T(8,128)}) %all-gather.2.cloned.1.call-update) | async-done | bytes 6291472 | tf_op jit(solution)/shard_map/all_gather | solution.py:51
  127.7 291.0 %while.10 = (s32[]{:T(128)}, f32[24,16384]{1,0:T(8,128)}, f32[96,96]{1,0:T(8,128)S(1)}, s32[24]{0:T(128)S(1)}, s32[96,96]{1,0:T(8,128)S(1)}, /*index=5*/f32[96,9...) while((s32[]{:T(128)}, f32[24,16384]{1,0:T(8,128)}, f32[96,96]{1,0:T(8,128)S(1)}, s32[24]{0:T(128)S(1)}, ...), condition=%wide.region_2.3_spmd, body=%wide.region_0.2_spmd.sunk | while | flops 1815151616 | bytes 6598777 | solution.py:41
  152.6 9.5 %fusion.46 = f32[16384]{0:T(1024)S(1)} fusion(f32[96,16384]{1,0:T(8,128)} %get-tuple-element.130, f32[96,96]{1,0:T(8,128)S(1)} %get-tuple-element.129, f32[96,96]{1,0:T(8,128)S(1)} %get-tuple-element.126, s32[96,96]{1,0:T(8,128)S(1)} %get-tuple-element.128, s32[]{:T(128)} %bitcast.43), kind=kOutput, calls=%fused_computation.1.clone.1 | convolution fusion | flops 1815151616 | bytes 6467588 | tf_op jit(solution)/shard_map/while/body/eval_jaxpr/dot_general | solution.py:37
  164.7 9.5 %fusion.46 = f32[16384]{0:T(1024)S(1)} fusion(f32[96,16384]{1,0:T(8,128)} %get-tuple-element.130, f32[96,96]{1,0:T(8,128)S(1)} %get-tuple-element.129, f32[96,96]{1,0:T(8,128)S(1)} %get-tuple-element.126, s32[96,96]{1,0:T(8,128)S(1)} %get-tuple-element.128, s32[]{:T(128)} %bitcast.43), kind=kOutput, calls=%fused_computation.1.clone.1 | convolution fusion | flops 1815151616 | bytes 6467588 | tf_op jit(solution)/shard_map/while/body/eval_jaxpr/dot_general | solution.py:37
  176.9 9.5 %fusion.46 = f32[16384]{0:T(1024)S(1)} fusion(f32[96,16384]{1,0:T(8,128)} %get-tuple-element.130, f32[96,96]{1,0:T(8,128)S(1)} %get-tuple-element.129, f32[96,96]{1,0:T(8,128)S(1)} %get-tuple-element.126, s32[96,96]{1,0:T(8,128)S(1)} %get-tuple-element.128, s32[]{:T(128)} %bitcast.43), kind=kOutput, calls=%fused_computation.1.clone.1 | convolution fusion | flops 1815151616 | bytes 6467588 | tf_op jit(solution)/shard_map/while/body/eval_jaxpr/dot_general | solution.py:37
  189.0 9.5 %fusion.46 = f32[16384]{0:T(1024)S(1)} fusion(f32[96,16384]{1,0:T(8,128)} %get-tuple-element.130, f32[96,96]{1,0:T(8,128)S(1)} %get-tuple-element.129, f32[96,96]{1,0:T(8,128)S(1)} %get-tuple-element.126, s32[96,96]{1,0:T(8,128)S(1)} %get-tuple-element.128, s32[]{:T(128)} %bitcast.43), kind=kOutput, calls=%fused_computation.1.clone.1 | convolution fusion | flops 1815151616 | bytes 6467588 | tf_op jit(solution)/shard_map/while/body/eval_jaxpr/dot_general | solution.py:37
  201.1 9.5 %fusion.46 = f32[16384]{0:T(1024)S(1)} fusion(f32[96,16384]{1,0:T(8,128)} %get-tuple-element.130, f32[96,96]{1,0:T(8,128)S(1)} %get-tuple-element.129, f32[96,96]{1,0:T(8,128)S(1)} %get-tuple-element.126, s32[96,96]{1,0:T(8,128)S(1)} %get-tuple-element.128, s32[]{:T(128)} %bitcast.43), kind=kOutput, calls=%fused_computation.1.clone.1 | convolution fusion | flops 1815151616 | bytes 6467588 | tf_op jit(solution)/shard_map/while/body/eval_jaxpr/dot_general | solution.py:37
  213.2 9.5 %fusion.46 = f32[16384]{0:T(1024)S(1)} fusion(f32[96,16384]{1,0:T(8,128)} %get-tuple-element.130, f32[96,96]{1,0:T(8,128)S(1)} %get-tuple-element.129, f32[96,96]{1,0:T(8,128)S(1)} %get-tuple-element.126, s32[96,96]{1,0:T(8,128)S(1)} %get-tuple-element.128, s32[]{:T(128)} %bitcast.43), kind=kOutput, calls=%fused_computation.1.clone.1 | convolution fusion | flops 1815151616 | bytes 6467588 | tf_op jit(solution)/shard_map/while/body/eval_jaxpr/dot_general | solution.py:37
  225.4 9.5 %fusion.46 = f32[16384]{0:T(1024)S(1)} fusion(f32[96,16384]{1,0:T(8,128)} %get-tuple-element.130, f32[96,96]{1,0:T(8,128)S(1)} %get-tuple-element.129, f32[96,96]{1,0:T(8,128)S(1)} %get-tuple-element.126, s32[96,96]{1,0:T(8,128)S(1)} %get-tuple-element.128, s32[]{:T(128)} %bitcast.43), kind=kOutput, calls=%fused_computation.1.clone.1 | convolution fusion | flops 1815151616 | bytes 6467588 | tf_op jit(solution)/shard_map/while/body/eval_jaxpr/dot_general | solution.py:37
  249.6 9.5 %fusion.46 = f32[16384]{0:T(1024)S(1)} fusion(f32[96,16384]{1,0:T(8,128)} %get-tuple-element.130, f32[96,96]{1,0:T(8,128)S(1)} %get-tuple-element.129, f32[96,96]{1,0:T(8,128)S(1)} %get-tuple-element.126, s32[96,96]{1,0:T(8,128)S(1)} %get-tuple-element.128, s32[]{:T(128)} %bitcast.43), kind=kOutput, calls=%fused_computation.1.clone.1 | convolution fusion | flops 1815151616 | bytes 6467588 | tf_op jit(solution)/shard_map/while/body/eval_jaxpr/dot_general | solution.py:37
  261.7 9.5 %fusion.46 = f32[16384]{0:T(1024)S(1)} fusion(f32[96,16384]{1,0:T(8,128)} %get-tuple-element.130, f32[96,96]{1,0:T(8,128)S(1)} %get-tuple-element.129, f32[96,96]{1,0:T(8,128)S(1)} %get-tuple-element.126, s32[96,96]{1,0:T(8,128)S(1)} %get-tuple-element.128, s32[]{:T(128)} %bitcast.43), kind=kOutput, calls=%fused_computation.1.clone.1 | convolution fusion | flops 1815151616 | bytes 6467588 | tf_op jit(solution)/shard_map/while/body/eval_jaxpr/dot_general | solution.py:37
  273.9 9.5 %fusion.46 = f32[16384]{0:T(1024)S(1)} fusion(f32[96,16384]{1,0:T(8,128)} %get-tuple-element.130, f32[96,96]{1,0:T(8,128)S(1)} %get-tuple-element.129, f32[96,96]{1,0:T(8,128)S(1)} %get-tuple-element.126, s32[96,96]{1,0:T(8,128)S(1)} %get-tuple-element.128, s32[]{:T(128)} %bitcast.43), kind=kOutput, calls=%fused_computation.1.clone.1 | convolution fusion | flops 1815151616 | bytes 6467588 | tf_op jit(solution)/shard_map/while/body/eval_jaxpr/dot_general | solution.py:37
  286.0 9.5 %fusion.46 = f32[16384]{0:T(1024)S(1)} fusion(f32[96,16384]{1,0:T(8,128)} %get-tuple-element.130, f32[96,96]{1,0:T(8,128)S(1)} %get-tuple-element.129, f32[96,96]{1,0:T(8,128)S(1)} %get-tuple-element.126, s32[96,96]{1,0:T(8,128)S(1)} %get-tuple-element.128, s32[]{:T(128)} %bitcast.43), kind=kOutput, calls=%fused_computation.1.clone.1 | convolution fusion | flops 1815151616 | bytes 6467588 | tf_op jit(solution)/shard_map/while/body/eval_jaxpr/dot_general | solution.py:37
  298.1 9.5 %fusion.46 = f32[16384]{0:T(1024)S(1)} fusion(f32[96,16384]{1,0:T(8,128)} %get-tuple-element.130, f32[96,96]{1,0:T(8,128)S(1)} %get-tuple-element.129, f32[96,96]{1,0:T(8,128)S(1)} %get-tuple-element.126, s32[96,96]{1,0:T(8,128)S(1)} %get-tuple-element.128, s32[]{:T(128)} %bitcast.43), kind=kOutput, calls=%fused_computation.1.clone.1 | convolution fusion | flops 1815151616 | bytes 6467588 | tf_op jit(solution)/shard_map/while/body/eval_jaxpr/dot_general | solution.py:37
  310.2 9.5 %fusion.46 = f32[16384]{0:T(1024)S(1)} fusion(f32[96,16384]{1,0:T(8,128)} %get-tuple-element.130, f32[96,96]{1,0:T(8,128)S(1)} %get-tuple-element.129, f32[96,96]{1,0:T(8,128)S(1)} %get-tuple-element.126, s32[96,96]{1,0:T(8,128)S(1)} %get-tuple-element.128, s32[]{:T(128)} %bitcast.43), kind=kOutput, calls=%fused_computation.1.clone.1 | convolution fusion | flops 1815151616 | bytes 6467588 | tf_op jit(solution)/shard_map/while/body/eval_jaxpr/dot_general | solution.py:37
  322.4 9.5 %fusion.46 = f32[16384]{0:T(1024)S(1)} fusion(f32[96,16384]{1,0:T(8,128)} %get-tuple-element.130, f32[96,96]{1,0:T(8,128)S(1)} %get-tuple-element.129, f32[96,96]{1,0:T(8,128)S(1)} %get-tuple-element.126, s32[96,96]{1,0:T(8,128)S(1)} %get-tuple-element.128, s32[]{:T(128)} %bitcast.43), kind=kOutput, calls=%fused_computation.1.clone.1 | convolution fusion | flops 1815151616 | bytes 6467588 | tf_op jit(solution)/shard_map/while/body/eval_jaxpr/dot_general | solution.py:37
  346.6 9.5 %fusion.46 = f32[16384]{0:T(1024)S(1)} fusion(f32[96,16384]{1,0:T(8,128)} %get-tuple-element.130, f32[96,96]{1,0:T(8,128)S(1)} %get-tuple-element.129, f32[96,96]{1,0:T(8,128)S(1)} %get-tuple-element.126, s32[96,96]{1,0:T(8,128)S(1)} %get-tuple-element.128, s32[]{:T(128)} %bitcast.43), kind=kOutput, calls=%fused_computation.1.clone.1 | convolution fusion | flops 1815151616 | bytes 6467588 | tf_op jit(solution)/shard_map/while/body/eval_jaxpr/dot_general | solution.py:37
  358.7 9.5 %fusion.46 = f32[16384]{0:T(1024)S(1)} fusion(f32[96,16384]{1,0:T(8,128)} %get-tuple-element.130, f32[96,96]{1,0:T(8,128)S(1)} %get-tuple-element.129, f32[96,96]{1,0:T(8,128)S(1)} %get-tuple-element.126, s32[96,96]{1,0:T(8,128)S(1)} %get-tuple-element.128, s32[]{:T(128)} %bitcast.43), kind=kOutput, calls=%fused_computation.1.clone.1 | convolution fusion | flops 1815151616 | bytes 6467588 | tf_op jit(solution)/shard_map/while/body/eval_jaxpr/dot_general | solution.py:37
  370.8 9.5 %fusion.46 = f32[16384]{0:T(1024)S(1)} fusion(f32[96,16384]{1,0:T(8,128)} %get-tuple-element.130, f32[96,96]{1,0:T(8,128)S(1)} %get-tuple-element.129, f32[96,96]{1,0:T(8,128)S(1)} %get-tuple-element.126, s32[96,96]{1,0:T(8,128)S(1)} %get-tuple-element.128, s32[]{:T(128)} %bitcast.43), kind=kOutput, calls=%fused_computation.1.clone.1 | convolution fusion | flops 1815151616 | bytes 6467588 | tf_op jit(solution)/shard_map/while/body/eval_jaxpr/dot_general | solution.py:37
  383.0 9.5 %fusion.46 = f32[16384]{0:T(1024)S(1)} fusion(f32[96,16384]{1,0:T(8,128)} %get-tuple-element.130, f32[96,96]{1,0:T(8,128)S(1)} %get-tuple-element.129, f32[96,96]{1,0:T(8,128)S(1)} %get-tuple-element.126, s32[96,96]{1,0:T(8,128)S(1)} %get-tuple-element.128, s32[]{:T(128)} %bitcast.43), kind=kOutput, calls=%fused_computation.1.clone.1 | convolution fusion | flops 1815151616 | bytes 6467588 | tf_op jit(solution)/shard_map/while/body/eval_jaxpr/dot_general | solution.py:37
  395.1 9.5 %fusion.46 = f32[16384]{0:T(1024)S(1)} fusion(f32[96,16384]{1,0:T(8,128)} %get-tuple-element.130, f32[96,96]{1,0:T(8,128)S(1)} %get-tuple-element.129, f32[96,96]{1,0:T(8,128)S(1)} %get-tuple-element.126, s32[96,96]{1,0:T(8,128)S(1)} %get-tuple-element.128, s32[]{:T(128)} %bitcast.43), kind=kOutput, calls=%fused_computation.1.clone.1 | convolution fusion | flops 1815151616 | bytes 6467588 | tf_op jit(solution)/shard_map/while/body/eval_jaxpr/dot_general | solution.py:37
  407.2 9.5 %fusion.46 = f32[16384]{0:T(1024)S(1)} fusion(f32[96,16384]{1,0:T(8,128)} %get-tuple-element.130, f32[96,96]{1,0:T(8,128)S(1)} %get-tuple-element.129, f32[96,96]{1,0:T(8,128)S(1)} %get-tuple-element.126, s32[96,96]{1,0:T(8,128)S(1)} %get-tuple-element.128, s32[]{:T(128)} %bitcast.43), kind=kOutput, calls=%fused_computation.1.clone.1 | convolution fusion | flops 1815151616 | bytes 6467588 | tf_op jit(solution)/shard_map/while/body/eval_jaxpr/dot_general | solution.py:37
  (101 shorter events, 144.0 us)
Async XLA Ops:
  7.2 48.4 %copy-start = (f32[40,40]{1,0:T(8,128)S(1)}, f32[40,40]{1,0:T(8,128)}, u32[]{:S(2)}) copy-start(f32[40,40]{1,0:T(8,128)} %param.18) | copy-start | bytes 19204
  7.2 4.1 copy-start.1
  7.2 48.4 %all-reduce.3.cloned.1.call-start = ((), (), s32[]{:S(2)}) async-start(), calls=%async_computation.1 | async-start | bytes 131072 | tf_op jit(solution)/shard_map/psum | solution.py:65
  11.2 116.5 %all-gather.2.cloned.1.call-start = ((), (), s32[]{:S(2)}) async-start(), calls=%async_computation | async-start | bytes 7864320 | tf_op jit(solution)/shard_map/all_gather | solution.py:51
  13.4 1.7 copy-start.3
  15.1 9.0 %copy-start.2 = (f32[3,8,16,1024]{3,1,2,0:T(8,128)S(1)}, f32[3,8,16,1024]{3,1,2,0:T(8,128)}, u32[]{:S(2)}) copy-start(f32[3,8,16,1024]{3,1,2,0:T(8,128)} %copy.28) | copy-start | bytes 4718596
  16.6 2.0 copy-start.4
  18.7 6.8 %copy-start.10 = (f32[96]{0:T(128)S(1)}, f32[96]{0:T(128)}, u32[]{:S(2)}) copy-start(f32[96]{0:T(128)} %param.16) | copy-start | bytes 1156
  19.5 7.3 %collective-permute-start.1 = (f32[64,1,1024]{2,0,1:T(8,128)}, f32[64,1,1024]{2,0,1:T(8,128)}, u32[]{:S(2)}, u32[]{:S(2)}) collective-permute-start(f32[64,1,1024]{2,0,1:T(8,128)} %get-tuple-element.59), channel_id=1, source_target_pairs={{0,1},{1,2},{2,3},{3,4},{4,5},{5,6},{6,7},{8,9},{9,10},{10,11},{11... | collective-permute-start | bytes 786440 | tf_op jit(solution)/shard_map/ppermute | solution.py:17
  22.6 5.3 %collective-permute-start = (f32[64,1,1024]{2,0,1:T(8,128)}, f32[64,1,1024]{2,0,1:T(8,128)}, u32[]{:S(2)}, u32[]{:S(2)}) collective-permute-start(f32[64,1,1024]{2,0,1:T(8,128)} %get-tuple-element.58), channel_id=1, source_target_pairs={{1,0},{2,1},{3,2},{4,3},{5,4},{6,5},{7,6},{9,8},{10,9},{11,10},{12... | collective-permute-start | bytes 786440 | tf_op jit(solution)/shard_map/ppermute | solution.py:19
  26.8 28.8 %copy-start.8 = (f32[40]{0:T(128)S(1)}, f32[40]{0:T(128)}, u32[]{:S(2)}) copy-start(f32[40]{0:T(128)} %param.19) | copy-start | bytes 484
  26.8 28.8 %copy-start.9 = (f32[40]{0:T(128)S(1)}, f32[40]{0:T(128)}, u32[]{:S(2)}) copy-start(f32[40]{0:T(128)} %param.17) | copy-start | bytes 484
  64.2 63.5 %copy-start.5 = (f32[96,96]{1,0:T(8,128)S(1)}, f32[96,96]{1,0:T(8,128)}, u32[]{:S(2)}) copy-start(f32[96,96]{1,0:T(8,128)} %param.13) | copy-start | bytes 110596
  64.2 63.5 %copy-start.6 = (s32[96,96]{1,0:T(8,128)S(1)}, s32[96,96]{1,0:T(8,128)}, u32[]{:S(2)}) copy-start(s32[96,96]{1,0:T(8,128)} %param.15) | copy-start | bytes 110596
  64.2 63.5 %copy-start.7 = (f32[96,96]{1,0:T(8,128)S(1)}, f32[96,96]{1,0:T(8,128)}, u32[]{:S(2)}) copy-start(f32[96,96]{1,0:T(8,128)} %param.14) | copy-start | bytes 110596
Sparse Core Ops, SparseCore 0:
  11.4 44.1 all-reduce.2
  57.5 70.1 all-gather.1
where the time goes:
time: 439 us; the launch traced here: 438 us
  matrix products  243 us (55%)
  waiting for transfers between devices  78.7 us (18%)
  local copies, waits for them, and re-layouts  78.1 us (18%)
  other arithmetic  18 us (4%)
  between operations  14.8 us (3%)
  starting transfers between devices  4.61 us (1%)
    dot_general x24, matrix products, one_target(): product = jnp.dot(weights, dense, precision=HI)  228 us
    all_gather x1, waiting for transfers between devices, shards(): whole = lax.all_gather(flat, 'sec', axis=0, tiled=True)  60.5 us
    dynamic_update_slice x24, local copies, waits for them, and re-layouts, birth_rows(): return lax.map(one_target, indices)  47 us
    psum x1, waiting for transfers between devices, shards(): consumption = lax.psum(jnp.sum(flux, axis=0), 'sec')  17.1 us
    dynamic_slice x24, local copies, waits for them, and re-layouts, birth_rows(): return lax.map(one_target, indices)  15.5 us
    unnamed x28, local copies, waits for them, and re-layouts  11 us
    sub x1, other arithmetic, shards(): lapl = beside - 4.0 * stacked  10.6 us
  transfers between devices with their start and end apart: 4, of which 3 were waited for; matrix products, arithmetic and copies ran while one was open for 7% of the time, Pallas kernels for 0%

commit v1 on v0

v1 whole, which is shorter than its diff:
```python
import functools

import jax
import jax.numpy as jnp
from jax import lax
from jax.experimental import pallas as pl
from jax.experimental.pallas import tpu as pltpu
from jax.sharding import PartitionSpec as P

F32 = jnp.float32
BF16 = jnp.bfloat16
SUB = 8
LANE = 128
SHIFTS = 5
ANY = pl.BlockSpec(memory_space=pl.ANY)
VMEM = pl.BlockSpec(memory_space=pltpu.VMEM)
SMEM = pl.BlockSpec(memory_space=pltpu.SMEM)
PARAMS = pltpu.CompilerParams(vmem_limit_bytes=48 * 1024 * 1024)


def halves(x):
    high = x.astype(BF16)
    return high, (x - high.astype(F32)).astype(BF16)


class Plan:
    def __init__(self, n, rows, width):
        self.n = n
        self.across = min(n, width // LANE)
        self.down = n // self.across
        self.rows = rows // self.down
        self.cols = width // self.across
        self.chunks = self.rows // SUB

    def place(self, owner, chunk):
        row = (owner // self.across) * self.rows + chunk * SUB
        col = (owner % self.across) * self.cols
        return pl.ds(pl.multiple_of(row, SUB), SUB), pl.ds(pl.multiple_of(col, LANE), self.cols)


def peer(k):
    return lax.axis_index("sec") ^ k


def cut_kernel(plan, soot, *rest):
    outs, sems = rest[:-1], rest[-1]
    copies = []
    for chunk in range(plan.chunks):
        for k in range(plan.n):
            at = chunk * plan.n + k
            rows, cols = plan.place(peer(k), chunk)
            copies.append(pltpu.make_async_copy(soot.at[:, rows, cols], outs[at], sems.at[at]))
            copies[-1].start()
    for copy in copies:
        copy.wait()


def cut(plan, soot):
    count = plan.chunks * plan.n
    shape = jax.ShapeDtypeStruct((soot.shape[0], SUB, plan.cols), F32)
    return pl.pallas_call(
        functools.partial(cut_kernel, plan),
        out_shape=[shape] * count,
        in_specs=[ANY],
        out_specs=[VMEM] * count,
        scratch_shapes=[pltpu.SemaphoreType.DMA((count,))],
        compiler_params=PARAMS,
        name="cut",
    )(soot)


def edge_kernel(soot, species, head, tail):
    local, rows, _ = soot.shape
    for ref, at in ((soot, 0), (species, local)):
        count = ref.shape[0]
        for out, row in ((head, 0), (tail, rows - 1)):
            out[at : at + count, :] = ref[:, row, :]


def edges(soot, species):
    shape = jax.ShapeDtypeStruct((soot.shape[0] + species.shape[0], soot.shape[2]), F32)
    return pl.pallas_call(
        edge_kernel,
        out_shape=[shape, shape],
        in_specs=[VMEM, VMEM],
        out_specs=[VMEM, VMEM],
        compiler_params=PARAMS,
        name="edges",
    )(soot, species)


def weight_kernel(kernel, split, target, growth, twice, rest, rate, rate_before, scratch):
    size = kernel.shape[0]
    row = lax.broadcasted_iota(jnp.int32, (size, size), 0)
    col = lax.broadcasted_iota(jnp.int32, (size, size), 1)
    k, sp = kernel[...], split[...]
    t = target[...].astype(F32)
    rowf = row.astype(F32)
    k_t, sp_t, t_t = k.T, sp.T, t.T
    low, high = 0.5 * k * sp, 0.5 * k * (1.0 - sp)
    low_t, high_t = 0.5 * k_t * sp_t, 0.5 * k_t * (1.0 - sp_t)

    def fed(shift):
        at = rowf + shift
        own = jnp.where(t == at, low, 0.0) + jnp.where(t + 1.0 == at, high, 0.0)
        other = jnp.where(t_t == at, low_t, 0.0) + jnp.where(t_t + 1.0 == at, high_t, 0.0)
        return jnp.where(col <= row, own, 0.0) + jnp.where(col < row, other, 0.0)

    scratch[...] = jnp.zeros_like(scratch)
    scratch[0:size, :] = fed(0) - k
    for shift in range(1, SHIFTS):
        scratch[shift * size + shift : (shift + 1) * size, :] = fed(shift)[: size - shift]
    last = SHIFTS * size
    scratch[last : last + SUB - 1, :] = fed(-1)[size - SUB + 1 :]
    w_high, w_low = halves(scratch[...])
    twice[:, :size] = w_high
    twice[:, size:] = w_high
    rest[...] = w_low
    diagonal = jnp.where(row == col, jnp.broadcast_to(growth[...], (size, size)), 0.0)
    column = jnp.sum(diagonal, axis=1, keepdims=True)
    rate[...] = jnp.broadcast_to(column, rate.shape)
    before = jnp.where(row == col + 1, jnp.broadcast_to(growth[...], (size, size)), 0.0)
    column = jnp.sum(before, axis=1, keepdims=True)
    rate_before[...] = jnp.broadcast_to(column, rate_before.shape)


def weights(plan, kernel, split, target, growth):
    size = kernel.shape[0]
    depth = SHIFTS * size + 2 * SUB
    return pl.pallas_call(
        weight_kernel,
        out_shape=[
            jax.ShapeDtypeStruct((depth, 2 * size), BF16),
            jax.ShapeDtypeStruct((depth, size), BF16),
            jax.ShapeDtypeStruct((size, plan.cols), F32),
            jax.ShapeDtypeStruct((size, plan.cols), F32),
        ],
        in_specs=[VMEM] * 4,
        out_specs=[VMEM] * 4,
        scratch_shapes=[pltpu.VMEM((depth, size), F32)],
        compiler_params=PARAMS,
        name="weights",
    )(kernel, split, target, growth.reshape(1, size))


def rate_kernel(plan, chunk, twice, rest, rate, rate_before, acet, *refs):
    n = plan.n
    pieces, outs = refs[:n], refs[n : 2 * n]
    whole, result, near, sem = refs[2 * n :]
    size = rate.shape[0]
    local = size // n
    rows, cols = plan.place(lax.axis_index("sec"), chunk)
    copy = pltpu.make_async_copy(acet.at[0, rows, cols], near, sem)
    copy.start()
    pad = SHIFTS - 1
    blocks = range(plan.cols // LANE)
    lanes = [slice(b * LANE, (b + 1) * LANE) for b in blocks]
    for b in blocks:
        whole[b, : pad * SUB, :] = jnp.zeros((pad * SUB, LANE), F32)
        whole[b, (pad + size) * SUB :, :] = jnp.zeros((SUB, LANE), F32)
        for k in range(n):
            start = pl.multiple_of((pad + local * peer(k)) * SUB, SUB)
            whole[b, pl.ds(start, local * SUB), :] = pieces[k][:, lanes[b]]
    copy.wait()

    def sections(first, count, row):
        parts = [whole[b, pl.ds((pad + first) * SUB + row, count, stride=SUB), :] for b in blocks]
        return jnp.concatenate(parts, axis=1)

    for row in range(SUB):
        here = sections(0, size, row)
        high, low = halves(here)
        product = jnp.dot(twice[...], jnp.concatenate([high, low], axis=0), preferred_element_type=F32)
        product += jnp.dot(rest[...], high, preferred_element_type=F32)
        total = here * product[:size]
        for shift in range(1, SHIFTS):
            total += sections(-shift, size, row) * product[shift * size : (shift + 1) * size]
        last = SHIFTS * size
        extra = sections(size - SUB + 1, SUB, row) * product[last : last + SUB]
        total = jnp.concatenate([total[: size - SUB], total[size - SUB :] + extra], axis=0)
        growing = near[row : row + 1, :]
        grown = rate[...] * here
        total -= growing * (grown - rate_before[...] * sections(-1, size, row))
        for b in blocks:
            result[b, pl.ds(row, size, stride=SUB), :] = total[:, lanes[b]]
        used = growing * jnp.sum(grown, axis=0, keepdims=True)
        for k in range(n):
            outs[k][local * SUB + row : local * SUB + row + 1, :] = used
    for k in range(n):
        start = pl.multiple_of(local * peer(k) * SUB, SUB)
        for b in blocks:
            outs[k][: local * SUB, lanes[b]] = result[b, pl.ds(start, local * SUB), :]


def rates(plan, chunk, prepared, acet, pieces):
    size = prepared[2].shape[0]
    local = size // plan.n
    shape = jax.ShapeDtypeStruct(((local + 1) * SUB, plan.cols), F32)
    outs = pl.pallas_call(
        functools.partial(rate_kernel, plan, chunk),
        out_shape=[shape] * plan.n,
        in_specs=[VMEM] * 4 + [ANY] + [VMEM] * plan.n,
        out_specs=[VMEM] * plan.n,
        scratch_shapes=[
            pltpu.VMEM((plan.cols // LANE, (SHIFTS + size) * SUB, LANE), F32),
            pltpu.VMEM((plan.cols // LANE, size * SUB, LANE), F32),
            pltpu.VMEM((SUB, plan.cols), F32),
            pltpu.SemaphoreType.DMA,
        ],
        compiler_params=PARAMS,
        name="rates",
    )(*prepared, acet, *[p.reshape(local * SUB, plan.cols) for p in pieces])
    return outs


def base_kernel(above, below, diffusivity, reaction, soot, species, soot_base, species_base, stack, mixed):
    local, rows, width = soot.shape
    kinds = species.shape[0]
    lanes = lax.broadcasted_iota(jnp.int32, (rows, width), 1)
    blocks = range(width // LANE)

    def spread(v, at, factor):
        up = jnp.concatenate([above[pl.ds(at, 1), :], v[:-1]], axis=0)
        down = jnp.concatenate([v[1:], below[pl.ds(at, 1), :]], axis=0)
        left = jnp.where(lanes == 0, 0.0, pltpu.roll(v, 1, 1))
        right = jnp.where(lanes == width - 1, 0.0, pltpu.roll(v, width - 1, 1))
        return v + factor * (up + down + left + right - 4.0 * v)

    def one_section(i, carry):
        soot_base[i] = spread(soot[i], i, 0.1)
        return carry

    lax.fori_loop(0, local, one_section, 0)
    for b in blocks:
        stack[b] = species[:, :, b * LANE : (b + 1) * LANE].reshape(kinds * rows, LANE)
    r_high, r_low = halves(reaction[...])
    r_all = jnp.concatenate([r_high.astype(F32), r_high.astype(F32), r_low.astype(F32)], axis=1).astype(BF16)
    for row in range(rows):
        at = pl.ds(row, kinds, stride=rows)
        v = jnp.concatenate([stack[b, at, :] for b in blocks], axis=1)
        high, low = halves(v)
        high, low = high.astype(F32), low.astype(F32)
        v_all = jnp.concatenate([high, low, high], axis=0).astype(BF16)
        product = jnp.dot(r_all, v_all, preferred_element_type=F32)
        for b in blocks:
            mixed[b, at, :] = product[:, b * LANE : (b + 1) * LANE]

    def one_species(i, carry):
        at = pl.ds(pl.multiple_of(i * rows, SUB), rows)
        more = jnp.concatenate([mixed[b, at, :] for b in blocks], axis=1)
        species_base[i] = spread(species[i], local + i, diffusivity[i]) + more
        return carry

    lax.fori_loop(0, kinds, one_species, 0)


def bases(above, below, diffusivity, reaction, soot, species):
    return pl.pallas_call(
        base_kernel,
        out_shape=[jax.ShapeDtypeStruct(soot.shape, F32), jax.ShapeDtypeStruct(species.shape, F32)],
        in_specs=[VMEM, VMEM, SMEM, VMEM, VMEM, VMEM],
        out_specs=[VMEM, VMEM],
        scratch_shapes=[pltpu.VMEM((soot.shape[2] // LANE, species.shape[0] * soot.shape[1], LANE), F32)] * 2,
        compiler_params=PARAMS,
        name="bases",
    )(above, below, diffusivity, reaction, soot, species)


def last_kernel(plan, stoich, soot_base, species_base, *refs):
    count = plan.n * plan.chunks
    pieces, (soot_out, species_out) = refs[:count], refs[count:]
    local, kinds = soot_out.shape[0], species_out.shape[0]
    for chunk in range(plan.chunks):
        for k in range(plan.n):
            piece = pieces[chunk * plan.n + k]
            rows, cols = plan.place(peer(k), chunk)
            soot_out[:, rows, cols] = soot_base[:, rows, cols] + piece[:local]
            used = piece[local]
            for kind in range(kinds):
                species_out[kind, rows, cols] = species_base[kind, rows, cols] - stoich[kind] * used


def last(plan, stoich, soot_base, species_base, pieces):
    local = soot_base.shape[0]
    return pl.pallas_call(
        functools.partial(last_kernel, plan),
        out_shape=[jax.ShapeDtypeStruct(soot_base.shape, F32), jax.ShapeDtypeStruct(species_base.shape, F32)],
        in_specs=[SMEM, VMEM, VMEM] + [VMEM] * len(pieces),
        out_specs=[VMEM, VMEM],
        compiler_params=PARAMS,
        name="last",
    )(stoich, soot_base, species_base, *[p.reshape(local + 1, SUB, plan.cols) for p in pieces])


def shards(soot, species, kernel, split, target, growth, diffusivity, reaction, stoich):
    n = lax.axis_size("sec")
    plan = Plan(n, soot.shape[1], soot.shape[2])

    def swap(x, k):
        return lax.ppermute(x, "sec", [(i, i ^ k) for i in range(n)]) if k else x

    sent = cut(plan, soot)
    got = [[swap(sent[chunk * n + k], k) for k in range(n)] for chunk in range(plan.chunks)]
    head, tail = edges(soot, species)
    count = lax.axis_size("xs")
    above = lax.ppermute(tail, "xs", [(i, i + 1) for i in range(count - 1)])
    below = lax.ppermute(head, "xs", [(i + 1, i) for i in range(count - 1)])
    prepared = weights(plan, kernel, split, target, growth)
    soot_base, species_base = bases(above, below, diffusivity, reaction, soot, species)
    back = []
    for chunk in range(plan.chunks):
        outs = rates(plan, chunk, prepared, species, got[chunk])
        back += [swap(outs[k], k) for k in range(n)]
    return tuple(last(plan, stoich, soot_base, species_base, back))


def solution(mesh):
    return jax.shard_map(
        shards,
        mesh=mesh,
        in_specs=(P("sec", "xs", None), P(None, "xs", None), P(), P(), P(), P(), P(), P(), P()),
        out_specs=(P("sec", "xs", None), P(None, "xs", None)),
        check_vma=False,
    )
```

time: 439 us -> 58 us (0.13)
  the two profiles are of different devices: /device:TPU:0 before, /device:TPU:26 now
where the time goes in v1:
time: 58 us; the launch traced here: 57.7 us
  starting transfers between devices  21.5 us (37%)
  Pallas kernels  21 us (36%)
  waiting for transfers between devices  9.41 us (16%)
  local copies, waits for them, and re-layouts  4.92 us (8%)
  between operations  0.84 us (1%)
    ppermute x12, starting transfers between devices, swap(): return lax.ppermute(x, 'sec', [(i, i ^ k) for i in range(n)]) if k else x  15.8 us
    pallas_call x1, Pallas kernels, bases(): pl.pallas_call(base_kernel, out_shape=[jax.ShapeDtypeStruct(soot.shape, F...  13.2 us
    ppermute x12, waiting for transfers between devices, swap(): return lax.ppermute(x, 'sec', [(i, i ^ k) for i in range(n)]) if k else x  9.41 us
    unnamed x24, local copies, waits for them, and re-layouts  4.92 us
    pallas_call x2, Pallas kernels, rates(): pl.pallas_call(functools.partial(rate_kernel, plan, chunk), out_shape=[sh...  3.9 us
    ppermute x1, starting transfers between devices, shards(): below = lax.ppermute(head, 'xs', [(i + 1, i) for i in range(count - 1)])  3.64 us
    pallas_call x1, Pallas kernels, last(): pl.pallas_call(functools.partial(last_kernel, plan), out_shape=[jax.Shape...  3.09 us
    ppermute x1, starting transfers between devices, shards(): above = lax.ppermute(tail, 'xs', [(i, i + 1) for i in range(count - 1)])  2.05 us
  transfers between devices with their start and end apart: 14, of which 2 were waited for; matrix products, arithmetic and copies ran while one was open for 0% of the time, Pallas kernels for 30%

profile of v1, /device:TPU:26, one launch (start us, length us, event | category | flops | bytes accessed | tf_op | source)
XLA Modules:
  0.0 57.7 jit_solution(5048991666699288798)
XLA Ops:
  0.6 1.4 %copy-done.2 = f32[24,16,1024]{2,1,0:T(8,128)S(1)} copy-done((f32[24,16,1024]{2,1,0:T(8,128)S(1)}, f32[24,16,1024]{2,1,0:T(8,128)}, u32[]{:S(2)}) %copy-start.2) | copy-done | bytes 1572888
  2.1 0.4 cut.1
  2.4 0.6 %collective-permute-start.8 = (f32[24,8,256]{2,1,0:T(8,128)S(1)}, f32[24,8,256]{2,1,0:T(8,128)S(1)}, u32[]{:S(2)}, u32[]{:S(2)}) collective-permute-start(f32[24,8,256]{2,1,0:T(8,128)S(1)} %get-tuple-element.43), channel_id=1, source_target_pairs={{0,8},{8,0},{16,24},{24,16},{1,9},{9,1},{17,25},{25,17},{2,10},{10... | collective-permute-start | bytes 589832 | tf_op jit(solution)/shard_map/ppermute | solution.py:300
  3.0 1.5 %collective-permute-start.9 = (f32[24,8,256]{2,1,0:T(8,128)S(1)}, f32[24,8,256]{2,1,0:T(8,128)S(1)}, u32[]{:S(2)}, u32[]{:S(2)}) collective-permute-start(f32[24,8,256]{2,1,0:T(8,128)S(1)} %get-tuple-element.44), channel_id=1, source_target_pairs={{0,16},{8,24},{16,0},{24,8},{1,17},{9,25},{17,1},{25,9},{2,18},{10... | collective-permute-start | bytes 589832 | tf_op jit(solution)/shard_map/ppermute | solution.py:300
  4.5 1.4 %collective-permute-start.10 = (f32[24,8,256]{2,1,0:T(8,128)S(1)}, f32[24,8,256]{2,1,0:T(8,128)S(1)}, u32[]{:S(2)}, u32[]{:S(2)}) collective-permute-start(f32[24,8,256]{2,1,0:T(8,128)S(1)} %get-tuple-element.45), channel_id=1, source_target_pairs={{0,24},{8,16},{16,8},{24,0},{1,25},{9,17},{17,9},{25,1},{2,26},{10... | collective-permute-start | bytes 589832 | tf_op jit(solution)/shard_map/ppermute | solution.py:300
  6.0 0.5 collective-permute-start.2
  6.5 1.7 %copy-done = f32[40,16,1024]{2,1,0:T(8,128)S(1)} copy-done((f32[40,16,1024]{2,1,0:T(8,128)S(1)}, f32[40,16,1024]{2,1,0:T(8,128)}, u32[]{:S(2)}) %copy-start) | copy-done | bytes 2621464
  8.4 2.1 %collective-permute-start = (f32[64,1024]{1,0:T(8,128)S(1)}, f32[64,1024]{1,0:T(8,128)S(1)}, u32[]{:S(2)}, u32[]{:S(2)}) collective-permute-start(f32[64,1024]{1,0:T(8,128)S(1)} %get-tuple-element.26), channel_id=1, source_target_pairs={{0,1},{1,2},{2,3},{3,4},{4,5},{5,6},{6,7},{8,9},{9,10},{10,11},{11... | collective-permute-start | bytes 786440 | tf_op jit(solution)/shard_map/ppermute | solution.py:306
  10.5 3.6 %collective-permute-start.1 = (f32[64,1024]{1,0:T(8,128)S(1)}, f32[64,1024]{1,0:T(8,128)S(1)}, u32[]{:S(2)}, u32[]{:S(2)}) collective-permute-start(f32[64,1024]{1,0:T(8,128)S(1)} %get-tuple-element.27), channel_id=1, source_target_pairs={{1,0},{2,1},{3,2},{4,3},{5,4},{6,5},{7,6},{9,8},{10,9},{11,10},{12... | collective-permute-start | bytes 786440 | tf_op jit(solution)/shard_map/ppermute | solution.py:307
  14.1 0.4 weights.1
  14.5 0.9 %collective-permute-done.10 = f32[24,8,256]{2,1,0:T(8,128)S(1)} collective-permute-done((f32[24,8,256]{2,1,0:T(8,128)S(1)}, f32[24,8,256]{2,1,0:T(8,128)S(1)}, u32[]{:S(2)}, u32[]{:S(2)}) %collective-permute-start.10) | collective-permute-done | bytes 196640 | tf_op jit(solution)/shard_map/ppermute | solution.py:300
  15.4 1.9 %rates.3 = (f32[200,256]{1,0:T(8,128)S(1)}, f32[200,256]{1,0:T(8,128)S(1)}, f32[200,256]{1,0:T(8,128)S(1)}, f32[200,256]{1,0:T(8,128)S(1)}) custom-call(bf16[496,192]{1,0:T(8,128)(2,1)S(1)} %get-tuple-element.30.twice, bf16[496,96]{1,0:T(8,128)(2,1)S(1)} %get-tuple-element.31.rest, f32[96,256]{1,0:T(8,128)S(1)} %get-tuple-element.32.rate, ...), custom_call_target="tpu_custom_call" | custom-call | tf_op jit(solution)/shard_map/rates/pallas_call | solution.py:199
  17.4 0.7 %collective-permute-start.11 = (f32[200,256]{1,0:T(8,128)S(1)}, f32[200,256]{1,0:T(8,128)S(1)}, u32[]{:S(2)}, u32[]{:S(2)}) collective-permute-start(f32[200,256]{1,0:T(8,128)S(1)} %get-tuple-element.47), channel_id=1, source_target_pairs={{0,8},{8,0},{16,24},{24,16},{1,9},{9,1},{17,25},{25,17},{2,10},{10... | collective-permute-start | bytes 614408 | tf_op jit(solution)/shard_map/ppermute | solution.py:300
  18.1 1.5 %collective-permute-start.3 = (f32[24,8,256]{2,1,0:T(8,128)S(1)}, f32[24,8,256]{2,1,0:T(8,128)S(1)}, u32[]{:S(2)}, u32[]{:S(2)}) collective-permute-start(f32[24,8,256]{2,1,0:T(8,128)S(1)} %get-tuple-element.36), channel_id=1, source_target_pairs={{0,16},{8,24},{16,0},{24,8},{1,17},{9,25},{17,1},{25,9},{2,18},{10... | collective-permute-start | bytes 589832 | tf_op jit(solution)/shard_map/ppermute | solution.py:300
  19.7 1.3 %collective-permute-start.4 = (f32[24,8,256]{2,1,0:T(8,128)S(1)}, f32[24,8,256]{2,1,0:T(8,128)S(1)}, u32[]{:S(2)}, u32[]{:S(2)}) collective-permute-start(f32[24,8,256]{2,1,0:T(8,128)S(1)} %get-tuple-element.37), channel_id=1, source_target_pairs={{0,24},{8,16},{16,8},{24,0},{1,25},{9,17},{17,9},{25,1},{2,26},{10... | collective-permute-start | bytes 589832 | tf_op jit(solution)/shard_map/ppermute | solution.py:300
  21.0 8.5 %collective-permute-done.3 = f32[24,8,256]{2,1,0:T(8,128)S(1)} collective-permute-done((f32[24,8,256]{2,1,0:T(8,128)S(1)}, f32[24,8,256]{2,1,0:T(8,128)S(1)}, u32[]{:S(2)}, u32[]{:S(2)}) %collective-permute-start.3) | collective-permute-done | bytes 196640 | tf_op jit(solution)/shard_map/ppermute | solution.py:300
  29.5 2.6 %collective-permute-start.12 = (f32[200,256]{1,0:T(8,128)S(1)}, f32[200,256]{1,0:T(8,128)S(1)}, u32[]{:S(2)}, u32[]{:S(2)}) collective-permute-start(f32[200,256]{1,0:T(8,128)S(1)} %get-tuple-element.48), channel_id=1, source_target_pairs={{0,16},{8,24},{16,0},{24,8},{1,17},{9,25},{17,1},{25,9},{2,18},{10... | collective-permute-start | bytes 614408 | tf_op jit(solution)/shard_map/ppermute | solution.py:300
  32.1 2.0 %collective-permute-start.13 = (f32[200,256]{1,0:T(8,128)S(1)}, f32[200,256]{1,0:T(8,128)S(1)}, u32[]{:S(2)}, u32[]{:S(2)}) collective-permute-start(f32[200,256]{1,0:T(8,128)S(1)} %get-tuple-element.49), channel_id=1, source_target_pairs={{0,24},{8,16},{16,8},{24,0},{1,25},{9,17},{17,9},{25,1},{2,26},{10... | collective-permute-start | bytes 614408 | tf_op jit(solution)/shard_map/ppermute | solution.py:300
  34.1 2.0 %rates.2 = (f32[200,256]{1,0:T(8,128)S(1)}, f32[200,256]{1,0:T(8,128)S(1)}, f32[200,256]{1,0:T(8,128)S(1)}, f32[200,256]{1,0:T(8,128)S(1)}) custom-call(bf16[496,192]{1,0:T(8,128)(2,1)S(1)} %get-tuple-element.30.twice, bf16[496,96]{1,0:T(8,128)(2,1)S(1)} %get-tuple-element.31.rest, f32[96,256]{1,0:T(8,128)S(1)} %get-tuple-element.32.rate, ...), custom_call_target="tpu_custom_call" | custom-call | tf_op jit(solution)/shard_map/rates/pallas_call | solution.py:199
  36.2 1.5 %collective-permute-start.6 = (f32[200,256]{1,0:T(8,128)S(1)}, f32[200,256]{1,0:T(8,128)S(1)}, u32[]{:S(2)}, u32[]{:S(2)}) collective-permute-start(f32[200,256]{1,0:T(8,128)S(1)} %get-tuple-element.40), channel_id=1, source_target_pairs={{0,16},{8,24},{16,0},{24,8},{1,17},{9,25},{17,1},{25,9},{2,18},{10... | collective-permute-start | bytes 614408 | tf_op jit(solution)/shard_map/ppermute | solution.py:300
  37.6 2.0 %collective-permute-start.7 = (f32[200,256]{1,0:T(8,128)S(1)}, f32[200,256]{1,0:T(8,128)S(1)}, u32[]{:S(2)}, u32[]{:S(2)}) collective-permute-start(f32[200,256]{1,0:T(8,128)S(1)} %get-tuple-element.41), channel_id=1, source_target_pairs={{0,24},{8,16},{16,8},{24,0},{1,25},{9,17},{17,9},{25,1},{2,26},{10... | collective-permute-start | bytes 614408 | tf_op jit(solution)/shard_map/ppermute | solution.py:300
  39.7 13.2 %bases.1 = (f32[24,16,1024]{2,1,0:T(8,128)S(1)}, f32[40,16,1024]{2,1,0:T(8,128)}) custom-call(f32[64,1024]{1,0:T(8,128)S(1)} %collective-permute-done.above, f32[64,1024]{1,0:T(8,128)S(1)} %collective-permute-done.1.below, f32[40]{0:T(128)S(1)} %copy-done.10, f32[40,40]{1,0:T(8,128)S(1)} %copy-done.8, f32[24,16,1024]{2,1,0:T(8,128)S(1)} %copy-done.3, ...), custom_call_target="tpu_custom_call" | custom-call | tf_op jit(solution)/shard_map/bases/pallas_call | solution.py:258
  52.9 1.7 %copy-done.4 = f32[40,16,1024]{2,1,0:T(8,128)S(1)} copy-done((f32[40,16,1024]{2,1,0:T(8,128)S(1)}, f32[40,16,1024]{2,1,0:T(8,128)}, u32[]{:S(2)}) %copy-start.4) | copy-done | bytes 2621464
  54.6 3.1 %last.1 = (f32[24,16,1024]{2,1,0:T(8,128)}, f32[40,16,1024]{2,1,0:T(8,128)}) custom-call(f32[40]{0:T(128)S(1)} %copy-done.11, f32[24,16,1024]{2,1,0:T(8,128)S(1)} %get-tuple-element.28.soot_base, f32[40,16,1024]{2,1,0:T(8,128)S(1)} %copy-done.4, f32[25,8,256]{2,1,0:T(8,128)S(1)} %bitcast.21, f32[25,8,256]{2,1,0:T(8,128)S(1)} %bitcast.22, ...), custom_call_target="tpu_custom_call" | custom-call | tf_op jit(solution)/shard_map/last/pallas_call | solution.py:285
  (35 shorter events, 0.3 us)
Async XLA Ops:
  2.0 12.1 %copy-start.5 = (f32[96,96]{1,0:T(8,128)S(1)}, f32[96,96]{1,0:T(8,128)}, u32[]{:S(2)}) copy-start(f32[96,96]{1,0:T(8,128)} %kernel.1) | copy-start | bytes 110596
  2.0 12.1 %copy-start.6 = (f32[96,96]{1,0:T(8,128)S(1)}, f32[96,96]{1,0:T(8,128)}, u32[]{:S(2)}) copy-start(f32[96,96]{1,0:T(8,128)} %split.1) | copy-start | bytes 110596
  2.0 12.1 %copy-start.7 = (s32[96,96]{1,0:T(8,128)S(1)}, s32[96,96]{1,0:T(8,128)}, u32[]{:S(2)}) copy-start(s32[96,96]{1,0:T(8,128)} %target.1) | copy-start | bytes 110596
  2.0 12.1 %copy-start.9 = (f32[96]{0:T(128)S(1)}, f32[96]{0:T(128)}, u32[]{:S(2)}) copy-start(f32[96]{0:T(128)} %param.14) | copy-start | bytes 1156
  2.4 8.0 %collective-permute-start.8 = (f32[24,8,256]{2,1,0:T(8,128)S(1)}, f32[24,8,256]{2,1,0:T(8,128)S(1)}, u32[]{:S(2)}, u32[]{:S(2)}) collective-permute-start(f32[24,8,256]{2,1,0:T(8,128)S(1)} %get-tuple-element.43), channel_id=1, source_target_pairs={{0,8},{8,0},{16,24},{24,16},{1,9},{9,1},{17,25},{25,17},{2,10},{10... | collective-permute-start | bytes 589832 | tf_op jit(solution)/shard_map/ppermute | solution.py:300
  3.0 11.5 %collective-permute-start.9 = (f32[24,8,256]{2,1,0:T(8,128)S(1)}, f32[24,8,256]{2,1,0:T(8,128)S(1)}, u32[]{:S(2)}, u32[]{:S(2)}) collective-permute-start(f32[24,8,256]{2,1,0:T(8,128)S(1)} %get-tuple-element.44), channel_id=1, source_target_pairs={{0,16},{8,24},{16,0},{24,8},{1,17},{9,25},{17,1},{25,9},{2,18},{10... | collective-permute-start | bytes 589832 | tf_op jit(solution)/shard_map/ppermute | solution.py:300
  4.5 10.9 %collective-permute-start.10 = (f32[24,8,256]{2,1,0:T(8,128)S(1)}, f32[24,8,256]{2,1,0:T(8,128)S(1)}, u32[]{:S(2)}, u32[]{:S(2)}) collective-permute-start(f32[24,8,256]{2,1,0:T(8,128)S(1)} %get-tuple-element.45), channel_id=1, source_target_pairs={{0,24},{8,16},{16,8},{24,0},{1,25},{9,17},{17,9},{25,1},{2,26},{10... | collective-permute-start | bytes 589832 | tf_op jit(solution)/shard_map/ppermute | solution.py:300
  6.0 13.7 %collective-permute-start.2 = (f32[24,8,256]{2,1,0:T(8,128)S(1)}, f32[24,8,256]{2,1,0:T(8,128)S(1)}, u32[]{:S(2)}, u32[]{:S(2)}) collective-permute-start(f32[24,8,256]{2,1,0:T(8,128)S(1)} %get-tuple-element.35), channel_id=1, source_target_pairs={{0,8},{8,0},{16,24},{24,16},{1,9},{9,1},{17,25},{25,17},{2,10},{10... | collective-permute-start | bytes 589832 | tf_op jit(solution)/shard_map/ppermute | solution.py:300
  8.3 7.2 %copy-start.1 = (f32[40,16,1024]{2,1,0:T(8,128)S(1)}, f32[40,16,1024]{2,1,0:T(8,128)}, u32[]{:S(2)}) copy-start(f32[40,16,1024]{2,1,0:T(8,128)} %acet.3) | copy-start | bytes 7864324
  8.4 27.7 %collective-permute-start = (f32[64,1024]{1,0:T(8,128)S(1)}, f32[64,1024]{1,0:T(8,128)S(1)}, u32[]{:S(2)}, u32[]{:S(2)}) collective-permute-start(f32[64,1024]{1,0:T(8,128)S(1)} %get-tuple-element.26), channel_id=1, source_target_pairs={{0,1},{1,2},{2,3},{3,4},{4,5},{5,6},{6,7},{8,9},{9,10},{10,11},{11... | collective-permute-start | bytes 786440 | tf_op jit(solution)/shard_map/ppermute | solution.py:306
  10.5 25.7 %collective-permute-start.1 = (f32[64,1024]{1,0:T(8,128)S(1)}, f32[64,1024]{1,0:T(8,128)S(1)}, u32[]{:S(2)}, u32[]{:S(2)}) collective-permute-start(f32[64,1024]{1,0:T(8,128)S(1)} %get-tuple-element.27), channel_id=1, source_target_pairs={{1,0},{2,1},{3,2},{4,3},{5,4},{6,5},{7,6},{9,8},{10,9},{11,10},{12... | collective-permute-start | bytes 786440 | tf_op jit(solution)/shard_map/ppermute | solution.py:307
  17.4 22.2 %copy-start.3 = (f32[24,16,1024]{2,1,0:T(8,128)S(1)}, f32[24,16,1024]{2,1,0:T(8,128)}, u32[]{:S(2)}) copy-start(f32[24,16,1024]{2,1,0:T(8,128)} %soot.5) | copy-start | bytes 4718596
  17.4 22.2 %copy-start.8 = (f32[40,40]{1,0:T(8,128)S(1)}, f32[40,40]{1,0:T(8,128)}, u32[]{:S(2)}) copy-start(f32[40,40]{1,0:T(8,128)} %reaction.1) | copy-start | bytes 19204
  17.4 22.2 %copy-start.10 = (f32[40]{0:T(128)S(1)}, f32[40]{0:T(128)}, u32[]{:S(2)}) copy-start(f32[40]{0:T(128)} %diffusivity.1) | copy-start | bytes 484
  17.4 20.2 %collective-permute-start.11 = (f32[200,256]{1,0:T(8,128)S(1)}, f32[200,256]{1,0:T(8,128)S(1)}, u32[]{:S(2)}, u32[]{:S(2)}) collective-permute-start(f32[200,256]{1,0:T(8,128)S(1)} %get-tuple-element.47), channel_id=1, source_target_pairs={{0,8},{8,0},{16,24},{24,16},{1,9},{9,1},{17,25},{25,17},{2,10},{10... | collective-permute-start | bytes 614408 | tf_op jit(solution)/shard_map/ppermute | solution.py:300
  18.1 11.3 %collective-permute-start.3 = (f32[24,8,256]{2,1,0:T(8,128)S(1)}, f32[24,8,256]{2,1,0:T(8,128)S(1)}, u32[]{:S(2)}, u32[]{:S(2)}) collective-permute-start(f32[24,8,256]{2,1,0:T(8,128)S(1)} %get-tuple-element.36), channel_id=1, source_target_pairs={{0,16},{8,24},{16,0},{24,8},{1,17},{9,25},{17,1},{25,9},{2,18},{10... | collective-permute-start | bytes 589832 | tf_op jit(solution)/shard_map/ppermute | solution.py:300
  19.7 12.4 %collective-permute-start.4 = (f32[24,8,256]{2,1,0:T(8,128)S(1)}, f32[24,8,256]{2,1,0:T(8,128)S(1)}, u32[]{:S(2)}, u32[]{:S(2)}) collective-permute-start(f32[24,8,256]{2,1,0:T(8,128)S(1)} %get-tuple-element.37), channel_id=1, source_target_pairs={{0,24},{8,16},{16,8},{24,0},{1,25},{9,17},{17,9},{25,1},{2,26},{10... | collective-permute-start | bytes 589832 | tf_op jit(solution)/shard_map/ppermute | solution.py:300
  29.5 23.4 %collective-permute-start.12 = (f32[200,256]{1,0:T(8,128)S(1)}, f32[200,256]{1,0:T(8,128)S(1)}, u32[]{:S(2)}, u32[]{:S(2)}) collective-permute-start(f32[200,256]{1,0:T(8,128)S(1)} %get-tuple-element.48), channel_id=1, source_target_pairs={{0,16},{8,24},{16,0},{24,8},{1,17},{9,25},{17,1},{25,9},{2,18},{10... | collective-permute-start | bytes 614408 | tf_op jit(solution)/shard_map/ppermute | solution.py:300
  32.1 20.7 %collective-permute-start.13 = (f32[200,256]{1,0:T(8,128)S(1)}, f32[200,256]{1,0:T(8,128)S(1)}, u32[]{:S(2)}, u32[]{:S(2)}) collective-permute-start(f32[200,256]{1,0:T(8,128)S(1)} %get-tuple-element.49), channel_id=1, source_target_pairs={{0,24},{8,16},{16,8},{24,0},{1,25},{9,17},{17,9},{25,1},{2,26},{10... | collective-permute-start | bytes 614408 | tf_op jit(solution)/shard_map/ppermute | solution.py:300
  36.1 16.8 %copy-start.11 = (f32[40]{0:T(128)S(1)}, f32[40]{0:T(128)}, u32[]{:S(2)}) copy-start(f32[40]{0:T(128)} %stoich.1) | copy-start | bytes 484
  36.1 16.7 %collective-permute-start.5 = (f32[200,256]{1,0:T(8,128)S(1)}, f32[200,256]{1,0:T(8,128)S(1)}, u32[]{:S(2)}, u32[]{:S(2)}) collective-permute-start(f32[200,256]{1,0:T(8,128)S(1)} %get-tuple-element.39), channel_id=1, source_target_pairs={{0,8},{8,0},{16,24},{24,16},{1,9},{9,1},{17,25},{25,17},{2,10},{10... | collective-permute-start | bytes 614408 | tf_op jit(solution)/shard_map/ppermute | solution.py:300
  36.2 16.7 %collective-permute-start.6 = (f32[200,256]{1,0:T(8,128)S(1)}, f32[200,256]{1,0:T(8,128)S(1)}, u32[]{:S(2)}, u32[]{:S(2)}) collective-permute-start(f32[200,256]{1,0:T(8,128)S(1)} %get-tuple-element.40), channel_id=1, source_target_pairs={{0,16},{8,24},{16,0},{24,8},{1,17},{9,25},{17,1},{25,9},{2,18},{10... | collective-permute-start | bytes 614408 | tf_op jit(solution)/shard_map/ppermute | solution.py:300
  37.6 15.2 %collective-permute-start.7 = (f32[200,256]{1,0:T(8,128)S(1)}, f32[200,256]{1,0:T(8,128)S(1)}, u32[]{:S(2)}, u32[]{:S(2)}) collective-permute-start(f32[200,256]{1,0:T(8,128)S(1)} %get-tuple-element.41), channel_id=1, source_target_pairs={{0,24},{8,16},{16,8},{24,0},{1,25},{9,17},{17,9},{25,1},{2,26},{10... | collective-permute-start | bytes 614408 | tf_op jit(solution)/shard_map/ppermute | solution.py:300
  52.9 1.7 %copy-start.4 = (f32[40,16,1024]{2,1,0:T(8,128)S(1)}, f32[40,16,1024]{2,1,0:T(8,128)}, u32[]{:S(2)}) copy-start(f32[40,16,1024]{2,1,0:T(8,128)} %get-tuple-element.29.species_base) | copy-start | bytes 7864324
  (2 other events, 3.2 us)

commit v2 on v1

--- a/solution.py
+++ b/solution.py
@@ -15,7 +15,8 @@
 ANY = pl.BlockSpec(memory_space=pl.ANY)
 VMEM = pl.BlockSpec(memory_space=pltpu.VMEM)
 SMEM = pl.BlockSpec(memory_space=pltpu.SMEM)
-PARAMS = pltpu.CompilerParams(vmem_limit_bytes=48 * 1024 * 1024)
+HBM = pl.BlockSpec(memory_space=pltpu.HBM)
+PARAMS = pltpu.CompilerParams(vmem_limit_bytes=16 * 1024 * 1024)
 
 
 def halves(x):
@@ -32,6 +33,11 @@
         self.cols = width // self.across
         self.chunks = self.rows // SUB
 
+    def whole(self, owner):
+        row = (owner // self.across) * self.rows
+        col = (owner % self.across) * self.cols
+        return pl.ds(pl.multiple_of(row, SUB), self.rows), pl.ds(pl.multiple_of(col, LANE), self.cols)
+
     def place(self, owner, chunk):
         row = (owner // self.across) * self.rows + chunk * SUB
         col = (owner % self.across) * self.cols
@@ -45,31 +51,28 @@
 def cut_kernel(plan, soot, *rest):
     outs, sems = rest[:-1], rest[-1]
     copies = []
-    for chunk in range(plan.chunks):
-        for k in range(plan.n):
-            at = chunk * plan.n + k
-            rows, cols = plan.place(peer(k), chunk)
-            copies.append(pltpu.make_async_copy(soot.at[:, rows, cols], outs[at], sems.at[at]))
-            copies[-1].start()
+    for k in range(plan.n):
+        rows, cols = plan.whole(peer(k))
+        copies.append(pltpu.make_async_copy(soot.at[:, rows, cols], outs[k], sems.at[k]))
+        copies[-1].start()
     for copy in copies:
         copy.wait()
 
 
 def cut(plan, soot):
-    count = plan.chunks * plan.n
-    shape = jax.ShapeDtypeStruct((soot.shape[0], SUB, plan.cols), F32)
+    shape = jax.ShapeDtypeStruct((soot.shape[0], plan.rows, plan.cols), F32)
     return pl.pallas_call(
         functools.partial(cut_kernel, plan),
-        out_shape=[shape] * count,
-        in_specs=[ANY],
-        out_specs=[VMEM] * count,
-        scratch_shapes=[pltpu.SemaphoreType.DMA((count,))],
+        out_shape=[shape] * plan.n,
+        in_specs=[HBM],
+        out_specs=[VMEM] * plan.n,
+        scratch_shapes=[pltpu.SemaphoreType.DMA((plan.n,))],
         compiler_params=PARAMS,
         name="cut",
-    )(soot)
-
-
-def edge_kernel(soot, species, head, tail):
+    )(pltpu.with_memory_space_constraint(soot, pltpu.HBM))
+
+
+def edge_kernel(soot, species, after, head, tail):
     local, rows, _ = soot.shape
     for ref, at in ((soot, 0), (species, local)):
         count = ref.shape[0]
@@ -77,16 +80,16 @@
             out[at : at + count, :] = ref[:, row, :]
 
 
-def edges(soot, species):
+def edges(soot, species, after):
     shape = jax.ShapeDtypeStruct((soot.shape[0] + species.shape[0], soot.shape[2]), F32)
     return pl.pallas_call(
         edge_kernel,
         out_shape=[shape, shape],
-        in_specs=[VMEM, VMEM],
+        in_specs=[VMEM, VMEM, ANY],
         out_specs=[VMEM, VMEM],
         compiler_params=PARAMS,
         name="edges",
-    )(soot, species)
+    )(soot, species, after)
 
 
 def weight_kernel(kernel, split, target, growth, twice, rest, rate, rate_before, scratch):
@@ -143,7 +146,7 @@
     )(kernel, split, target, growth.reshape(1, size))
 
 
-def rate_kernel(plan, chunk, twice, rest, rate, rate_before, acet, *refs):
+def rate_kernel(plan, chunk, twice, rest, rate, rate_before, acet, after, *refs):
     n = plan.n
     pieces, outs = refs[:n], refs[n : 2 * n]
     whole, result, near, sem = refs[2 * n :]
@@ -160,7 +163,8 @@
         whole[b, (pad + size) * SUB :, :] = jnp.zeros((SUB, LANE), F32)
         for k in range(n):
             start = pl.multiple_of((pad + local * peer(k)) * SUB, SUB)
-            whole[b, pl.ds(start, local * SUB), :] = pieces[k][:, lanes[b]]
+            piece = pieces[k][:, chunk * SUB : (chunk + 1) * SUB, lanes[b]]
+            whole[b, pl.ds(start, local * SUB), :] = piece.reshape(local * SUB, LANE)
     copy.wait()
 
     def sections(first, count, row):
@@ -192,14 +196,14 @@
             outs[k][: local * SUB, lanes[b]] = result[b, pl.ds(start, local * SUB), :]
 
 
-def rates(plan, chunk, prepared, acet, pieces):
+def rates(plan, chunk, prepared, acet, after, pieces):
     size = prepared[2].shape[0]
     local = size // plan.n
     shape = jax.ShapeDtypeStruct(((local + 1) * SUB, plan.cols), F32)
     outs = pl.pallas_call(
         functools.partial(rate_kernel, plan, chunk),
         out_shape=[shape] * plan.n,
-        in_specs=[VMEM] * 4 + [ANY] + [VMEM] * plan.n,
+        in_specs=[VMEM] * 4 + [ANY] * 2 + [VMEM] * plan.n,
         out_specs=[VMEM] * plan.n,
         scratch_shapes=[
             pltpu.VMEM((plan.cols // LANE, (SHIFTS + size) * SUB, LANE), F32),
@@ -209,28 +213,13 @@
         ],
         compiler_params=PARAMS,
         name="rates",
-    )(*prepared, acet, *[p.reshape(local * SUB, plan.cols) for p in pieces])
+    )(*prepared, acet, after, *pieces)
     return outs
 
 
-def base_kernel(above, below, diffusivity, reaction, soot, species, soot_base, species_base, stack, mixed):
-    local, rows, width = soot.shape
-    kinds = species.shape[0]
-    lanes = lax.broadcasted_iota(jnp.int32, (rows, width), 1)
+def mix_kernel(reaction, species, mixed, stack):
+    kinds, rows, width = species.shape
     blocks = range(width // LANE)
-
-    def spread(v, at, factor):
-        up = jnp.concatenate([above[pl.ds(at, 1), :], v[:-1]], axis=0)
-        down = jnp.concatenate([v[1:], below[pl.ds(at, 1), :]], axis=0)
-        left = jnp.where(lanes == 0, 0.0, pltpu.roll(v, 1, 1))
-        right = jnp.where(lanes == width - 1, 0.0, pltpu.roll(v, width - 1, 1))
-        return v + factor * (up + down + left + right - 4.0 * v)
-
-    def one_section(i, carry):
-        soot_base[i] = spread(soot[i], i, 0.1)
-        return carry
-
-    lax.fori_loop(0, local, one_section, 0)
     for b in blocks:
         stack[b] = species[:, :, b * LANE : (b + 1) * LANE].reshape(kinds * rows, LANE)
     r_high, r_low = halves(reaction[...])
@@ -245,51 +234,96 @@
         for b in blocks:
             mixed[b, at, :] = product[:, b * LANE : (b + 1) * LANE]
 
+
+def mix(reaction, species):
+    shape = (species.shape[2] // LANE, species.shape[0] * species.shape[1], LANE)
+    return pl.pallas_call(
+        mix_kernel,
+        out_shape=jax.ShapeDtypeStruct(shape, F32),
+        in_specs=[VMEM, VMEM],
+        out_specs=VMEM,
+        scratch_shapes=[pltpu.VMEM(shape, F32)],
+        compiler_params=PARAMS,
+        name="mix",
+    )(reaction, species)
+
+
+def base_kernel(above, below, diffusivity, mixed, soot, species, after, soot_base, species_base):
+    local, rows, width = soot.shape
+    kinds = species.shape[0]
+    lanes = lax.broadcasted_iota(jnp.int32, (rows, width), 1)
+    blocks = range(width // LANE)
+
+    def spread(v, at, factor):
+        up = jnp.concatenate([above[pl.ds(at, 1), :], v[:-1]], axis=0)
+        down = jnp.concatenate([v[1:], below[pl.ds(at, 1), :]], axis=0)
+        left = jnp.where(lanes == 0, 0.0, pltpu.roll(v, 1, 1))
+        right = jnp.where(lanes == width - 1, 0.0, pltpu.roll(v, width - 1, 1))
+        return v + factor * (up + down + left + right - 4.0 * v)
+
+    def one_section(i, carry):
+        soot_base[i] = spread(soot[i], i, 0.1)
+        return carry
+
+    lax.fori_loop(0, local, one_section, 0, unroll=2)
+
     def one_species(i, carry):
         at = pl.ds(pl.multiple_of(i * rows, SUB), rows)
         more = jnp.concatenate([mixed[b, at, :] for b in blocks], axis=1)
         species_base[i] = spread(species[i], local + i, diffusivity[i]) + more
         return carry
 
-    lax.fori_loop(0, kinds, one_species, 0)
-
-
-def bases(above, below, diffusivity, reaction, soot, species):
+    lax.fori_loop(0, kinds, one_species, 0, unroll=2)
+
+
+def bases(above, below, diffusivity, mixed, soot, species, after):
     return pl.pallas_call(
         base_kernel,
         out_shape=[jax.ShapeDtypeStruct(soot.shape, F32), jax.ShapeDtypeStruct(species.shape, F32)],
-        in_specs=[VMEM, VMEM, SMEM, VMEM, VMEM, VMEM],
+        in_specs=[VMEM, VMEM, SMEM, VMEM, VMEM, VMEM, ANY],
         out_specs=[VMEM, VMEM],
-        scratch_shapes=[pltpu.VMEM((soot.shape[2] // LANE, species.shape[0] * soot.shape[1], LANE), F32)] * 2,
         compiler_params=PARAMS,
         name="bases",
-    )(above, below, diffusivity, reaction, soot, species)
-
-
-def last_kernel(plan, stoich, soot_base, species_base, *refs):
-    count = plan.n * plan.chunks
-    pieces, (soot_out, species_out) = refs[:count], refs[count:]
+    )(above, below, diffusivity, mixed, soot, species, after)
+
+
+def last_kernel(plan, chunk, stoich, soot_base, species_base, *refs):
+    n = plan.n
+    pieces, refs = refs[:n], refs[n:]
+    soot_out, species_out, soot_held, species_held, sems = refs[-5:]
     local, kinds = soot_out.shape[0], species_out.shape[0]
-    for chunk in range(plan.chunks):
-        for k in range(plan.n):
-            piece = pieces[chunk * plan.n + k]
-            rows, cols = plan.place(peer(k), chunk)
-            soot_out[:, rows, cols] = soot_base[:, rows, cols] + piece[:local]
-            used = piece[local]
-            for kind in range(kinds):
-                species_out[kind, rows, cols] = species_base[kind, rows, cols] - stoich[kind] * used
-
-
-def last(plan, stoich, soot_base, species_base, pieces):
-    local = soot_base.shape[0]
-    return pl.pallas_call(
-        functools.partial(last_kernel, plan),
+    copies = []
+    for k in range(n):
+        rows, cols = plan.place(peer(k), chunk)
+        soot_held[k] = soot_base[:, rows, cols] + pieces[k][:local]
+        copies.append(pltpu.make_async_copy(soot_held.at[k], soot_out.at[:, rows, cols], sems.at[0, k]))
+        copies[-1].start()
+        used = pieces[k][local]
+        for kind in range(kinds):
+            species_held[k, kind] = species_base[kind, rows, cols] - stoich[kind] * used
+        copies.append(pltpu.make_async_copy(species_held.at[k], species_out.at[:, rows, cols], sems.at[1, k]))
+        copies[-1].start()
+    for copy in copies:
+        copy.wait()
+
+
+def last(plan, chunk, stoich, soot_base, species_base, pieces, before):
+    local, kinds = soot_base.shape[0], species_base.shape[0]
+    first = 3 + len(pieces)
+    return pl.pallas_call(
+        functools.partial(last_kernel, plan, chunk),
         out_shape=[jax.ShapeDtypeStruct(soot_base.shape, F32), jax.ShapeDtypeStruct(species_base.shape, F32)],
-        in_specs=[SMEM, VMEM, VMEM] + [VMEM] * len(pieces),
-        out_specs=[VMEM, VMEM],
+        in_specs=[SMEM, VMEM, VMEM] + [VMEM] * len(pieces) + [HBM] * len(before),
+        out_specs=[HBM, HBM],
+        scratch_shapes=[
+            pltpu.VMEM((plan.n, local, SUB, plan.cols), F32),
+            pltpu.VMEM((plan.n, kinds, SUB, plan.cols), F32),
+            pltpu.SemaphoreType.DMA((2, plan.n)),
+        ],
+        input_output_aliases={first + i: i for i in range(len(before))},
         compiler_params=PARAMS,
         name="last",
-    )(stoich, soot_base, species_base, *[p.reshape(local + 1, SUB, plan.cols) for p in pieces])
+    )(stoich, soot_base, species_base, *[p.reshape(local + 1, SUB, plan.cols) for p in pieces], *before)
 
 
 def shards(soot, species, kernel, split, target, growth, diffusivity, reaction, stoich):
@@ -300,18 +334,22 @@
         return lax.ppermute(x, "sec", [(i, i ^ k) for i in range(n)]) if k else x
 
     sent = cut(plan, soot)
-    got = [[swap(sent[chunk * n + k], k) for k in range(n)] for chunk in range(plan.chunks)]
-    head, tail = edges(soot, species)
+    got = [swap(sent[k], k) for k in range(n)]
+    prepared = weights(plan, kernel, split, target, growth)
+    mixed = mix(reaction, species)
+    head, tail = edges(soot, species, sent[0])
     count = lax.axis_size("xs")
     above = lax.ppermute(tail, "xs", [(i, i + 1) for i in range(count - 1)])
     below = lax.ppermute(head, "xs", [(i + 1, i) for i in range(count - 1)])
-    prepared = weights(plan, kernel, split, target, growth)
-    soot_base, species_base = bases(above, below, diffusivity, reaction, soot, species)
+    soot_base, species_base = bases(above, below, diffusivity, mixed, soot, species, mixed)
     back = []
     for chunk in range(plan.chunks):
-        outs = rates(plan, chunk, prepared, species, got[chunk])
-        back += [swap(outs[k], k) for k in range(n)]
-    return tuple(last(plan, stoich, soot_base, species_base, back))
+        outs = rates(plan, chunk, prepared, species, soot_base, got)
+        back.append([swap(outs[k], k) for k in range(n)])
+    result = ()
+    for chunk in range(plan.chunks):
+        result = last(plan, chunk, stoich, soot_base, species_base, back[chunk], result)
+    return tuple(result)
 
 
 def solution(mesh):

time: 58 us -> 50.7 us (0.87)
  the two profiles are of different devices: /device:TPU:26 before, /device:TPU:0 now
where the time goes in v2:
time: 50.7 us; the launch traced here: 50.4 us
  Pallas kernels  18 us (36%)
  waiting for transfers between devices  15.3 us (30%)
  starting transfers between devices  14.5 us (29%)
  local copies, waits for them, and re-layouts  1.79 us (4%)
  between operations  0.82 us (2%)
    ppermute x9, waiting for transfers between devices, swap(): return lax.ppermute(x, 'sec', [(i, i ^ k) for i in range(n)]) if k else x  14.3 us
    ppermute x9, starting transfers between devices, swap(): return lax.ppermute(x, 'sec', [(i, i ^ k) for i in range(n)]) if k else x  11.7 us
    pallas_call x1, Pallas kernels, bases(): pl.pallas_call(base_kernel, out_shape=[jax.ShapeDtypeStruct(soot.shape, F...  5.21 us
    pallas_call x2, Pallas kernels, rates(): pl.pallas_call(functools.partial(rate_kernel, plan, chunk), out_shape=[sh...  3.93 us
    pallas_call x2, Pallas kernels, last(): pl.pallas_call(functools.partial(last_kernel, plan, chunk), out_shape=[ja...  3.9 us
    pallas_call x1, Pallas kernels, mix(): pl.pallas_call(mix_kernel, out_shape=jax.ShapeDtypeStruct(shape, F32), in...  2.9 us
    unnamed x20, local copies, waits for them, and re-layouts  1.79 us
    pallas_call x1, Pallas kernels, cut(): pl.pallas_call(functools.partial(cut_kernel, plan), out_shape=[shape] * p...  1.53 us
  transfers between devices with their start and end apart: 11, of which 5 were waited for; matrix products, arithmetic and copies ran while one was open for 0% of the time, Pallas kernels for 25%

profile of v2, /device:TPU:0, one launch (start us, length us, event | category | flops | bytes accessed | tf_op | source)
XLA Modules:
  0.0 50.4 jit_solution(7378777084212247899)
XLA Ops:
  0.6 1.5 %cut.1 = (f32[24,16,256]{2,1,0:T(8,128)S(1)}, f32[24,16,256]{2,1,0:T(8,128)S(1)}, f32[24,16,256]{2,1,0:T(8,128)S(1)}, f32[24,16,256]{2,1,0:T(8,128)S(1)}) custom-call(f32[24,16,1024]{2,1,0:T(8,128)} %soot.5), custom_call_target="tpu_custom_call" | custom-call | tf_op jit(solution)/shard_map/cut/pallas_call | solution.py:64
  2.2 3.0 %collective-permute-start.2 = (f32[24,16,256]{2,1,0:T(8,128)S(1)}, f32[24,16,256]{2,1,0:T(8,128)S(1)}, u32[]{:S(2)}, u32[]{:S(2)}) collective-permute-start(f32[24,16,256]{2,1,0:T(8,128)S(1)} %get-tuple-element.33), channel_id=1, source_target_pairs={{0,8},{8,0},{16,24},{24,16},{1,9},{9,1},{17,25},{25,17},{2,10},{10... | collective-permute-start | bytes 1179656 | tf_op jit(solution)/shard_map/ppermute | solution.py:334
  5.2 1.5 %collective-permute-start.3 = (f32[24,16,256]{2,1,0:T(8,128)S(1)}, f32[24,16,256]{2,1,0:T(8,128)S(1)}, u32[]{:S(2)}, u32[]{:S(2)}) collective-permute-start(f32[24,16,256]{2,1,0:T(8,128)S(1)} %get-tuple-element.34), channel_id=1, source_target_pairs={{0,16},{8,24},{16,0},{24,8},{1,17},{9,25},{17,1},{25,9},{2,18},{10... | collective-permute-start | bytes 1179656 | tf_op jit(solution)/shard_map/ppermute | solution.py:334
  6.7 1.7 %copy-done = f32[40,16,1024]{2,1,0:T(8,128)S(1)} copy-done((f32[40,16,1024]{2,1,0:T(8,128)S(1)}, f32[40,16,1024]{2,1,0:T(8,128)}, u32[]{:S(2)}) %copy-start) | copy-done | bytes 2621464
  8.6 1.4 %collective-permute-start = (f32[64,1024]{1,0:T(8,128)S(1)}, f32[64,1024]{1,0:T(8,128)S(1)}, u32[]{:S(2)}, u32[]{:S(2)}) collective-permute-start(f32[64,1024]{1,0:T(8,128)S(1)} %get-tuple-element.25), channel_id=1, source_target_pairs={{0,1},{1,2},{2,3},{3,4},{4,5},{5,6},{6,7},{8,9},{9,10},{10,11},{11... | collective-permute-start | bytes 786440 | tf_op jit(solution)/shard_map/ppermute | solution.py:342
  10.1 1.4 %collective-permute-start.1 = (f32[64,1024]{1,0:T(8,128)S(1)}, f32[64,1024]{1,0:T(8,128)S(1)}, u32[]{:S(2)}, u32[]{:S(2)}) collective-permute-start(f32[64,1024]{1,0:T(8,128)S(1)} %get-tuple-element.26), channel_id=1, source_target_pairs={{1,0},{2,1},{3,2},{4,3},{5,4},{6,5},{7,6},{9,8},{10,9},{11,10},{12... | collective-permute-start | bytes 786440 | tf_op jit(solution)/shard_map/ppermute | solution.py:343
  11.6 2.9 %mix.1.mixed.after = f32[8,640,128]{2,1,0:T(8,128)S(1)} custom-call(f32[40,40]{1,0:T(8,128)S(1)} %copy-done.6, f32[40,16,1024]{2,1,0:T(8,128)S(1)} %copy-done.1), custom_call_target="tpu_custom_call" | custom-call | tf_op jit(solution)/shard_map/mix/pallas_call | solution.py:240
  14.5 0.4 weights.1
  14.9 1.0 %collective-permute-done.1.below = f32[64,1024]{1,0:T(8,128)S(1)} collective-permute-done((f32[64,1024]{1,0:T(8,128)S(1)}, f32[64,1024]{1,0:T(8,128)S(1)}, u32[]{:S(2)}, u32[]{:S(2)}) %collective-permute-start.1) | collective-permute-done | bytes 262176 | tf_op jit(solution)/shard_map/ppermute | solution.py:343
  15.9 5.2 %bases.1 = (f32[24,16,1024]{2,1,0:T(8,128)S(1)}, f32[40,16,1024]{2,1,0:T(8,128)S(1)}) custom-call(f32[64,1024]{1,0:T(8,128)S(1)} %collective-permute-done.above, f32[64,1024]{1,0:T(8,128)S(1)} %collective-permute-done.1.below, f32[40]{0:T(128)S(1)} %copy-done.9, f32[8,640,128]{2,1,0:T(8,128)S(1)} %mix.1.mixed.after, f32[24,16,1024]{2,1,0:T(8,128)S(1)} %copy-done.2, ...), custom_call_target="tpu_custom_call" | custom-call | tf_op jit(solution)/shard_map/bases/pallas_call | solution.py:280
  21.1 3.0 %collective-permute-done.3.refs_2_ = f32[24,16,256]{2,1,0:T(8,128)S(1)} collective-permute-done((f32[24,16,256]{2,1,0:T(8,128)S(1)}, f32[24,16,256]{2,1,0:T(8,128)S(1)}, u32[]{:S(2)}, u32[]{:S(2)}) %collective-permute-start.3) | collective-permute-done | bytes 393248 | tf_op jit(solution)/shard_map/ppermute | solution.py:334
  24.2 2.0 %rates.3 = (f32[200,256]{1,0:T(8,128)S(1)}, f32[200,256]{1,0:T(8,128)S(1)}, f32[200,256]{1,0:T(8,128)S(1)}, f32[200,256]{1,0:T(8,128)S(1)}) custom-call(bf16[496,192]{1,0:T(8,128)(2,1)S(1)} %get-tuple-element.29.twice, bf16[496,96]{1,0:T(8,128)(2,1)S(1)} %get-tuple-element.30.rest, f32[96,256]{1,0:T(8,128)S(1)} %get-tuple-element.31.rate, ...), custom_call_target="tpu_custom_call" | custom-call | tf_op jit(solution)/shard_map/rates/pallas_call | solution.py:203
  26.2 1.3 %collective-permute-start.8 = (f32[200,256]{1,0:T(8,128)S(1)}, f32[200,256]{1,0:T(8,128)S(1)}, u32[]{:S(2)}, u32[]{:S(2)}) collective-permute-start(f32[200,256]{1,0:T(8,128)S(1)} %get-tuple-element.41), channel_id=1, source_target_pairs={{0,8},{8,0},{16,24},{24,16},{1,9},{9,1},{17,25},{25,17},{2,10},{10... | collective-permute-start | bytes 614408 | tf_op jit(solution)/shard_map/ppermute | solution.py:334
  27.5 0.8 %collective-permute-start.9 = (f32[200,256]{1,0:T(8,128)S(1)}, f32[200,256]{1,0:T(8,128)S(1)}, u32[]{:S(2)}, u32[]{:S(2)}) collective-permute-start(f32[200,256]{1,0:T(8,128)S(1)} %get-tuple-element.42), channel_id=1, source_target_pairs={{0,16},{8,24},{16,0},{24,8},{1,17},{9,25},{17,1},{25,9},{2,18},{10... | collective-permute-start | bytes 614408 | tf_op jit(solution)/shard_map/ppermute | solution.py:334
  28.3 1.4 %collective-permute-start.10 = (f32[200,256]{1,0:T(8,128)S(1)}, f32[200,256]{1,0:T(8,128)S(1)}, u32[]{:S(2)}, u32[]{:S(2)}) collective-permute-start(f32[200,256]{1,0:T(8,128)S(1)} %get-tuple-element.43), channel_id=1, source_target_pairs={{0,24},{8,16},{16,8},{24,0},{1,25},{9,17},{17,9},{25,1},{2,26},{10... | collective-permute-start | bytes 614408 | tf_op jit(solution)/shard_map/ppermute | solution.py:334
  29.7 2.0 %rates.2 = (f32[200,256]{1,0:T(8,128)S(1)}, f32[200,256]{1,0:T(8,128)S(1)}, f32[200,256]{1,0:T(8,128)S(1)}, f32[200,256]{1,0:T(8,128)S(1)}) custom-call(bf16[496,192]{1,0:T(8,128)(2,1)S(1)} %get-tuple-element.29.twice, bf16[496,96]{1,0:T(8,128)(2,1)S(1)} %get-tuple-element.30.rest, f32[96,256]{1,0:T(8,128)S(1)} %get-tuple-element.31.rate, ...), custom_call_target="tpu_custom_call" | custom-call | tf_op jit(solution)/shard_map/rates/pallas_call | solution.py:203
  31.7 1.3 %collective-permute-start.5 = (f32[200,256]{1,0:T(8,128)S(1)}, f32[200,256]{1,0:T(8,128)S(1)}, u32[]{:S(2)}, u32[]{:S(2)}) collective-permute-start(f32[200,256]{1,0:T(8,128)S(1)} %get-tuple-element.37), channel_id=1, source_target_pairs={{0,8},{8,0},{16,24},{24,16},{1,9},{9,1},{17,25},{25,17},{2,10},{10... | collective-permute-start | bytes 614408 | tf_op jit(solution)/shard_map/ppermute | solution.py:334
  33.0 0.8 %collective-permute-start.6 = (f32[200,256]{1,0:T(8,128)S(1)}, f32[200,256]{1,0:T(8,128)S(1)}, u32[]{:S(2)}, u32[]{:S(2)}) collective-permute-start(f32[200,256]{1,0:T(8,128)S(1)} %get-tuple-element.38), channel_id=1, source_target_pairs={{0,16},{8,24},{16,0},{24,8},{1,17},{9,25},{17,1},{25,9},{2,18},{10... | collective-permute-start | bytes 614408 | tf_op jit(solution)/shard_map/ppermute | solution.py:334
  33.8 1.4 %collective-permute-start.7 = (f32[200,256]{1,0:T(8,128)S(1)}, f32[200,256]{1,0:T(8,128)S(1)}, u32[]{:S(2)}, u32[]{:S(2)}) collective-permute-start(f32[200,256]{1,0:T(8,128)S(1)} %get-tuple-element.39), channel_id=1, source_target_pairs={{0,24},{8,16},{16,8},{24,0},{1,25},{9,17},{17,9},{25,1},{2,26},{10... | collective-permute-start | bytes 614408 | tf_op jit(solution)/shard_map/ppermute | solution.py:334
  35.3 3.2 %collective-permute-done.10 = f32[200,256]{1,0:T(8,128)S(1)} collective-permute-done((f32[200,256]{1,0:T(8,128)S(1)}, f32[200,256]{1,0:T(8,128)S(1)}, u32[]{:S(2)}, u32[]{:S(2)}) %collective-permute-start.10) | collective-permute-done | bytes 204832 | tf_op jit(solution)/shard_map/ppermute | solution.py:334
  38.5 2.0 %last.2 = (f32[24,16,1024]{2,1,0:T(8,128)}, f32[40,16,1024]{2,1,0:T(8,128)}) custom-call(f32[40]{0:T(128)S(1)} %copy-done.7, f32[24,16,1024]{2,1,0:T(8,128)S(1)} %get-tuple-element.27.after.soot_base, f32[40,16,1024]{2,1,0:T(8,128)S(1)} %get-tuple-element.28.species_base, f32[25,8,256]{2,1,0:T(8,128)S(1)} %bitcast.13, f32[25,8,256]{2,1,0:T(8,128)S(1)} %bitcast.14, ...), custom_call_target="tpu_custom_call" | custom-call | tf_op jit(solution)/shard_map/last/pallas_call | solution.py:313
  40.5 1.4 %collective-permute-done.5 = f32[200,256]{1,0:T(8,128)S(1)} collective-permute-done((f32[200,256]{1,0:T(8,128)S(1)}, f32[200,256]{1,0:T(8,128)S(1)}, u32[]{:S(2)}, u32[]{:S(2)}) %collective-permute-start.5) | collective-permute-done | bytes 204832 | tf_op jit(solution)/shard_map/ppermute | solution.py:334
  41.9 6.6 %collective-permute-done.6 = f32[200,256]{1,0:T(8,128)S(1)} collective-permute-done((f32[200,256]{1,0:T(8,128)S(1)}, f32[200,256]{1,0:T(8,128)S(1)}, u32[]{:S(2)}, u32[]{:S(2)}) %collective-permute-start.6) | collective-permute-done | bytes 204832 | tf_op jit(solution)/shard_map/ppermute | solution.py:334
  48.5 2.0 %last.3 = (f32[24,16,1024]{2,1,0:T(8,128)}, f32[40,16,1024]{2,1,0:T(8,128)}) custom-call(f32[40]{0:T(128)S(1)} %copy-done.7, f32[24,16,1024]{2,1,0:T(8,128)S(1)} %get-tuple-element.27.after.soot_base, f32[40,16,1024]{2,1,0:T(8,128)S(1)} %get-tuple-element.28.species_base, f32[25,8,256]{2,1,0:T(8,128)S(1)} %bitcast.9, ...), custom_call_target="tpu_custom_call", output_to_operand_aliasing={{0}: (7, {}), {1}: (8, {})} | custom-call | tf_op jit(solution)/shard_map/last/pallas_call | solution.py:313
  (27 shorter events, 0.2 us)
Async XLA Ops:
  0.6 6.1 %copy-start.2 = (f32[24,16,1024]{2,1,0:T(8,128)S(1)}, f32[24,16,1024]{2,1,0:T(8,128)}, u32[]{:S(2)}) copy-start(f32[24,16,1024]{2,1,0:T(8,128)} %soot.5) | copy-start | bytes 4718596
  2.2 19.0 %collective-permute-start.2 = (f32[24,16,256]{2,1,0:T(8,128)S(1)}, f32[24,16,256]{2,1,0:T(8,128)S(1)}, u32[]{:S(2)}, u32[]{:S(2)}) collective-permute-start(f32[24,16,256]{2,1,0:T(8,128)S(1)} %get-tuple-element.33), channel_id=1, source_target_pairs={{0,8},{8,0},{16,24},{24,16},{1,9},{9,1},{17,25},{25,17},{2,10},{10... | collective-permute-start | bytes 1179656 | tf_op jit(solution)/shard_map/ppermute | solution.py:334
  5.2 19.0 %collective-permute-start.3 = (f32[24,16,256]{2,1,0:T(8,128)S(1)}, f32[24,16,256]{2,1,0:T(8,128)S(1)}, u32[]{:S(2)}, u32[]{:S(2)}) collective-permute-start(f32[24,16,256]{2,1,0:T(8,128)S(1)} %get-tuple-element.34), channel_id=1, source_target_pairs={{0,16},{8,24},{16,0},{24,8},{1,17},{9,25},{17,1},{25,9},{2,18},{10... | collective-permute-start | bytes 1179656 | tf_op jit(solution)/shard_map/ppermute | solution.py:334
  6.7 17.5 %collective-permute-start.4 = (f32[24,16,256]{2,1,0:T(8,128)S(1)}, f32[24,16,256]{2,1,0:T(8,128)S(1)}, u32[]{:S(2)}, u32[]{:S(2)}) collective-permute-start(f32[24,16,256]{2,1,0:T(8,128)S(1)} %get-tuple-element.35), channel_id=1, source_target_pairs={{0,24},{8,16},{16,8},{24,0},{1,25},{9,17},{17,9},{25,1},{2,26},{10... | collective-permute-start | bytes 1179656 | tf_op jit(solution)/shard_map/ppermute | solution.py:334
  6.7 1.7 %copy-start = (f32[40,16,1024]{2,1,0:T(8,128)S(1)}, f32[40,16,1024]{2,1,0:T(8,128)}, u32[]{:S(2)}) copy-start(f32[40,16,1024]{2,1,0:T(8,128)} %acet.3) | copy-start | bytes 7864324
  8.5 3.1 %copy-start.1 = (f32[40,16,1024]{2,1,0:T(8,128)S(1)}, f32[40,16,1024]{2,1,0:T(8,128)}, u32[]{:S(2)}) copy-start(f32[40,16,1024]{2,1,0:T(8,128)} %acet.3) | copy-start | bytes 7864324
  8.5 3.1 %copy-start.6 = (f32[40,40]{1,0:T(8,128)S(1)}, f32[40,40]{1,0:T(8,128)}, u32[]{:S(2)}) copy-start(f32[40,40]{1,0:T(8,128)} %reaction.1) | copy-start | bytes 19204
  8.6 6.3 %collective-permute-start = (f32[64,1024]{1,0:T(8,128)S(1)}, f32[64,1024]{1,0:T(8,128)S(1)}, u32[]{:S(2)}, u32[]{:S(2)}) collective-permute-start(f32[64,1024]{1,0:T(8,128)S(1)} %get-tuple-element.25), channel_id=1, source_target_pairs={{0,1},{1,2},{2,3},{3,4},{4,5},{5,6},{6,7},{8,9},{9,10},{10,11},{11... | collective-permute-start | bytes 786440 | tf_op jit(solution)/shard_map/ppermute | solution.py:342
  10.0 4.4 %copy-start.3 = (f32[96,96]{1,0:T(8,128)S(1)}, f32[96,96]{1,0:T(8,128)}, u32[]{:S(2)}) copy-start(f32[96,96]{1,0:T(8,128)} %kernel.1) | copy-start | bytes 110596
  10.1 4.4 %copy-start.4 = (f32[96,96]{1,0:T(8,128)S(1)}, f32[96,96]{1,0:T(8,128)}, u32[]{:S(2)}) copy-start(f32[96,96]{1,0:T(8,128)} %split.1) | copy-start | bytes 110596
  10.1 4.4 %copy-start.5 = (s32[96,96]{1,0:T(8,128)S(1)}, s32[96,96]{1,0:T(8,128)}, u32[]{:S(2)}) copy-start(s32[96,96]{1,0:T(8,128)} %target.1) | copy-start | bytes 110596
  10.1 4.4 %copy-start.8 = (f32[96]{0:T(128)S(1)}, f32[96]{0:T(128)}, u32[]{:S(2)}) copy-start(f32[96]{0:T(128)} %param.14) | copy-start | bytes 1156
  10.1 5.8 %copy-start.9 = (f32[40]{0:T(128)S(1)}, f32[40]{0:T(128)}, u32[]{:S(2)}) copy-start(f32[40]{0:T(128)} %diffusivity.1) | copy-start | bytes 484
  10.1 5.8 %collective-permute-start.1 = (f32[64,1024]{1,0:T(8,128)S(1)}, f32[64,1024]{1,0:T(8,128)S(1)}, u32[]{:S(2)}, u32[]{:S(2)}) collective-permute-start(f32[64,1024]{1,0:T(8,128)S(1)} %get-tuple-element.26), channel_id=1, source_target_pairs={{1,0},{2,1},{3,2},{4,3},{5,4},{6,5},{7,6},{9,8},{10,9},{11,10},{12... | collective-permute-start | bytes 786440 | tf_op jit(solution)/shard_map/ppermute | solution.py:343
  26.2 7.7 %collective-permute-start.8 = (f32[200,256]{1,0:T(8,128)S(1)}, f32[200,256]{1,0:T(8,128)S(1)}, u32[]{:S(2)}, u32[]{:S(2)}) collective-permute-start(f32[200,256]{1,0:T(8,128)S(1)} %get-tuple-element.41), channel_id=1, source_target_pairs={{0,8},{8,0},{16,24},{24,16},{1,9},{9,1},{17,25},{25,17},{2,10},{10... | collective-permute-start | bytes 614408 | tf_op jit(solution)/shard_map/ppermute | solution.py:334
  27.5 7.8 %collective-permute-start.9 = (f32[200,256]{1,0:T(8,128)S(1)}, f32[200,256]{1,0:T(8,128)S(1)}, u32[]{:S(2)}, u32[]{:S(2)}) collective-permute-start(f32[200,256]{1,0:T(8,128)S(1)} %get-tuple-element.42), channel_id=1, source_target_pairs={{0,16},{8,24},{16,0},{24,8},{1,17},{9,25},{17,1},{25,9},{2,18},{10... | collective-permute-start | bytes 614408 | tf_op jit(solution)/shard_map/ppermute | solution.py:334
  28.3 10.2 %copy-start.7 = (f32[40]{0:T(128)S(1)}, f32[40]{0:T(128)}, u32[]{:S(2)}) copy-start(f32[40]{0:T(128)} %stoich.3) | copy-start | bytes 484
  28.3 10.2 %collective-permute-start.10 = (f32[200,256]{1,0:T(8,128)S(1)}, f32[200,256]{1,0:T(8,128)S(1)}, u32[]{:S(2)}, u32[]{:S(2)}) collective-permute-start(f32[200,256]{1,0:T(8,128)S(1)} %get-tuple-element.43), channel_id=1, source_target_pairs={{0,24},{8,16},{16,8},{24,0},{1,25},{9,17},{17,9},{25,1},{2,26},{10... | collective-permute-start | bytes 614408 | tf_op jit(solution)/shard_map/ppermute | solution.py:334
  31.7 10.2 %collective-permute-start.5 = (f32[200,256]{1,0:T(8,128)S(1)}, f32[200,256]{1,0:T(8,128)S(1)}, u32[]{:S(2)}, u32[]{:S(2)}) collective-permute-start(f32[200,256]{1,0:T(8,128)S(1)} %get-tuple-element.37), channel_id=1, source_target_pairs={{0,8},{8,0},{16,24},{24,16},{1,9},{9,1},{17,25},{25,17},{2,10},{10... | collective-permute-start | bytes 614408 | tf_op jit(solution)/shard_map/ppermute | solution.py:334
  33.0 15.5 %collective-permute-start.6 = (f32[200,256]{1,0:T(8,128)S(1)}, f32[200,256]{1,0:T(8,128)S(1)}, u32[]{:S(2)}, u32[]{:S(2)}) collective-permute-start(f32[200,256]{1,0:T(8,128)S(1)} %get-tuple-element.38), channel_id=1, source_target_pairs={{0,16},{8,24},{16,0},{24,8},{1,17},{9,25},{17,1},{25,9},{2,18},{10... | collective-permute-start | bytes 614408 | tf_op jit(solution)/shard_map/ppermute | solution.py:334
  33.8 14.6 %collective-permute-start.7 = (f32[200,256]{1,0:T(8,128)S(1)}, f32[200,256]{1,0:T(8,128)S(1)}, u32[]{:S(2)}, u32[]{:S(2)}) collective-permute-start(f32[200,256]{1,0:T(8,128)S(1)} %get-tuple-element.39), channel_id=1, source_target_pairs={{0,24},{8,16},{16,8},{24,0},{1,25},{9,17},{17,9},{25,1},{2,26},{10... | collective-permute-start | bytes 614408 | tf_op jit(solution)/shard_map/ppermute | solution.py:334

commit v3 on v1

v3 whole, which is shorter than its diff:
```python
import functools

import jax
import jax.numpy as jnp
from jax import lax
from jax.experimental import pallas as pl
from jax.experimental.pallas import tpu as pltpu
from jax.sharding import PartitionSpec as P

F32 = jnp.float32
BF16 = jnp.bfloat16
SUB = 8
LANE = 128
GROUP = 2
SHIFTS = 5
ANY = pl.BlockSpec(memory_space=pl.ANY)
VMEM = pl.BlockSpec(memory_space=pltpu.VMEM)
SMEM = pl.BlockSpec(memory_space=pltpu.SMEM)
HBM = pl.BlockSpec(memory_space=pltpu.HBM)
PARAMS = pltpu.CompilerParams(vmem_limit_bytes=16 * 1024 * 1024)


def halves(x):
    high = x.astype(BF16)
    return high, (x - high.astype(F32)).astype(BF16)


class Plan:
    def __init__(self, n, rows, width):
        self.n = n
        self.across = min(n, width // LANE)
        self.rows = rows // (n // self.across)
        self.cols = width // self.across
        self.blocks = [(r, c) for r in range(self.rows // SUB) for c in range(self.cols // LANE)]

    def parts(self, ends):
        stops = [round(end * len(self.blocks)) for end in ends]
        whole = list(range(len(self.blocks)))
        return [p for p in (whole[x:y] for x, y in zip([0] + stops, stops + [None])) if p]

    def place(self, owner, block):
        r, c = self.blocks[block]
        row = (owner // self.across) * self.rows + r * SUB
        col = (owner % self.across) * self.cols + c * LANE
        return pl.ds(pl.multiple_of(row, SUB), SUB), pl.ds(pl.multiple_of(col, LANE), LANE)


def peer(k):
    return lax.axis_index("sec") ^ k


def cut_kernel(plan, pieces, soot, *rest):
    outs, sem = rest[:-1], rest[-1]
    copies = []
    for out, (k, part) in zip(outs, pieces):
        for b, block in enumerate(part):
            rows, cols = plan.place(peer(k), block)
            copies.append(pltpu.make_async_copy(soot.at[:, rows, cols], out.at[b], sem.at[len(copies)]))
            copies[-1].start()
    for copy in copies:
        copy.wait()


def cut(plan, pieces, soot):
    shapes = [jax.ShapeDtypeStruct((len(part), soot.shape[0], SUB, LANE), F32) for _, part in pieces]
    return pl.pallas_call(
        functools.partial(cut_kernel, plan, pieces),
        out_shape=shapes,
        in_specs=[HBM],
        out_specs=[VMEM] * len(shapes),
        scratch_shapes=[pltpu.SemaphoreType.DMA((sum(len(part) for _, part in pieces),))],
        compiler_params=PARAMS,
        name="cut",
    )(pltpu.with_memory_space_constraint(soot, pltpu.HBM))


def edge_kernel(soot, species, after, inner, outer):
    local, rows, _ = soot.shape
    odd = lax.axis_index("xs") % 2 == 1
    for ref, at in ((soot, 0), (species, local)):
        count = ref.shape[0]
        head, tail = ref[:, 0, :], ref[:, rows - 1, :]
        inner[at : at + count, :] = jnp.where(odd, head, tail)
        outer[at : at + count, :] = jnp.where(odd, tail, head)


def edges(soot, species, after):
    shape = jax.ShapeDtypeStruct((soot.shape[0] + species.shape[0], soot.shape[2]), F32)
    return pl.pallas_call(
        edge_kernel,
        out_shape=[shape, shape],
        in_specs=[VMEM, VMEM, ANY],
        out_specs=[VMEM, VMEM],
        compiler_params=PARAMS,
        name="edges",
    )(soot, species, after)


def weight_kernel(kernel, split, target, growth, reaction, stack, rate, rate_before, spread_out, scratch):
    size = kernel.shape[0]
    row = lax.broadcasted_iota(jnp.int32, (size, size), 0)
    col = lax.broadcasted_iota(jnp.int32, (size, size), 1)
    k, sp = kernel[...], split[...]
    t = target[...].astype(F32)
    rowf = row.astype(F32)
    k_t, sp_t, t_t = k.T, sp.T, t.T
    low, high = 0.5 * k * sp, 0.5 * k * (1.0 - sp)
    low_t, high_t = 0.5 * k_t * sp_t, 0.5 * k_t * (1.0 - sp_t)

    def fed(shift):
        at = rowf + shift
        own = jnp.where(t == at, low, 0.0) + jnp.where(t + 1.0 == at, high, 0.0)
        other = jnp.where(t_t == at, low_t, 0.0) + jnp.where(t_t + 1.0 == at, high_t, 0.0)
        return jnp.where(col <= row, own, 0.0) + jnp.where(col < row, other, 0.0)

    scratch[...] = jnp.zeros_like(scratch)
    scratch[0:size, :] = fed(0) - k
    for shift in range(1, SHIFTS):
        scratch[shift * size + shift : (shift + 1) * size, :] = fed(shift)[: size - shift]
    last = SHIFTS * size
    scratch[last : last + SUB - 1, :] = fed(-1)[size - SUB + 1 :]
    w_high, w_low = halves(scratch[...])
    stack[:, :size] = w_high
    stack[:, size : 2 * size] = w_high
    stack[:, 2 * size :] = w_low
    diagonal = jnp.where(row == col, jnp.broadcast_to(growth[...], (size, size)), 0.0)
    column = jnp.sum(diagonal, axis=1, keepdims=True)
    rate[...] = jnp.broadcast_to(column, rate.shape)
    before = jnp.where(row == col + 1, jnp.broadcast_to(growth[...], (size, size)), 0.0)
    column = jnp.sum(before, axis=1, keepdims=True)
    rate_before[...] = jnp.broadcast_to(column, rate_before.shape)


    kinds = reaction.shape[0]
    wide = kinds * SUB
    tall = lax.broadcasted_iota(jnp.int32, (wide, kinds), 0) // SUB == lax.broadcasted_iota(jnp.int32, (wide, kinds), 1)
    flat = lax.broadcasted_iota(jnp.int32, (kinds, wide), 1) // SUB == lax.broadcasted_iota(jnp.int32, (kinds, wide), 0)
    tall, flat = tall.astype(F32).astype(BF16), flat.astype(F32).astype(BF16)
    same = lax.broadcasted_iota(jnp.int32, (wide, wide), 0) % SUB == lax.broadcasted_iota(jnp.int32, (wide, wide), 1) % SUB
    wider = []
    for half in halves(reaction[...]):
        rows = jnp.dot(tall, half, preferred_element_type=F32).astype(BF16)
        wider.append(jnp.where(same, jnp.dot(rows, flat, preferred_element_type=F32), 0.0))
    spread_out[...] = jnp.concatenate([wider[0], wider[0], wider[1]], axis=1).astype(BF16)


def weights(plan, kernel, split, target, growth, reaction):
    size, kinds = kernel.shape[0], reaction.shape[0]
    depth = SHIFTS * size + 2 * SUB
    return pl.pallas_call(
        weight_kernel,
        out_shape=[
            jax.ShapeDtypeStruct((depth, 3 * size), BF16),
            jax.ShapeDtypeStruct((size, GROUP * LANE), F32),
            jax.ShapeDtypeStruct((size, GROUP * LANE), F32),
            jax.ShapeDtypeStruct((kinds * SUB, 3 * kinds * SUB), BF16),
        ],
        in_specs=[VMEM] * 5,
        out_specs=[VMEM] * 4,
        scratch_shapes=[pltpu.VMEM((depth, size), F32)],
        compiler_params=PARAMS,
        name="weights",
    )(kernel, split, target, growth.reshape(1, size), reaction)


def rate_kernel(plan, sources, count, part, stack, rate, rate_before, soot, acet, after, *refs):
    n = plan.n
    pieces, outs = refs[:count], refs[count : count + n]
    whole, result, near, shifted = refs[count + n :]
    size = rate.shape[0]
    local = size // n
    for b, block in enumerate(part):
        rows, cols = plan.place(lax.axis_index("sec"), block)
        near[b] = acet[0, rows, cols]
    pad = SHIFTS - 1
    for b in range(len(part)):
        whole[b, : pad * SUB, :] = jnp.zeros((pad * SUB, LANE), F32)
        whole[b, (pad + size) * SUB :, :] = jnp.zeros((SUB, LANE), F32)
        for k in range(n):
            start = pl.multiple_of((pad + local * peer(k)) * SUB, SUB)
            if k:
                source, at = sources[k, b]
                piece = pieces[source][at]
            else:
                rows, cols = plan.place(lax.axis_index("sec"), part[b])
                piece = soot[:, rows, cols]
            whole[b, pl.ds(start, local * SUB), :] = piece.reshape(local * SUB, LANE)
    def sections(first, count, pair):
        found = [whole[b, pl.ds((pad + first) * SUB + row, count, stride=SUB), :] for b, row in pair]
        return jnp.concatenate(found, axis=1)

    units = [(b, row) for row in range(SUB) for b in range(len(part))]
    for i in range(GROUP):
        shifted[:, i, :pad, :] = jnp.zeros((2, pad, LANE), F32)
        shifted[:, i, pad + size :, :] = jnp.zeros((2, SHIFTS + SUB - pad, LANE), F32)
    for step, pair in enumerate([units[i : i + GROUP] for i in range(0, len(units), GROUP)]):
        here = sections(0, size, pair)
        moved = shifted.at[step % 2]
        for i in range(GROUP):
            moved[i, pad : pad + size, :] = here[:, i * LANE : (i + 1) * LANE]

        def near_by(first, count):
            return jnp.concatenate([moved[i, pad + first : pad + first + count, :] for i in range(GROUP)], axis=1)

        high, low = halves(here)
        product = jnp.dot(stack[...], jnp.concatenate([high, low, high], axis=0), preferred_element_type=F32)
        total = here * product[:size]
        for shift in range(1, SHIFTS):
            total += near_by(-shift, size) * product[shift * size : (shift + 1) * size]
        last = SHIFTS * size
        extra = near_by(size - SUB + 1, SUB) * product[last : last + SUB]
        total = jnp.concatenate([total[: size - SUB], total[size - SUB :] + extra], axis=0)
        growing = jnp.concatenate([near[b, row : row + 1, :] for b, row in pair], axis=1)
        grown = rate[...] * here
        total -= growing * (grown - rate_before[...] * near_by(-1, size))
        used = growing * jnp.sum(grown, axis=0, keepdims=True)
        for i, (b, row) in enumerate(pair):
            lanes = slice(i * LANE, (i + 1) * LANE)
            result[b, pl.ds(row, size, stride=SUB), :] = total[:, lanes]
            for k in range(n):
                outs[k][b, local, row : row + 1, :] = used[:, lanes]
    for b in range(len(part)):
        for k in range(n):
            start = pl.multiple_of(local * peer(k) * SUB, SUB)
            outs[k][b, :local] = result[b, pl.ds(start, local * SUB), :].reshape(local, SUB, LANE)


def rates(plan, part, prepared, soot, acet, after, pieces, got):
    size = prepared[1].shape[0]
    local = size // plan.n
    sources, used = {}, []
    for (k, blocks), x in zip(pieces, got):
        if set(blocks) & set(part):
            for block in set(blocks) & set(part):
                sources[k, part.index(block)] = (len(used), blocks.index(block))
            used.append(x)
    shape = jax.ShapeDtypeStruct((len(part), local + 1, SUB, LANE), F32)
    return pl.pallas_call(
        functools.partial(rate_kernel, plan, sources, len(used), part),
        out_shape=[shape] * plan.n,
        in_specs=[VMEM] * 5 + [ANY] + [VMEM] * len(used),
        out_specs=[VMEM] * plan.n,
        scratch_shapes=[
            pltpu.VMEM((len(part), (SHIFTS + size) * SUB, LANE), F32),
            pltpu.VMEM((len(part), size * SUB, LANE), F32),
            pltpu.VMEM((len(part), SUB, LANE), F32),
            pltpu.VMEM((2, GROUP, SHIFTS + SUB + size, LANE), F32),
        ],
        compiler_params=PARAMS,
        name="rates",
    )(*prepared, soot, acet, after, *used)


def gate(pieces, late):
    return pl.pallas_call(
        lambda *refs: None,
        out_shape=[jax.ShapeDtypeStruct(x.shape, x.dtype) for x in pieces],
        in_specs=[VMEM] * len(pieces) + [ANY] * len(late),
        out_specs=[VMEM] * len(pieces),
        input_output_aliases={i: i for i in range(len(pieces))},
        compiler_params=PARAMS,
        name="gate",
    )(*pieces, *late)


def base_kernel(diffusivity, kinetics, soot, species, soot_base, species_base):
    local, rows, width = soot.shape
    kinds = species.shape[0]
    lanes = lax.broadcasted_iota(jnp.int32, (rows, LANE), 1)
    none = jnp.zeros((1, width), F32)

    def spread(v, factor):
        up = jnp.concatenate([none, v[:-1]], axis=0)
        down = jnp.concatenate([v[1:], none], axis=0)
        left, right = pltpu.roll(v, 1, 1), pltpu.roll(v, width - 1, 1)
        left = jnp.concatenate([jnp.where(lanes == 0, 0.0, left[:, :LANE]), left[:, LANE:]], axis=1)
        right = jnp.concatenate([right[:, :-LANE], jnp.where(lanes == LANE - 1, 0.0, right[:, -LANE:])], axis=1)
        return (1.0 - 4.0 * factor) * v + factor * ((up + down) + (left + right))

    def one_section(i, carry):
        soot_base[i] = spread(soot[i], 0.1)
        return carry

    lax.fori_loop(0, local, one_section, 0, unroll=8)

    for row in range(0, rows, SUB):
        for col in range(0, width, 2 * LANE):
            tile = (slice(None), slice(row, row + SUB), slice(col, col + 2 * LANE))
            high, low = halves(species[tile].reshape(kinds * SUB, 2 * LANE))
            product = jnp.dot(kinetics[...], jnp.concatenate([high, low, high], axis=0), preferred_element_type=F32)
            species_base[tile] = product.reshape(kinds, SUB, 2 * LANE)

    def one_species(i, carry):
        species_base[i] += spread(species[i], diffusivity[i])
        return carry

    lax.fori_loop(0, kinds, one_species, 0, unroll=8)


def bases(diffusivity, kinetics, soot, species):
    return pl.pallas_call(
        base_kernel,
        out_shape=[jax.ShapeDtypeStruct(soot.shape, F32), jax.ShapeDtypeStruct(species.shape, F32)],
        in_specs=[SMEM, VMEM, VMEM, VMEM],
        out_specs=[VMEM, VMEM],
        compiler_params=PARAMS,
        name="bases",
    )(diffusivity, kinetics, soot, species)


def rim_kernel(inner, outer, diffusivity, soot_in, species_in, soot_base, species_base):
    local, rows, _ = soot_base.shape
    odd = lax.axis_index("xs") % 2 == 1
    for ref, at in ((soot_base, 0), (species_base, local)):
        for i in range(ref.shape[0]):
            factor = diffusivity[i] if at else 0.1
            one, other = inner[at + i : at + i + 1, :], outer[at + i : at + i + 1, :]
            ref[i, 0:1, :] += factor * jnp.where(odd, one, other)
            ref[i, rows - 1 : rows, :] += factor * jnp.where(odd, other, one)


def rim(inner, outer, diffusivity, soot_base, species_base):
    return pl.pallas_call(
        rim_kernel,
        out_shape=[jax.ShapeDtypeStruct(soot_base.shape, F32), jax.ShapeDtypeStruct(species_base.shape, F32)],
        in_specs=[VMEM, VMEM, SMEM, VMEM, VMEM],
        out_specs=[VMEM, VMEM],
        input_output_aliases={3: 0, 4: 1},
        compiler_params=PARAMS,
        name="rim",
    )(inner, outer, diffusivity, soot_base, species_base)


def last_kernel(plan, part, peers, stoich, soot_base, species_base, *refs):
    pieces = refs[: len(peers)]
    soot_out, species_out, soot_held, species_held, sems = refs[-5:]
    local, kinds = soot_out.shape[0], species_out.shape[0]
    copies = []
    for k, far in enumerate(peers):
        for b, block in enumerate(part):
            rows, cols = plan.place(peer(far), block)
            soot_held[k, b] = soot_base[:, rows, cols] + pieces[k][b, :local]
            copies.append(pltpu.make_async_copy(soot_held.at[k, b], soot_out.at[:, rows, cols], sems.at[0, k, b]))
            copies[-1].start()
            used = pieces[k][b, local]
            for kind in range(kinds):
                species_held[k, b, kind] = species_base[kind, rows, cols] - stoich[kind] * used
            copies.append(pltpu.make_async_copy(species_held.at[k, b], species_out.at[:, rows, cols], sems.at[1, k, b]))
            copies[-1].start()
    for copy in copies:
        copy.wait()


def last(plan, part, peers, stoich, soot_base, species_base, pieces, before):
    local, kinds = soot_base.shape[0], species_base.shape[0]
    first = 3 + len(pieces)
    return pl.pallas_call(
        functools.partial(last_kernel, plan, part, peers),
        out_shape=[jax.ShapeDtypeStruct(soot_base.shape, F32), jax.ShapeDtypeStruct(species_base.shape, F32)],
        in_specs=[SMEM, VMEM, VMEM] + [VMEM] * len(pieces) + [HBM] * len(before),
        out_specs=[HBM, HBM],
        scratch_shapes=[
            pltpu.VMEM((len(peers), len(part), local, SUB, LANE), F32),
            pltpu.VMEM((len(peers), len(part), kinds, SUB, LANE), F32),
            pltpu.SemaphoreType.DMA((2, len(peers), len(part))),
        ],
        input_output_aliases={first + i: i for i in range(len(before))},
        compiler_params=PARAMS,
        name="last",
    )(stoich, soot_base, species_base, *pieces, *before)


def shards(soot, species, kernel, split, target, growth, diffusivity, reaction, stoich):
    n = lax.axis_size("sec")
    count = lax.axis_size("xs")
    plan = Plan(n, soot.shape[1], soot.shape[2])

    def swap(x, k):
        return lax.ppermute(x, "sec", [(i, i ^ k) for i in range(n)])

    order = [k for k in (2, 1, 3) if k < n] + list(range(4, n))
    pieces = [(k, part) for k in order for part in plan.parts((0.75,) if k == n - 1 else ())]
    sent = cut(plan, pieces, soot)
    got = [swap(x, k) for (k, _), x in zip(pieces, sent)]

    inner, outer = edges(soot, species, sent[0])
    pairs = [[(i, i + 1) for i in range(first, count - 1, 2)] for first in (0, 1)]
    inner, outer = (lax.ppermute(x, "xs", [q for i, j in p for q in ((i, j), (j, i))]) for x, p in zip((inner, outer), pairs))
    *prepared, kinetics = weights(plan, kernel, split, target, growth, reaction)
    base = bases(diffusivity, kinetics, soot, species)
    base = rim(inner, outer, diffusivity, *base)

    back = []
    for part in plan.parts((0.5,)):
        outs = rates(plan, part, prepared, soot, species, base[0] if not back else stoich, pieces, got)
        late = [x for (_, blocks), x in zip(pieces, got) if not set(blocks) & set(part)]
        away = gate(outs[1:], late) if late else outs[1:]
        back.append((part, [outs[0]] + [swap(x, k) for k, x in enumerate(away, 1)]))
    result = ()
    for i, (part, moved) in enumerate(back):
        early = 2 if i == len(back) - 1 else n
        for peers in (range(early), range(early, n)):
            if peers:
                result = last(plan, part, peers, stoich, *base, [moved[k] for k in peers], result)
    return tuple(result)


def solution(mesh):
    return jax.shard_map(
        shards,
        mesh=mesh,
        in_specs=(P("sec", "xs", None), P(None, "xs", None), P(), P(), P(), P(), P(), P(), P()),
        out_specs=(P("sec", "xs", None), P(None, "xs", None)),
        check_vma=False,
    )
```

time: 58 us -> 46.1 us (0.79)
  the two profiles are of different devices: /device:TPU:26 before, /device:TPU:0 now
where the time goes in v3:
time: 46.1 us; the launch traced here: 45.9 us
  Pallas kernels  17.1 us (37%)
  starting transfers between devices  14.9 us (32%)
  waiting for transfers between devices  11.4 us (25%)
  local copies, waits for them, and re-layouts  1.78 us (4%)
  between operations  0.82 us (2%)
    ppermute x10, starting transfers between devices, swap(): return lax.ppermute(x, 'sec', [(i, i ^ k) for i in range(n)])  14 us
    ppermute x10, waiting for transfers between devices, swap(): return lax.ppermute(x, 'sec', [(i, i ^ k) for i in range(n)])  10.8 us
    pallas_call x3, Pallas kernels, last(): pl.pallas_call(functools.partial(last_kernel, plan, part, peers), out_sha...  5.24 us
    pallas_call x1, Pallas kernels, bases(): pl.pallas_call(base_kernel, out_shape=[jax.ShapeDtypeStruct(soot.shape, F...  5.02 us
    pallas_call x2, Pallas kernels, rates(): pl.pallas_call(functools.partial(rate_kernel, plan, sources, len(used), p...  3.65 us
    unnamed x20, local copies, waits for them, and re-layouts  1.78 us
    pallas_call x1, Pallas kernels, cut(): pl.pallas_call(functools.partial(cut_kernel, plan, pieces), out_shape=sha...  1.58 us
  transfers between devices with their start and end apart: 12, of which 7 were waited for; matrix products, arithmetic and copies ran while one was open for 0% of the time, Pallas kernels for 30%

profile of v3, /device:TPU:0, one launch (start us, length us, event | category | flops | bytes accessed | tf_op | source)
XLA Modules:
  0.0 45.9 jit_solution(4988505493601197566)
XLA Ops:
  0.6 1.6 %cut.1 = (f32[4,24,8,128]{3,2,1,0:T(8,128)S(1)}, f32[4,24,8,128]{3,2,1,0:T(8,128)S(1)}, f32[3,24,8,128]{3,2,1,0:T(8,128)S(1)}, f32[1,24,8,128]{3,2,1,0:T(8,128)S(1)}) custom-call(f32[24,16,1024]{2,1,0:T(8,128)} %soot.9), custom_call_target="tpu_custom_call" | custom-call | tf_op jit(solution)/shard_map/cut/pallas_call | solution.py:66
  2.2 3.0 %collective-permute-start.3 = (f32[4,24,8,128]{3,2,1,0:T(8,128)S(1)}, f32[4,24,8,128]{3,2,1,0:T(8,128)S(1)}, u32[]{:S(2)}, u32[]{:S(2)}) collective-permute-start(f32[4,24,8,128]{3,2,1,0:T(8,128)S(1)} %get-tuple-element.42), channel_id=1, source_target_pairs={{0,8},{8,0},{16,24},{24,16},{1,9},{9,1},{17,25},{25,17},{2,10},{10... | collective-permute-start | bytes 1179656 | tf_op jit(solution)/shard_map/ppermute | solution.py:379
  5.3 1.5 %collective-permute-start.2 = (f32[4,24,8,128]{3,2,1,0:T(8,128)S(1)}, f32[4,24,8,128]{3,2,1,0:T(8,128)S(1)}, u32[]{:S(2)}, u32[]{:S(2)}) collective-permute-start(f32[4,24,8,128]{3,2,1,0:T(8,128)S(1)} %get-tuple-element.31.after), channel_id=1, source_target_pairs={{0,16},{8,24},{16,0},{24,8},{1,17},{9,25},{17,1},{25,9},{2,18},{10... | collective-permute-start | bytes 1179656 | tf_op jit(solution)/shard_map/ppermute | solution.py:379
  6.8 1.7 %copy-done = f32[40,16,1024]{2,1,0:T(8,128)S(1)} copy-done((f32[40,16,1024]{2,1,0:T(8,128)S(1)}, f32[40,16,1024]{2,1,0:T(8,128)}, u32[]{:S(2)}) %copy-start) | copy-done | bytes 2621464
  8.9 0.8 %collective-permute-start.1 = (f32[64,1024]{1,0:T(8,128)S(1)}, f32[64,1024]{1,0:T(8,128)S(1)}, u32[]{:S(2)}, u32[]{:S(2)}) collective-permute-start(f32[64,1024]{1,0:T(8,128)S(1)} %get-tuple-element.33), channel_id=1, source_target_pairs={{1,2},{2,1},{3,4},{4,3},{5,6},{6,5},{9,10},{10,9},{11,12},{12,11},... | collective-permute-start | bytes 786440 | tf_op jit(solution)/shard_map/ppermute | solution.py:388
  9.7 0.6 %collective-permute-done.inner = f32[64,1024]{1,0:T(8,128)S(1)} collective-permute-done((f32[64,1024]{1,0:T(8,128)S(1)}, f32[64,1024]{1,0:T(8,128)S(1)}, u32[]{:S(2)}, u32[]{:S(2)}) %collective-permute-start) | collective-permute-done | bytes 262176 | tf_op jit(solution)/shard_map/ppermute | solution.py:388
  10.3 2.2 %collective-permute-start.5 = (f32[1,24,8,128]{3,2,1,0:T(8,128)S(1)}, f32[1,24,8,128]{3,2,1,0:T(8,128)S(1)}, u32[]{:S(2)}, u32[]{:S(2)}) collective-permute-start(f32[1,24,8,128]{3,2,1,0:T(8,128)S(1)} %get-tuple-element.44), channel_id=1, source_target_pairs={{0,24},{8,16},{16,8},{24,0},{1,25},{9,17},{17,9},{25,1},{2,26},{10... | collective-permute-start | bytes 294920 | tf_op jit(solution)/shard_map/ppermute | solution.py:379
  12.5 0.6 %weights.1 = (bf16[496,288]{1,0:T(8,128)(2,1)S(1)}, f32[96,256]{1,0:T(8,128)S(1)}, f32[96,256]{1,0:T(8,128)S(1)}, bf16[320,960]{1,0:T(8,128)(2,1)S(1)}) custom-call(f32[96,96]{1,0:T(8,128)S(1)} %copy-done.3, f32[96,96]{1,0:T(8,128)S(1)} %copy-done.4, s32[96,96]{1,0:T(8,128)S(1)} %copy-done.5, f32[1,96]{1,0:T(1,128)S(1)} %bitcast.1, f32[40,40]{1,0:T(8,128)S(1)} %copy-done.6), custom_call_target="tpu_custom_call" | custom-call | tf_op jit(solution)/shard_map/weights/pallas_call | solution.py:150
  13.2 5.0 %bases.1 = (f32[24,16,1024]{2,1,0:T(8,128)S(1)}, f32[40,16,1024]{2,1,0:T(8,128)S(1)}) custom-call(f32[40]{0:T(128)S(1)} %copy-done.8, bf16[320,960]{1,0:T(8,128)(2,1)S(1)} %get-tuple-element.34.kinetics, f32[24,16,1024]{2,1,0:T(8,128)S(1)} %copy-done.2, f32[40,16,1024]{2,1,0:T(8,128)S(1)} %copy-done.1), custom_call_target="tpu_custom_call" | custom-call | tf_op jit(solution)/shard_map/bases/pallas_call | solution.py:301
  18.3 0.8 %rim.1 = (f32[24,16,1024]{2,1,0:T(8,128)S(1)}, f32[40,16,1024]{2,1,0:T(8,128)S(1)}) custom-call(f32[64,1024]{1,0:T(8,128)S(1)} %collective-permute-done.inner, f32[64,1024]{1,0:T(8,128)S(1)} %collective-permute-done.1.outer, f32[40]{0:T(128)S(1)} %copy-done.8, ...), custom_call_target="tpu_custom_call", output_to_operand_aliasing={{0}: (3, {}), {1}: (4, {})} | custom-call | tf_op jit(solution)/shard_map/rim/pallas_call | solution.py:323
  19.0 4.0 %collective-permute-done.4.refs_2_ = f32[3,24,8,128]{3,2,1,0:T(8,128)S(1)} collective-permute-done((f32[3,24,8,128]{3,2,1,0:T(8,128)S(1)}, f32[3,24,8,128]{3,2,1,0:T(8,128)S(1)}, u32[]{:S(2)}, u32[]{:S(2)}) %collective-permute-start.4) | collective-permute-done | bytes 294944 | tf_op jit(solution)/shard_map/ppermute | solution.py:379
  23.1 1.2 %collective-permute-done.2.refs_0_ = f32[4,24,8,128]{3,2,1,0:T(8,128)S(1)} collective-permute-done((f32[4,24,8,128]{3,2,1,0:T(8,128)S(1)}, f32[4,24,8,128]{3,2,1,0:T(8,128)S(1)}, u32[]{:S(2)}, u32[]{:S(2)}) %collective-permute-start.2) | collective-permute-done | bytes 393248 | tf_op jit(solution)/shard_map/ppermute | solution.py:379
  24.3 1.8 %rates.3 = (f32[2,25,8,128]{3,2,1,0:T(8,128)S(1)}, f32[2,25,8,128]{3,2,1,0:T(8,128)S(1)}, f32[2,25,8,128]{3,2,1,0:T(8,128)S(1)}, f32[2,25,8,128]{3,2,1,0:T(8,128)S(1)}) custom-call(bf16[496,288]{1,0:T(8,128)(2,1)S(1)} %get-tuple-element.39.stack, f32[96,256]{1,0:T(8,128)S(1)} %get-tuple-element.40.rate, f32[96,256]{1,0:T(8,128)S(1)} %get-tuple-element.41.rate_before, ...), custom_call_target="tpu_custom_call" | custom-call | tf_op jit(solution)/shard_map/rates/pallas_call | solution.py:238
  26.4 1.9 %collective-permute-start.10 = (f32[2,25,8,128]{3,2,1,0:T(8,128)S(1)}, f32[2,25,8,128]{3,2,1,0:T(8,128)S(1)}, u32[]{:S(2)}, u32[]{:S(2)}) collective-permute-start(f32[2,25,8,128]{3,2,1,0:T(8,128)S(1)} %get-tuple-element.54), channel_id=1, source_target_pairs={{0,16},{8,24},{16,0},{24,8},{1,17},{9,25},{17,1},{25,9},{2,18},{10... | collective-permute-start | bytes 614408 | tf_op jit(solution)/shard_map/ppermute | solution.py:379
  28.2 1.4 %collective-permute-start.11 = (f32[2,25,8,128]{3,2,1,0:T(8,128)S(1)}, f32[2,25,8,128]{3,2,1,0:T(8,128)S(1)}, u32[]{:S(2)}, u32[]{:S(2)}) collective-permute-start(f32[2,25,8,128]{3,2,1,0:T(8,128)S(1)} %get-tuple-element.55), channel_id=1, source_target_pairs={{0,24},{8,16},{16,8},{24,0},{1,25},{9,17},{17,9},{25,1},{2,26},{10... | collective-permute-start | bytes 614408 | tf_op jit(solution)/shard_map/ppermute | solution.py:379
  29.7 1.8 %rates.2 = (f32[2,25,8,128]{3,2,1,0:T(8,128)S(1)}, f32[2,25,8,128]{3,2,1,0:T(8,128)S(1)}, f32[2,25,8,128]{3,2,1,0:T(8,128)S(1)}, f32[2,25,8,128]{3,2,1,0:T(8,128)S(1)}) custom-call(bf16[496,288]{1,0:T(8,128)(2,1)S(1)} %get-tuple-element.39.stack, f32[96,256]{1,0:T(8,128)S(1)} %get-tuple-element.40.rate, f32[96,256]{1,0:T(8,128)S(1)} %get-tuple-element.41.rate_before, ...), custom_call_target="tpu_custom_call" | custom-call | tf_op jit(solution)/shard_map/rates/pallas_call | solution.py:238
  31.8 1.9 %collective-permute-start.6 = (f32[2,25,8,128]{3,2,1,0:T(8,128)S(1)}, f32[2,25,8,128]{3,2,1,0:T(8,128)S(1)}, u32[]{:S(2)}, u32[]{:S(2)}) collective-permute-start(f32[2,25,8,128]{3,2,1,0:T(8,128)S(1)} %get-tuple-element.45), channel_id=1, source_target_pairs={{0,16},{8,24},{16,0},{24,8},{1,17},{9,25},{17,1},{25,9},{2,18},{10... | collective-permute-start | bytes 614408 | tf_op jit(solution)/shard_map/ppermute | solution.py:379
  33.6 0.6 %collective-permute-done.9.refs_1_ = f32[2,25,8,128]{3,2,1,0:T(8,128)S(1)} collective-permute-done((f32[2,25,8,128]{3,2,1,0:T(8,128)S(1)}, f32[2,25,8,128]{3,2,1,0:T(8,128)S(1)}, u32[]{:S(2)}, u32[]{:S(2)}) %collective-permute-start.9) | collective-permute-done | bytes 204832 | tf_op jit(solution)/shard_map/ppermute | solution.py:379
  34.2 1.5 %collective-permute-start.7 = (f32[2,25,8,128]{3,2,1,0:T(8,128)S(1)}, f32[2,25,8,128]{3,2,1,0:T(8,128)S(1)}, u32[]{:S(2)}, u32[]{:S(2)}) collective-permute-start(f32[2,25,8,128]{3,2,1,0:T(8,128)S(1)} %get-tuple-element.46), channel_id=1, source_target_pairs={{0,24},{8,16},{16,8},{24,0},{1,25},{9,17},{17,9},{25,1},{2,26},{10... | collective-permute-start | bytes 614408 | tf_op jit(solution)/shard_map/ppermute | solution.py:379
  35.7 3.9 %collective-permute-done.11.refs_3_ = f32[2,25,8,128]{3,2,1,0:T(8,128)S(1)} collective-permute-done((f32[2,25,8,128]{3,2,1,0:T(8,128)S(1)}, f32[2,25,8,128]{3,2,1,0:T(8,128)S(1)}, u32[]{:S(2)}, u32[]{:S(2)}) %collective-permute-start.11) | collective-permute-done | bytes 204832 | tf_op jit(solution)/shard_map/ppermute | solution.py:379
  39.5 2.0 %last.3 = (f32[24,16,1024]{2,1,0:T(8,128)}, f32[40,16,1024]{2,1,0:T(8,128)}) custom-call(f32[40]{0:T(128)S(1)} %copy-done.7, f32[24,16,1024]{2,1,0:T(8,128)S(1)} %get-tuple-element.37.after.soot_base, f32[40,16,1024]{2,1,0:T(8,128)S(1)} %get-tuple-element.38.species_base, f32[2,25,8,128]{3,2,1,0:T(8,128)S(1)} %get-tuple-element.49.refs_0_, ...), custom_call_target="tpu_custom_call" | custom-call | tf_op jit(solution)/shard_map/last/pallas_call | solution.py:357
  41.6 1.6 %last.4 = (f32[24,16,1024]{2,1,0:T(8,128)}, f32[40,16,1024]{2,1,0:T(8,128)}) custom-call(f32[40]{0:T(128)S(1)} %copy-done.7, f32[24,16,1024]{2,1,0:T(8,128)S(1)} %get-tuple-element.37.after.soot_base, f32[40,16,1024]{2,1,0:T(8,128)S(1)} %get-tuple-element.38.species_base, ...), custom_call_target="tpu_custom_call", output_to_operand_aliasing={{0}: (5, {}), {1}: (6, {})} | custom-call | tf_op jit(solution)/shard_map/last/pallas_call | solution.py:357
  43.3 1.1 %collective-permute-done.6.refs_0_ = f32[2,25,8,128]{3,2,1,0:T(8,128)S(1)} collective-permute-done((f32[2,25,8,128]{3,2,1,0:T(8,128)S(1)}, f32[2,25,8,128]{3,2,1,0:T(8,128)S(1)}, u32[]{:S(2)}, u32[]{:S(2)}) %collective-permute-start.6) | collective-permute-done | bytes 204832 | tf_op jit(solution)/shard_map/ppermute | solution.py:379
  44.3 1.6 %last.5 = (f32[24,16,1024]{2,1,0:T(8,128)}, f32[40,16,1024]{2,1,0:T(8,128)}) custom-call(f32[40]{0:T(128)S(1)} %copy-done.7, f32[24,16,1024]{2,1,0:T(8,128)S(1)} %get-tuple-element.37.after.soot_base, f32[40,16,1024]{2,1,0:T(8,128)S(1)} %get-tuple-element.38.species_base, ...), custom_call_target="tpu_custom_call", output_to_operand_aliasing={{0}: (5, {}), {1}: (6, {})} | custom-call | tf_op jit(solution)/shard_map/last/pallas_call | solution.py:357
  (31 shorter events, 1.0 us)
Async XLA Ops:
  0.6 6.1 %copy-start.2 = (f32[24,16,1024]{2,1,0:T(8,128)S(1)}, f32[24,16,1024]{2,1,0:T(8,128)}, u32[]{:S(2)}) copy-start(f32[24,16,1024]{2,1,0:T(8,128)} %soot.9) | copy-start | bytes 4718596
  2.2 10.3 %copy-start.9 = (f32[96]{0:T(128)S(1)}, f32[96]{0:T(128)}, u32[]{:S(2)}) copy-start(f32[96]{0:T(128)} %param.14) | copy-start | bytes 1156
  2.2 11.0 %copy-start.8 = (f32[40]{0:T(128)S(1)}, f32[40]{0:T(128)}, u32[]{:S(2)}) copy-start(f32[40]{0:T(128)} %diffusivity.3) | copy-start | bytes 484
  2.2 20.8 %collective-permute-start.3 = (f32[4,24,8,128]{3,2,1,0:T(8,128)S(1)}, f32[4,24,8,128]{3,2,1,0:T(8,128)S(1)}, u32[]{:S(2)}, u32[]{:S(2)}) collective-permute-start(f32[4,24,8,128]{3,2,1,0:T(8,128)S(1)} %get-tuple-element.42), channel_id=1, source_target_pairs={{0,8},{8,0},{16,24},{24,16},{1,9},{9,1},{17,25},{25,17},{2,10},{10... | collective-permute-start | bytes 1179656 | tf_op jit(solution)/shard_map/ppermute | solution.py:379
  5.3 19.0 %collective-permute-start.2 = (f32[4,24,8,128]{3,2,1,0:T(8,128)S(1)}, f32[4,24,8,128]{3,2,1,0:T(8,128)S(1)}, u32[]{:S(2)}, u32[]{:S(2)}) collective-permute-start(f32[4,24,8,128]{3,2,1,0:T(8,128)S(1)} %get-tuple-element.31.after), channel_id=1, source_target_pairs={{0,16},{8,24},{16,0},{24,8},{1,17},{9,25},{17,1},{25,9},{2,18},{10... | collective-permute-start | bytes 1179656 | tf_op jit(solution)/shard_map/ppermute | solution.py:379
  6.8 1.7 %copy-start = (f32[40,16,1024]{2,1,0:T(8,128)S(1)}, f32[40,16,1024]{2,1,0:T(8,128)}, u32[]{:S(2)}) copy-start(f32[40,16,1024]{2,1,0:T(8,128)} %acet.3) | copy-start | bytes 7864324
  8.5 4.0 %copy-start.3 = (f32[96,96]{1,0:T(8,128)S(1)}, f32[96,96]{1,0:T(8,128)}, u32[]{:S(2)}) copy-start(f32[96,96]{1,0:T(8,128)} %kernel.1) | copy-start | bytes 110596
  8.5 4.0 %copy-start.4 = (f32[96,96]{1,0:T(8,128)S(1)}, f32[96,96]{1,0:T(8,128)}, u32[]{:S(2)}) copy-start(f32[96,96]{1,0:T(8,128)} %split.1) | copy-start | bytes 110596
  8.5 4.0 %copy-start.5 = (s32[96,96]{1,0:T(8,128)S(1)}, s32[96,96]{1,0:T(8,128)}, u32[]{:S(2)}) copy-start(s32[96,96]{1,0:T(8,128)} %target.1) | copy-start | bytes 110596
  8.5 4.0 %copy-start.6 = (f32[40,40]{1,0:T(8,128)S(1)}, f32[40,40]{1,0:T(8,128)}, u32[]{:S(2)}) copy-start(f32[40,40]{1,0:T(8,128)} %reaction.1) | copy-start | bytes 19204
  8.5 4.7 %copy-start.1 = (f32[40,16,1024]{2,1,0:T(8,128)S(1)}, f32[40,16,1024]{2,1,0:T(8,128)}, u32[]{:S(2)}) copy-start(f32[40,16,1024]{2,1,0:T(8,128)} %acet.3) | copy-start | bytes 7864324
  8.7 1.6 %collective-permute-start = (f32[64,1024]{1,0:T(8,128)S(1)}, f32[64,1024]{1,0:T(8,128)S(1)}, u32[]{:S(2)}, u32[]{:S(2)}) collective-permute-start(f32[64,1024]{1,0:T(8,128)S(1)} %get-tuple-element.32), channel_id=1, source_target_pairs={{0,1},{1,0},{2,3},{3,2},{4,5},{5,4},{6,7},{7,6},{8,9},{9,8},{10,11... | collective-permute-start | bytes 786440 | tf_op jit(solution)/shard_map/ppermute | solution.py:388
  8.8 14.3 %collective-permute-start.4 = (f32[3,24,8,128]{3,2,1,0:T(8,128)S(1)}, f32[3,24,8,128]{3,2,1,0:T(8,128)S(1)}, u32[]{:S(2)}, u32[]{:S(2)}) collective-permute-start(f32[3,24,8,128]{3,2,1,0:T(8,128)S(1)} %get-tuple-element.43), channel_id=1, source_target_pairs={{0,24},{8,16},{16,8},{24,0},{1,25},{9,17},{17,9},{25,1},{2,26},{10... | collective-permute-start | bytes 884744 | tf_op jit(solution)/shard_map/ppermute | solution.py:379
  8.9 9.4 %collective-permute-start.1 = (f32[64,1024]{1,0:T(8,128)S(1)}, f32[64,1024]{1,0:T(8,128)S(1)}, u32[]{:S(2)}, u32[]{:S(2)}) collective-permute-start(f32[64,1024]{1,0:T(8,128)S(1)} %get-tuple-element.33), channel_id=1, source_target_pairs={{1,2},{2,1},{3,4},{4,3},{5,6},{6,5},{9,10},{10,9},{11,12},{12,11},... | collective-permute-start | bytes 786440 | tf_op jit(solution)/shard_map/ppermute | solution.py:388
  10.3 15.8 %collective-permute-start.5 = (f32[1,24,8,128]{3,2,1,0:T(8,128)S(1)}, f32[1,24,8,128]{3,2,1,0:T(8,128)S(1)}, u32[]{:S(2)}, u32[]{:S(2)}) collective-permute-start(f32[1,24,8,128]{3,2,1,0:T(8,128)S(1)} %get-tuple-element.44), channel_id=1, source_target_pairs={{0,24},{8,16},{16,8},{24,0},{1,25},{9,17},{17,9},{25,1},{2,26},{10... | collective-permute-start | bytes 294920 | tf_op jit(solution)/shard_map/ppermute | solution.py:379
  24.3 5.4 %copy-start.7 = (f32[40]{0:T(128)S(1)}, f32[40]{0:T(128)}, u32[]{:S(2)}) copy-start(f32[40]{0:T(128)} %stoich.5) | copy-start | bytes 484
  26.1 8.1 %collective-permute-start.9 = (f32[2,25,8,128]{3,2,1,0:T(8,128)S(1)}, f32[2,25,8,128]{3,2,1,0:T(8,128)S(1)}, u32[]{:S(2)}, u32[]{:S(2)}) collective-permute-start(f32[2,25,8,128]{3,2,1,0:T(8,128)S(1)} %get-tuple-element.53), channel_id=1, source_target_pairs={{0,8},{8,0},{16,24},{24,16},{1,9},{9,1},{17,25},{25,17},{2,10},{10... | collective-permute-start | bytes 614408 | tf_op jit(solution)/shard_map/ppermute | solution.py:379
  26.4 9.3 %collective-permute-start.10 = (f32[2,25,8,128]{3,2,1,0:T(8,128)S(1)}, f32[2,25,8,128]{3,2,1,0:T(8,128)S(1)}, u32[]{:S(2)}, u32[]{:S(2)}) collective-permute-start(f32[2,25,8,128]{3,2,1,0:T(8,128)S(1)} %get-tuple-element.54), channel_id=1, source_target_pairs={{0,16},{8,24},{16,0},{24,8},{1,17},{9,25},{17,1},{25,9},{2,18},{10... | collective-permute-start | bytes 614408 | tf_op jit(solution)/shard_map/ppermute | solution.py:379
  28.2 11.3 %collective-permute-start.11 = (f32[2,25,8,128]{3,2,1,0:T(8,128)S(1)}, f32[2,25,8,128]{3,2,1,0:T(8,128)S(1)}, u32[]{:S(2)}, u32[]{:S(2)}) collective-permute-start(f32[2,25,8,128]{3,2,1,0:T(8,128)S(1)} %get-tuple-element.55), channel_id=1, source_target_pairs={{0,24},{8,16},{16,8},{24,0},{1,25},{9,17},{17,9},{25,1},{2,26},{10... | collective-permute-start | bytes 614408 | tf_op jit(solution)/shard_map/ppermute | solution.py:379
  31.5 10.1 %collective-permute-start.8 = (f32[2,25,8,128]{3,2,1,0:T(8,128)S(1)}, f32[2,25,8,128]{3,2,1,0:T(8,128)S(1)}, u32[]{:S(2)}, u32[]{:S(2)}) collective-permute-start(f32[2,25,8,128]{3,2,1,0:T(8,128)S(1)} %get-tuple-element.48), channel_id=1, source_target_pairs={{0,8},{8,0},{16,24},{24,16},{1,9},{9,1},{17,25},{25,17},{2,10},{10... | collective-permute-start | bytes 614408 | tf_op jit(solution)/shard_map/ppermute | solution.py:379
  31.8 12.6 %collective-permute-start.6 = (f32[2,25,8,128]{3,2,1,0:T(8,128)S(1)}, f32[2,25,8,128]{3,2,1,0:T(8,128)S(1)}, u32[]{:S(2)}, u32[]{:S(2)}) collective-permute-start(f32[2,25,8,128]{3,2,1,0:T(8,128)S(1)} %get-tuple-element.45), channel_id=1, source_target_pairs={{0,16},{8,24},{16,0},{24,8},{1,17},{9,25},{17,1},{25,9},{2,18},{10... | collective-permute-start | bytes 614408 | tf_op jit(solution)/shard_map/ppermute | solution.py:379
  34.2 10.1 %collective-permute-start.7 = (f32[2,25,8,128]{3,2,1,0:T(8,128)S(1)}, f32[2,25,8,128]{3,2,1,0:T(8,128)S(1)}, u32[]{:S(2)}, u32[]{:S(2)}) collective-permute-start(f32[2,25,8,128]{3,2,1,0:T(8,128)S(1)} %get-tuple-element.46), channel_id=1, source_target_pairs={{0,24},{8,16},{16,8},{24,0},{1,25},{9,17},{17,9},{25,1},{2,26},{10... | collective-permute-start | bytes 614408 | tf_op jit(solution)/shard_map/ppermute | solution.py:379

commit v4 on v3

--- a/solution.py
+++ b/solution.py
@@ -96,7 +96,7 @@
     )(soot, species, after)
 
 
-def weight_kernel(kernel, split, target, growth, reaction, stack, rate, rate_before, spread_out, scratch):
+def weight_kernel(kernel, split, target, growth, reaction, lower, upper, rate, rate_before, spread_out, scratch):
     size = kernel.shape[0]
     row = lax.broadcasted_iota(jnp.int32, (size, size), 0)
     col = lax.broadcasted_iota(jnp.int32, (size, size), 1)
@@ -120,9 +120,18 @@
     last = SHIFTS * size
     scratch[last : last + SUB - 1, :] = fed(-1)[size - SUB + 1 :]
     w_high, w_low = halves(scratch[...])
-    stack[:, :size] = w_high
-    stack[:, size : 2 * size] = w_high
-    stack[:, 2 * size :] = w_low
+    most = size - 2 * SUB
+    for i in range(1, SHIFTS):
+        at = slice(most * (i - 1), most * i)
+        for j, part in enumerate((w_high, w_high, w_low)):
+            lower[at, most * j : most * (j + 1)] = part[i * size : i * size + most, :most]
+    rest = [slice(0, size)] + [slice(i * size + most, (i + 1) * size) for i in range(1, SHIFTS)] + [slice(last, last + 2 * SUB)]
+    at = 0
+    for rows in rest:
+        count = rows.stop - rows.start
+        for j, part in enumerate((w_high, w_high, w_low)):
+            upper[at : at + count, size * j : size * (j + 1)] = part[rows]
+        at += count
     diagonal = jnp.where(row == col, jnp.broadcast_to(growth[...], (size, size)), 0.0)
     column = jnp.sum(diagonal, axis=1, keepdims=True)
     rate[...] = jnp.broadcast_to(column, rate.shape)
@@ -150,20 +159,21 @@
     return pl.pallas_call(
         weight_kernel,
         out_shape=[
-            jax.ShapeDtypeStruct((depth, 3 * size), BF16),
+            jax.ShapeDtypeStruct(((SHIFTS - 1) * (size - 2 * SUB), 3 * (size - 2 * SUB)), BF16),
+            jax.ShapeDtypeStruct((size + 2 * SUB * SHIFTS, 3 * size), BF16),
             jax.ShapeDtypeStruct((size, GROUP * LANE), F32),
             jax.ShapeDtypeStruct((size, GROUP * LANE), F32),
             jax.ShapeDtypeStruct((kinds * SUB, 3 * kinds * SUB), BF16),
         ],
         in_specs=[VMEM] * 5,
-        out_specs=[VMEM] * 4,
+        out_specs=[VMEM] * 5,
         scratch_shapes=[pltpu.VMEM((depth, size), F32)],
         compiler_params=PARAMS,
         name="weights",
     )(kernel, split, target, growth.reshape(1, size), reaction)
 
 
-def rate_kernel(plan, sources, count, part, stack, rate, rate_before, soot, acet, after, *refs):
+def rate_kernel(plan, sources, count, part, lower, upper, rate, rate_before, soot, acet, after, *refs):
     n = plan.n
     pieces, outs = refs[:count], refs[count : count + n]
     whole, result, near, shifted = refs[count + n :]
@@ -172,7 +182,7 @@
     for b, block in enumerate(part):
         rows, cols = plan.place(lax.axis_index("sec"), block)
         near[b] = acet[0, rows, cols]
-    pad = SHIFTS - 1
+    pad, most = SHIFTS - 1, size - 2 * SUB
     for b in range(len(part)):
         whole[b, : pad * SUB, :] = jnp.zeros((pad * SUB, LANE), F32)
         whole[b, (pad + size) * SUB :, :] = jnp.zeros((SUB, LANE), F32)
@@ -203,16 +213,21 @@
             return jnp.concatenate([moved[i, pad + first : pad + first + count, :] for i in range(GROUP)], axis=1)
 
         high, low = halves(here)
-        product = jnp.dot(stack[...], jnp.concatenate([high, low, high], axis=0), preferred_element_type=F32)
+        product = jnp.dot(upper[...], jnp.concatenate([high, low, high], axis=0), preferred_element_type=F32)
+        high, low = high[:most], low[:most]
+        below = jnp.dot(lower[...], jnp.concatenate([high, low, high], axis=0), preferred_element_type=F32)
         total = here * product[:size]
         for shift in range(1, SHIFTS):
-            total += near_by(-shift, size) * product[shift * size : (shift + 1) * size]
-        last = SHIFTS * size
+            moved_here = near_by(-shift, size)
+            before = moved_here if shift == 1 else before
+            top = size + 2 * SUB * (shift - 1)
+            total += moved_here * jnp.concatenate([below[most * (shift - 1) : most * shift], product[top : top + 2 * SUB]], axis=0)
+        last = size + 2 * SUB * (SHIFTS - 1)
         extra = near_by(size - SUB + 1, SUB) * product[last : last + SUB]
         total = jnp.concatenate([total[: size - SUB], total[size - SUB :] + extra], axis=0)
         growing = jnp.concatenate([near[b, row : row + 1, :] for b, row in pair], axis=1)
         grown = rate[...] * here
-        total -= growing * (grown - rate_before[...] * near_by(-1, size))
+        total -= growing * (grown - rate_before[...] * before)
         used = growing * jnp.sum(grown, axis=0, keepdims=True)
         for i, (b, row) in enumerate(pair):
             lanes = slice(i * LANE, (i + 1) * LANE)
@@ -226,7 +241,7 @@
 
 
 def rates(plan, part, prepared, soot, acet, after, pieces, got):
-    size = prepared[1].shape[0]
+    size = prepared[2].shape[0]
     local = size // plan.n
     sources, used = {}, []
     for (k, blocks), x in zip(pieces, got):
@@ -238,17 +253,35 @@
     return pl.pallas_call(
         functools.partial(rate_kernel, plan, sources, len(used), part),
         out_shape=[shape] * plan.n,
-        in_specs=[VMEM] * 5 + [ANY] + [VMEM] * len(used),
+        in_specs=[VMEM] * 6 + [ANY] + [VMEM] * len(used),
         out_specs=[VMEM] * plan.n,
         scratch_shapes=[
             pltpu.VMEM((len(part), (SHIFTS + size) * SUB, LANE), F32),
-            pltpu.VMEM((len(part), size * SUB, LANE), F32),
+            pltpu.VMEM((len(part), (size + 1) * SUB, LANE), F32),
             pltpu.VMEM((len(part), SUB, LANE), F32),
             pltpu.VMEM((2, GROUP, SHIFTS + SUB + size, LANE), F32),
         ],
         compiler_params=PARAMS,
         name="rates",
     )(*prepared, soot, acet, after, *used)
+
+
+def near_kernel(given, after, out, sem):
+    copy = pltpu.make_async_copy(given, out, sem)
+    copy.start()
+    copy.wait()
+
+
+def near(soot, after):
+    return pl.pallas_call(
+        near_kernel,
+        out_shape=jax.ShapeDtypeStruct(soot.shape, F32),
+        in_specs=[HBM, ANY],
+        out_specs=VMEM,
+        scratch_shapes=[pltpu.SemaphoreType.DMA],
+        compiler_params=PARAMS,
+        name="near",
+    )(pltpu.with_memory_space_constraint(soot, pltpu.HBM), after)
 
 
 def gate(pieces, late):
@@ -335,18 +368,27 @@
     pieces = refs[: len(peers)]
     soot_out, species_out, soot_held, species_held, sems = refs[-5:]
     local, kinds = soot_out.shape[0], species_out.shape[0]
+    units = [(k, b) for k in range(len(peers)) for b in range(len(part))]
+    places = {(k, b): plan.place(peer(peers[k]), part[b]) for k, b in units}
     copies = []
-    for k, far in enumerate(peers):
-        for b, block in enumerate(part):
-            rows, cols = plan.place(peer(far), block)
-            soot_held[k, b] = soot_base[:, rows, cols] + pieces[k][b, :local]
-            copies.append(pltpu.make_async_copy(soot_held.at[k, b], soot_out.at[:, rows, cols], sems.at[0, k, b]))
-            copies[-1].start()
-            used = pieces[k][b, local]
-            for kind in range(kinds):
-                species_held[k, b, kind] = species_base[kind, rows, cols] - stoich[kind] * used
-            copies.append(pltpu.make_async_copy(species_held.at[k, b], species_out.at[:, rows, cols], sems.at[1, k, b]))
-            copies[-1].start()
+
+    def send(source, target, sem):
+        copies.append(pltpu.make_async_copy(source, target, sem))
+        copies[-1].start()
+
+    for k, b in units:
+        rows, cols = places[k, b]
+        soot_held[k, b] = soot_base[:, rows, cols] + pieces[k][b, :local]
+        send(soot_held.at[k, b], soot_out.at[:, rows, cols], sems.at[0, k, b])
+    used = {(k, b): pieces[k][b, local] for k, b in units}
+    for kind in range(kinds):
+        factor = stoich[kind]
+        for k, b in units:
+            rows, cols = places[k, b]
+            species_held[k, b, kind] = species_base[kind, rows, cols] - factor * used[k, b]
+    for k, b in units:
+        rows, cols = places[k, b]
+        send(species_held.at[k, b], species_out.at[:, rows, cols], sems.at[1, k, b])
     for copy in copies:
         copy.wait()
 
@@ -381,6 +423,7 @@
     order = [k for k in (2, 1, 3) if k < n] + list(range(4, n))
     pieces = [(k, part) for k in order for part in plan.parts((0.75,) if k == n - 1 else ())]
     sent = cut(plan, pieces, soot)
+    soot = near(soot, sent[0])
     got = [swap(x, k) for (k, _), x in zip(pieces, sent)]
 
     inner, outer = edges(soot, species, sent[0])

time: 46.1 us -> 46 us (level)
  local copies, waits for them, and re-layouts: 1.78 us -> 0.05 us
  Pallas kernels: 17.1 us -> 17.9 us
  starting transfers between devices: 14.9 us -> 15.4 us
    unnamed x20 -> x16, local copies, waits for them, and re-layouts: 1.78 us -> 0.05 us
    pallas_call x1 -> x2, Pallas kernels: 0.65 us -> 2.05 us  [the longest x1 1.42 us: near(): pl.pallas_call(near_kernel, out_shape=jax.ShapeDtypeStruct(soot.shape, F3...]
    ppermute x10, waiting for transfers between devices: 10.8 us -> 11.6 us  [swap(): return lax.ppermute(x, 'sec', [(i, i ^ k) for i in range(n)])]
    ppermute x10, starting transfers between devices: 14 us -> 14.7 us  [swap(): return lax.ppermute(x, 'sec', [(i, i ^ k) for i in range(n)])]
    ppermute x2, waiting for transfers between devices: 0.63 us -> 0.07 us  [shards(): lax.ppermute(x, 'xs', [q for i, j in p for q in ((i, j), (j, i))])]
    pallas_call x2, Pallas kernels: 3.65 us -> 3.1 us  [rates(): pl.pallas_call(functools.partial(rate_kernel, plan, sources, len(used), p...]
  transfers between devices with their start and end apart: 12 -> 12, of which waited for: 7 -> 6; matrix products, arithmetic and copies ran while one was open for 0% -> 0% of each run, Pallas kernels for 30% -> 32%
where the time goes in v4:
time: 46 us; the launch traced here: 45.8 us
  Pallas kernels  17.9 us (39%)
  starting transfers between devices  15.4 us (33%)
  waiting for transfers between devices  11.6 us (25%)
  between operations  0.84 us (2%)
    ppermute x10, starting transfers between devices, swap(): return lax.ppermute(x, 'sec', [(i, i ^ k) for i in range(n)])  14.7 us
    ppermute x10, waiting for transfers between devices, swap(): return lax.ppermute(x, 'sec', [(i, i ^ k) for i in range(n)])  11.6 us
    pallas_call x3, Pallas kernels, last(): pl.pallas_call(functools.partial(last_kernel, plan, part, peers), out_sha...  5.3 us
    pallas_call x1, Pallas kernels, bases(): pl.pallas_call(base_kernel, out_shape=[jax.ShapeDtypeStruct(soot.shape, F...  5.02 us
    pallas_call x2, Pallas kernels, rates(): pl.pallas_call(functools.partial(rate_kernel, plan, sources, len(used), p...  3.1 us
    pallas_call x1, Pallas kernels, cut(): pl.pallas_call(functools.partial(cut_kernel, plan, pieces), out_shape=sha...  1.48 us
    pallas_call x1, Pallas kernels, near(): pl.pallas_call(near_kernel, out_shape=jax.ShapeDtypeStruct(soot.shape, F3...  1.42 us
  transfers between devices with their start and end apart: 12, of which 6 were waited for; matrix products, arithmetic and copies ran while one was open for 0% of the time, Pallas kernels for 32%

profile of v4, /device:TPU:0, one launch (start us, length us, event | category | flops | bytes accessed | tf_op | source)
XLA Modules:
  0.0 45.8 jit_solution(17740680974420352290)
XLA Ops:
  0.6 1.5 %cut.1 = (f32[4,24,8,128]{3,2,1,0:T(8,128)S(1)}, f32[4,24,8,128]{3,2,1,0:T(8,128)S(1)}, f32[3,24,8,128]{3,2,1,0:T(8,128)S(1)}, f32[1,24,8,128]{3,2,1,0:T(8,128)S(1)}) custom-call(f32[24,16,1024]{2,1,0:T(8,128)} %given.1), custom_call_target="tpu_custom_call" | custom-call | tf_op jit(solution)/shard_map/cut/pallas_call | solution.py:66
  2.1 3.0 %collective-permute-start.3 = (f32[4,24,8,128]{3,2,1,0:T(8,128)S(1)}, f32[4,24,8,128]{3,2,1,0:T(8,128)S(1)}, u32[]{:S(2)}, u32[]{:S(2)}) collective-permute-start(f32[4,24,8,128]{3,2,1,0:T(8,128)S(1)} %get-tuple-element.44), channel_id=1, source_target_pairs={{0,8},{8,0},{16,24},{24,16},{1,9},{9,1},{17,25},{25,17},{2,10},{10... | collective-permute-start | bytes 1179656 | tf_op jit(solution)/shard_map/ppermute | solution.py:421
  5.1 1.5 %collective-permute-start.2 = (f32[4,24,8,128]{3,2,1,0:T(8,128)S(1)}, f32[4,24,8,128]{3,2,1,0:T(8,128)S(1)}, u32[]{:S(2)}, u32[]{:S(2)}) collective-permute-start(f32[4,24,8,128]{3,2,1,0:T(8,128)S(1)} %get-tuple-element.32.after), channel_id=1, source_target_pairs={{0,16},{8,24},{16,0},{24,8},{1,17},{9,25},{17,1},{25,9},{2,18},{10... | collective-permute-start | bytes 1179656 | tf_op jit(solution)/shard_map/ppermute | solution.py:421
  6.6 1.4 %near.1.soot = f32[24,16,1024]{2,1,0:T(8,128)S(1)} custom-call(f32[24,16,1024]{2,1,0:T(8,128)} %given.1, f32[4,24,8,128]{3,2,1,0:T(8,128)S(1)} %get-tuple-element.32.after), custom_call_target="tpu_custom_call" | custom-call | tf_op jit(solution)/shard_map/near/pallas_call | solution.py:276
  8.4 0.8 %collective-permute-start.4 = (f32[3,24,8,128]{3,2,1,0:T(8,128)S(1)}, f32[3,24,8,128]{3,2,1,0:T(8,128)S(1)}, u32[]{:S(2)}, u32[]{:S(2)}) collective-permute-start(f32[3,24,8,128]{3,2,1,0:T(8,128)S(1)} %get-tuple-element.45), channel_id=1, source_target_pairs={{0,24},{8,16},{16,8},{24,0},{1,25},{9,17},{17,9},{25,1},{2,26},{10... | collective-permute-start | bytes 884744 | tf_op jit(solution)/shard_map/ppermute | solution.py:421
  9.2 0.7 %collective-permute-start.1 = (f32[64,1024]{1,0:T(8,128)S(1)}, f32[64,1024]{1,0:T(8,128)S(1)}, u32[]{:S(2)}, u32[]{:S(2)}) collective-permute-start(f32[64,1024]{1,0:T(8,128)S(1)} %get-tuple-element.34), channel_id=1, source_target_pairs={{1,2},{2,1},{3,4},{4,3},{5,6},{6,5},{9,10},{10,9},{11,12},{12,11},... | collective-permute-start | bytes 786440 | tf_op jit(solution)/shard_map/ppermute | solution.py:431
  9.9 2.2 %collective-permute-start.5 = (f32[1,24,8,128]{3,2,1,0:T(8,128)S(1)}, f32[1,24,8,128]{3,2,1,0:T(8,128)S(1)}, u32[]{:S(2)}, u32[]{:S(2)}) collective-permute-start(f32[1,24,8,128]{3,2,1,0:T(8,128)S(1)} %get-tuple-element.46), channel_id=1, source_target_pairs={{0,24},{8,16},{16,8},{24,0},{1,25},{9,17},{17,9},{25,1},{2,26},{10... | collective-permute-start | bytes 294920 | tf_op jit(solution)/shard_map/ppermute | solution.py:421
  12.1 0.6 %weights.1 = (bf16[320,240]{1,0:T(8,128)(2,1)S(1)}, bf16[176,288]{1,0:T(8,128)(2,1)S(1)}, f32[96,256]{1,0:T(8,128)S(1)}, f32[96,256]{1,0:T(8,128)S(1)}, bf16[320,960]{1,0:T(8,128)(2,1)S(1)}) custom-call(f32[96,96]{1,0:T(8,128)S(1)} %copy-done.1, f32[96,96]{1,0:T(8,128)S(1)} %copy-done.2, s32[96,96]{1,0:T(8,128)S(1)} %copy-done.3, f32[1,96]{1,0:T(1,128)S(1)} %bitcast.1, ...), custom_call_target="tpu_custom_call" | custom-call | tf_op jit(solution)/shard_map/weights/pallas_call | solution.py:159
  12.8 5.0 %bases.1 = (f32[24,16,1024]{2,1,0:T(8,128)S(1)}, f32[40,16,1024]{2,1,0:T(8,128)S(1)}) custom-call(f32[40]{0:T(128)S(1)} %copy-done.6, bf16[320,960]{1,0:T(8,128)(2,1)S(1)} %get-tuple-element.35.kinetics, f32[24,16,1024]{2,1,0:T(8,128)S(1)} %near.1.soot, f32[40,16,1024]{2,1,0:T(8,128)S(1)} %copy-done), custom_call_target="tpu_custom_call" | custom-call | tf_op jit(solution)/shard_map/bases/pallas_call | solution.py:334
  17.8 0.8 %rim.1 = (f32[24,16,1024]{2,1,0:T(8,128)S(1)}, f32[40,16,1024]{2,1,0:T(8,128)S(1)}) custom-call(f32[64,1024]{1,0:T(8,128)S(1)} %collective-permute-done.inner, f32[64,1024]{1,0:T(8,128)S(1)} %collective-permute-done.1.outer, f32[40]{0:T(128)S(1)} %copy-done.6, ...), custom_call_target="tpu_custom_call", output_to_operand_aliasing={{0}: (3, {}), {1}: (4, {})} | custom-call | tf_op jit(solution)/shard_map/rim/pallas_call | solution.py:356
  18.6 4.3 %collective-permute-done.4.refs_2_ = f32[3,24,8,128]{3,2,1,0:T(8,128)S(1)} collective-permute-done((f32[3,24,8,128]{3,2,1,0:T(8,128)S(1)}, f32[3,24,8,128]{3,2,1,0:T(8,128)S(1)}, u32[]{:S(2)}, u32[]{:S(2)}) %collective-permute-start.4) | collective-permute-done | bytes 294944 | tf_op jit(solution)/shard_map/ppermute | solution.py:421
  22.9 1.2 %collective-permute-done.2.refs_0_ = f32[4,24,8,128]{3,2,1,0:T(8,128)S(1)} collective-permute-done((f32[4,24,8,128]{3,2,1,0:T(8,128)S(1)}, f32[4,24,8,128]{3,2,1,0:T(8,128)S(1)}, u32[]{:S(2)}, u32[]{:S(2)}) %collective-permute-start.2) | collective-permute-done | bytes 393248 | tf_op jit(solution)/shard_map/ppermute | solution.py:421
  24.1 1.5 %rates.3 = (f32[2,25,8,128]{3,2,1,0:T(8,128)S(1)}, f32[2,25,8,128]{3,2,1,0:T(8,128)S(1)}, f32[2,25,8,128]{3,2,1,0:T(8,128)S(1)}, f32[2,25,8,128]{3,2,1,0:T(8,128)S(1)}) custom-call(bf16[320,240]{1,0:T(8,128)(2,1)S(1)} %get-tuple-element.40.lower, bf16[176,288]{1,0:T(8,128)(2,1)S(1)} %get-tuple-element.41.upper, f32[96,256]{1,0:T(8,128)S(1)} %get-tuple-element.42.rate, ...), custom_call_target="tpu_custom_call" | custom-call | tf_op jit(solution)/shard_map/rates/pallas_call | solution.py:253
  26.0 1.9 %collective-permute-start.10 = (f32[2,25,8,128]{3,2,1,0:T(8,128)S(1)}, f32[2,25,8,128]{3,2,1,0:T(8,128)S(1)}, u32[]{:S(2)}, u32[]{:S(2)}) collective-permute-start(f32[2,25,8,128]{3,2,1,0:T(8,128)S(1)} %get-tuple-element.56), channel_id=1, source_target_pairs={{0,16},{8,24},{16,0},{24,8},{1,17},{9,25},{17,1},{25,9},{2,18},{10... | collective-permute-start | bytes 614408 | tf_op jit(solution)/shard_map/ppermute | solution.py:421
  27.8 1.4 %collective-permute-start.11 = (f32[2,25,8,128]{3,2,1,0:T(8,128)S(1)}, f32[2,25,8,128]{3,2,1,0:T(8,128)S(1)}, u32[]{:S(2)}, u32[]{:S(2)}) collective-permute-start(f32[2,25,8,128]{3,2,1,0:T(8,128)S(1)} %get-tuple-element.57), channel_id=1, source_target_pairs={{0,24},{8,16},{16,8},{24,0},{1,25},{9,17},{17,9},{25,1},{2,26},{10... | collective-permute-start | bytes 614408 | tf_op jit(solution)/shard_map/ppermute | solution.py:421
  29.3 1.5 %rates.2 = (f32[2,25,8,128]{3,2,1,0:T(8,128)S(1)}, f32[2,25,8,128]{3,2,1,0:T(8,128)S(1)}, f32[2,25,8,128]{3,2,1,0:T(8,128)S(1)}, f32[2,25,8,128]{3,2,1,0:T(8,128)S(1)}) custom-call(bf16[320,240]{1,0:T(8,128)(2,1)S(1)} %get-tuple-element.40.lower, bf16[176,288]{1,0:T(8,128)(2,1)S(1)} %get-tuple-element.41.upper, f32[96,256]{1,0:T(8,128)S(1)} %get-tuple-element.42.rate, ...), custom_call_target="tpu_custom_call" | custom-call | tf_op jit(solution)/shard_map/rates/pallas_call | solution.py:253
  31.1 1.9 %collective-permute-start.6 = (f32[2,25,8,128]{3,2,1,0:T(8,128)S(1)}, f32[2,25,8,128]{3,2,1,0:T(8,128)S(1)}, u32[]{:S(2)}, u32[]{:S(2)}) collective-permute-start(f32[2,25,8,128]{3,2,1,0:T(8,128)S(1)} %get-tuple-element.47), channel_id=1, source_target_pairs={{0,16},{8,24},{16,0},{24,8},{1,17},{9,25},{17,1},{25,9},{2,18},{10... | collective-permute-start | bytes 614408 | tf_op jit(solution)/shard_map/ppermute | solution.py:421
  32.9 0.8 %collective-permute-done.9.refs_1_ = f32[2,25,8,128]{3,2,1,0:T(8,128)S(1)} collective-permute-done((f32[2,25,8,128]{3,2,1,0:T(8,128)S(1)}, f32[2,25,8,128]{3,2,1,0:T(8,128)S(1)}, u32[]{:S(2)}, u32[]{:S(2)}) %collective-permute-start.9) | collective-permute-done | bytes 204832 | tf_op jit(solution)/shard_map/ppermute | solution.py:421
  33.8 1.5 %collective-permute-start.7 = (f32[2,25,8,128]{3,2,1,0:T(8,128)S(1)}, f32[2,25,8,128]{3,2,1,0:T(8,128)S(1)}, u32[]{:S(2)}, u32[]{:S(2)}) collective-permute-start(f32[2,25,8,128]{3,2,1,0:T(8,128)S(1)} %get-tuple-element.48), channel_id=1, source_target_pairs={{0,24},{8,16},{16,8},{24,0},{1,25},{9,17},{17,9},{25,1},{2,26},{10... | collective-permute-start | bytes 614408 | tf_op jit(solution)/shard_map/ppermute | solution.py:421
  35.3 3.8 %collective-permute-done.10.refs_2_ = f32[2,25,8,128]{3,2,1,0:T(8,128)S(1)} collective-permute-done((f32[2,25,8,128]{3,2,1,0:T(8,128)S(1)}, f32[2,25,8,128]{3,2,1,0:T(8,128)S(1)}, u32[]{:S(2)}, u32[]{:S(2)}) %collective-permute-start.10) | collective-permute-done | bytes 204832 | tf_op jit(solution)/shard_map/ppermute | solution.py:421
  39.1 2.1 %last.3 = (f32[24,16,1024]{2,1,0:T(8,128)}, f32[40,16,1024]{2,1,0:T(8,128)}) custom-call(f32[40]{0:T(128)S(1)} %copy-done.5, f32[24,16,1024]{2,1,0:T(8,128)S(1)} %get-tuple-element.38.after.soot_base, f32[40,16,1024]{2,1,0:T(8,128)S(1)} %get-tuple-element.39.species_base, f32[2,25,8,128]{3,2,1,0:T(8,128)S(1)} %get-tuple-element.51.refs_0_, ...), custom_call_target="tpu_custom_call" | custom-call | tf_op jit(solution)/shard_map/last/pallas_call | solution.py:399
  41.1 1.6 %last.4 = (f32[24,16,1024]{2,1,0:T(8,128)}, f32[40,16,1024]{2,1,0:T(8,128)}) custom-call(f32[40]{0:T(128)S(1)} %copy-done.5, f32[24,16,1024]{2,1,0:T(8,128)S(1)} %get-tuple-element.38.after.soot_base, f32[40,16,1024]{2,1,0:T(8,128)S(1)} %get-tuple-element.39.species_base, ...), custom_call_target="tpu_custom_call", output_to_operand_aliasing={{0}: (5, {}), {1}: (6, {})} | custom-call | tf_op jit(solution)/shard_map/last/pallas_call | solution.py:399
  42.8 1.4 %collective-permute-done.6.refs_0_ = f32[2,25,8,128]{3,2,1,0:T(8,128)S(1)} collective-permute-done((f32[2,25,8,128]{3,2,1,0:T(8,128)S(1)}, f32[2,25,8,128]{3,2,1,0:T(8,128)S(1)}, u32[]{:S(2)}, u32[]{:S(2)}) %collective-permute-start.6) | collective-permute-done | bytes 204832 | tf_op jit(solution)/shard_map/ppermute | solution.py:421
  44.2 1.6 %last.5 = (f32[24,16,1024]{2,1,0:T(8,128)}, f32[40,16,1024]{2,1,0:T(8,128)}) custom-call(f32[40]{0:T(128)S(1)} %copy-done.5, f32[24,16,1024]{2,1,0:T(8,128)S(1)} %get-tuple-element.38.after.soot_base, f32[40,16,1024]{2,1,0:T(8,128)S(1)} %get-tuple-element.39.species_base, ...), custom_call_target="tpu_custom_call", output_to_operand_aliasing={{0}: (5, {}), {1}: (6, {})} | custom-call | tf_op jit(solution)/shard_map/last/pallas_call | solution.py:399
  (28 shorter events, 0.9 us)
Async XLA Ops:
  2.1 20.8 %collective-permute-start.3 = (f32[4,24,8,128]{3,2,1,0:T(8,128)S(1)}, f32[4,24,8,128]{3,2,1,0:T(8,128)S(1)}, u32[]{:S(2)}, u32[]{:S(2)}) collective-permute-start(f32[4,24,8,128]{3,2,1,0:T(8,128)S(1)} %get-tuple-element.44), channel_id=1, source_target_pairs={{0,8},{8,0},{16,24},{24,16},{1,9},{9,1},{17,25},{25,17},{2,10},{10... | collective-permute-start | bytes 1179656 | tf_op jit(solution)/shard_map/ppermute | solution.py:421
  5.1 2.9 %copy-start = (f32[40,16,1024]{2,1,0:T(8,128)S(1)}, f32[40,16,1024]{2,1,0:T(8,128)}, u32[]{:S(2)}) copy-start(f32[40,16,1024]{2,1,0:T(8,128)} %acet.3) | copy-start | bytes 7864324
  5.1 19.0 %collective-permute-start.2 = (f32[4,24,8,128]{3,2,1,0:T(8,128)S(1)}, f32[4,24,8,128]{3,2,1,0:T(8,128)S(1)}, u32[]{:S(2)}, u32[]{:S(2)}) collective-permute-start(f32[4,24,8,128]{3,2,1,0:T(8,128)S(1)} %get-tuple-element.32.after), channel_id=1, source_target_pairs={{0,16},{8,24},{16,0},{24,8},{1,17},{9,25},{17,1},{25,9},{2,18},{10... | collective-permute-start | bytes 1179656 | tf_op jit(solution)/shard_map/ppermute | solution.py:421
  8.1 4.1 %copy-start.1 = (f32[96,96]{1,0:T(8,128)S(1)}, f32[96,96]{1,0:T(8,128)}, u32[]{:S(2)}) copy-start(f32[96,96]{1,0:T(8,128)} %kernel.1) | copy-start | bytes 110596
  8.1 4.0 %copy-start.2 = (f32[96,96]{1,0:T(8,128)S(1)}, f32[96,96]{1,0:T(8,128)}, u32[]{:S(2)}) copy-start(f32[96,96]{1,0:T(8,128)} %split.1) | copy-start | bytes 110596
  8.1 4.0 %copy-start.3 = (s32[96,96]{1,0:T(8,128)S(1)}, s32[96,96]{1,0:T(8,128)}, u32[]{:S(2)}) copy-start(s32[96,96]{1,0:T(8,128)} %target.1) | copy-start | bytes 110596
  8.1 4.0 %copy-start.4 = (f32[40,40]{1,0:T(8,128)S(1)}, f32[40,40]{1,0:T(8,128)}, u32[]{:S(2)}) copy-start(f32[40,40]{1,0:T(8,128)} %reaction.1) | copy-start | bytes 19204
  8.1 4.0 %copy-start.7 = (f32[96]{0:T(128)S(1)}, f32[96]{0:T(128)}, u32[]{:S(2)}) copy-start(f32[96]{0:T(128)} %param.14) | copy-start | bytes 1156
  8.1 4.7 %copy-start.6 = (f32[40]{0:T(128)S(1)}, f32[40]{0:T(128)}, u32[]{:S(2)}) copy-start(f32[40]{0:T(128)} %diffusivity.3) | copy-start | bytes 484
  8.3 1.6 %collective-permute-start = (f32[64,1024]{1,0:T(8,128)S(1)}, f32[64,1024]{1,0:T(8,128)S(1)}, u32[]{:S(2)}, u32[]{:S(2)}) collective-permute-start(f32[64,1024]{1,0:T(8,128)S(1)} %get-tuple-element.33), channel_id=1, source_target_pairs={{0,1},{1,0},{2,3},{3,2},{4,5},{5,4},{6,7},{7,6},{8,9},{9,8},{10,11... | collective-permute-start | bytes 786440 | tf_op jit(solution)/shard_map/ppermute | solution.py:431
  8.4 14.5 %collective-permute-start.4 = (f32[3,24,8,128]{3,2,1,0:T(8,128)S(1)}, f32[3,24,8,128]{3,2,1,0:T(8,128)S(1)}, u32[]{:S(2)}, u32[]{:S(2)}) collective-permute-start(f32[3,24,8,128]{3,2,1,0:T(8,128)S(1)} %get-tuple-element.45), channel_id=1, source_target_pairs={{0,24},{8,16},{16,8},{24,0},{1,25},{9,17},{17,9},{25,1},{2,26},{10... | collective-permute-start | bytes 884744 | tf_op jit(solution)/shard_map/ppermute | solution.py:421
  9.2 8.7 %collective-permute-start.1 = (f32[64,1024]{1,0:T(8,128)S(1)}, f32[64,1024]{1,0:T(8,128)S(1)}, u32[]{:S(2)}, u32[]{:S(2)}) collective-permute-start(f32[64,1024]{1,0:T(8,128)S(1)} %get-tuple-element.34), channel_id=1, source_target_pairs={{1,2},{2,1},{3,4},{4,3},{5,6},{6,5},{9,10},{10,9},{11,12},{12,11},... | collective-permute-start | bytes 786440 | tf_op jit(solution)/shard_map/ppermute | solution.py:431
  9.9 15.8 %collective-permute-start.5 = (f32[1,24,8,128]{3,2,1,0:T(8,128)S(1)}, f32[1,24,8,128]{3,2,1,0:T(8,128)S(1)}, u32[]{:S(2)}, u32[]{:S(2)}) collective-permute-start(f32[1,24,8,128]{3,2,1,0:T(8,128)S(1)} %get-tuple-element.46), channel_id=1, source_target_pairs={{0,24},{8,16},{16,8},{24,0},{1,25},{9,17},{17,9},{25,1},{2,26},{10... | collective-permute-start | bytes 294920 | tf_op jit(solution)/shard_map/ppermute | solution.py:421
  24.1 5.1 %copy-start.5 = (f32[40]{0:T(128)S(1)}, f32[40]{0:T(128)}, u32[]{:S(2)}) copy-start(f32[40]{0:T(128)} %stoich.5) | copy-start | bytes 484
  25.7 8.1 %collective-permute-start.9 = (f32[2,25,8,128]{3,2,1,0:T(8,128)S(1)}, f32[2,25,8,128]{3,2,1,0:T(8,128)S(1)}, u32[]{:S(2)}, u32[]{:S(2)}) collective-permute-start(f32[2,25,8,128]{3,2,1,0:T(8,128)S(1)} %get-tuple-element.55), channel_id=1, source_target_pairs={{0,8},{8,0},{16,24},{24,16},{1,9},{9,1},{17,25},{25,17},{2,10},{10... | collective-permute-start | bytes 614408 | tf_op jit(solution)/shard_map/ppermute | solution.py:421
  26.0 13.1 %collective-permute-start.10 = (f32[2,25,8,128]{3,2,1,0:T(8,128)S(1)}, f32[2,25,8,128]{3,2,1,0:T(8,128)S(1)}, u32[]{:S(2)}, u32[]{:S(2)}) collective-permute-start(f32[2,25,8,128]{3,2,1,0:T(8,128)S(1)} %get-tuple-element.56), channel_id=1, source_target_pairs={{0,16},{8,24},{16,0},{24,8},{1,17},{9,25},{17,1},{25,9},{2,18},{10... | collective-permute-start | bytes 614408 | tf_op jit(solution)/shard_map/ppermute | solution.py:421
  27.8 11.2 %collective-permute-start.11 = (f32[2,25,8,128]{3,2,1,0:T(8,128)S(1)}, f32[2,25,8,128]{3,2,1,0:T(8,128)S(1)}, u32[]{:S(2)}, u32[]{:S(2)}) collective-permute-start(f32[2,25,8,128]{3,2,1,0:T(8,128)S(1)} %get-tuple-element.57), channel_id=1, source_target_pairs={{0,24},{8,16},{16,8},{24,0},{1,25},{9,17},{17,9},{25,1},{2,26},{10... | collective-permute-start | bytes 614408 | tf_op jit(solution)/shard_map/ppermute | solution.py:421
  30.8 10.3 %collective-permute-start.8 = (f32[2,25,8,128]{3,2,1,0:T(8,128)S(1)}, f32[2,25,8,128]{3,2,1,0:T(8,128)S(1)}, u32[]{:S(2)}, u32[]{:S(2)}) collective-permute-start(f32[2,25,8,128]{3,2,1,0:T(8,128)S(1)} %get-tuple-element.50), channel_id=1, source_target_pairs={{0,8},{8,0},{16,24},{24,16},{1,9},{9,1},{17,25},{25,17},{2,10},{10... | collective-permute-start | bytes 614408 | tf_op jit(solution)/shard_map/ppermute | solution.py:421
  31.1 13.1 %collective-permute-start.6 = (f32[2,25,8,128]{3,2,1,0:T(8,128)S(1)}, f32[2,25,8,128]{3,2,1,0:T(8,128)S(1)}, u32[]{:S(2)}, u32[]{:S(2)}) collective-permute-start(f32[2,25,8,128]{3,2,1,0:T(8,128)S(1)} %get-tuple-element.47), channel_id=1, source_target_pairs={{0,16},{8,24},{16,0},{24,8},{1,17},{9,25},{17,1},{25,9},{2,18},{10... | collective-permute-start | bytes 614408 | tf_op jit(solution)/shard_map/ppermute | solution.py:421
  33.8 10.4 %collective-permute-start.7 = (f32[2,25,8,128]{3,2,1,0:T(8,128)S(1)}, f32[2,25,8,128]{3,2,1,0:T(8,128)S(1)}, u32[]{:S(2)}, u32[]{:S(2)}) collective-permute-start(f32[2,25,8,128]{3,2,1,0:T(8,128)S(1)} %get-tuple-element.48), channel_id=1, source_target_pairs={{0,24},{8,16},{16,8},{24,0},{1,25},{9,17},{17,9},{25,1},{2,26},{10... | collective-permute-start | bytes 614408 | tf_op jit(solution)/shard_map/ppermute | solution.py:421

commit v5 on v4

--- a/solution.py
+++ b/solution.py
@@ -314,7 +314,7 @@
         soot_base[i] = spread(soot[i], 0.1)
         return carry
 
-    lax.fori_loop(0, local, one_section, 0, unroll=8)
+    lax.fori_loop(0, local, one_section, 0, unroll=True)
 
     for row in range(0, rows, SUB):
         for col in range(0, width, 2 * LANE):
@@ -327,7 +327,7 @@
         species_base[i] += spread(species[i], diffusivity[i])
         return carry
 
-    lax.fori_loop(0, kinds, one_species, 0, unroll=8)
+    lax.fori_loop(0, kinds, one_species, 0, unroll=True)
 
 
 def bases(diffusivity, kinetics, soot, species):
@@ -437,7 +437,7 @@
     for part in plan.parts((0.5,)):
         outs = rates(plan, part, prepared, soot, species, base[0] if not back else stoich, pieces, got)
         late = [x for (_, blocks), x in zip(pieces, got) if not set(blocks) & set(part)]
-        away = gate(outs[1:], late) if late else outs[1:]
+        away = [*outs[1 : n - 1], *gate(outs[n - 1 :], late)] if late else outs[1:]
         back.append((part, [outs[0]] + [swap(x, k) for k, x in enumerate(away, 1)]))
     result = ()
     for i, (part, moved) in enumerate(back):

time: 46 us -> 45.7 us (level)
  Pallas kernels: 17.9 us -> 16.5 us
  waiting for transfers between devices: 11.6 us -> 12.7 us
    pallas_call x1, Pallas kernels: 5.02 us -> 3.65 us  [bases(): pl.pallas_call(base_kernel, out_shape=[jax.ShapeDtypeStruct(soot.shape, F...]
    ppermute x10, waiting for transfers between devices: 11.6 us -> 12.7 us  [swap(): return lax.ppermute(x, 'sec', [(i, i ^ k) for i in range(n)])]
  transfers between devices with their start and end apart: 12 -> 12, of which waited for: 6 -> 7; matrix products, arithmetic and copies ran while one was open for 0% -> 0% of each run, Pallas kernels for 32% -> 29%
where the time goes in v5:
time: 45.7 us; the launch traced here: 45.5 us
  Pallas kernels  16.5 us (36%)
  starting transfers between devices  15.4 us (34%)
  waiting for transfers between devices  12.7 us (28%)
  between operations  0.85 us (2%)
    ppermute x10, starting transfers between devices, swap(): return lax.ppermute(x, 'sec', [(i, i ^ k) for i in range(n)])  14.7 us
    ppermute x10, waiting for transfers between devices, swap(): return lax.ppermute(x, 'sec', [(i, i ^ k) for i in range(n)])  12.7 us
    pallas_call x3, Pallas kernels, last(): pl.pallas_call(functools.partial(last_kernel, plan, part, peers), out_sha...  5.29 us
    pallas_call x1, Pallas kernels, bases(): pl.pallas_call(base_kernel, out_shape=[jax.ShapeDtypeStruct(soot.shape, F...  3.65 us
    pallas_call x2, Pallas kernels, rates(): pl.pallas_call(functools.partial(rate_kernel, plan, sources, len(used), p...  3.1 us
    pallas_call x1, Pallas kernels, cut(): pl.pallas_call(functools.partial(cut_kernel, plan, pieces), out_shape=sha...  1.48 us
    pallas_call x1, Pallas kernels, near(): pl.pallas_call(near_kernel, out_shape=jax.ShapeDtypeStruct(soot.shape, F3...  1.42 us
  transfers between devices with their start and end apart: 12, of which 7 were waited for; matrix products, arithmetic and copies ran while one was open for 0% of the time, Pallas kernels for 29%

profile of v5, /device:TPU:0, one launch (start us, length us, event | category | flops | bytes accessed | tf_op | source)
XLA Modules:
  0.0 45.5 jit_solution(11039941874498307471)
XLA Ops:
  0.6 1.5 %cut.1 = (f32[4,24,8,128]{3,2,1,0:T(8,128)S(1)}, f32[4,24,8,128]{3,2,1,0:T(8,128)S(1)}, f32[3,24,8,128]{3,2,1,0:T(8,128)S(1)}, f32[1,24,8,128]{3,2,1,0:T(8,128)S(1)}) custom-call(f32[24,16,1024]{2,1,0:T(8,128)} %given.1), custom_call_target="tpu_custom_call" | custom-call | tf_op jit(solution)/shard_map/cut/pallas_call | solution.py:66
  2.1 3.0 %collective-permute-start.3 = (f32[4,24,8,128]{3,2,1,0:T(8,128)S(1)}, f32[4,24,8,128]{3,2,1,0:T(8,128)S(1)}, u32[]{:S(2)}, u32[]{:S(2)}) collective-permute-start(f32[4,24,8,128]{3,2,1,0:T(8,128)S(1)} %get-tuple-element.41), channel_id=1, source_target_pairs={{0,8},{8,0},{16,24},{24,16},{1,9},{9,1},{17,25},{25,17},{2,10},{10... | collective-permute-start | bytes 1179656 | tf_op jit(solution)/shard_map/ppermute | solution.py:421
  5.1 1.5 %collective-permute-start.2 = (f32[4,24,8,128]{3,2,1,0:T(8,128)S(1)}, f32[4,24,8,128]{3,2,1,0:T(8,128)S(1)}, u32[]{:S(2)}, u32[]{:S(2)}) collective-permute-start(f32[4,24,8,128]{3,2,1,0:T(8,128)S(1)} %get-tuple-element.29.after), channel_id=1, source_target_pairs={{0,16},{8,24},{16,0},{24,8},{1,17},{9,25},{17,1},{25,9},{2,18},{10... | collective-permute-start | bytes 1179656 | tf_op jit(solution)/shard_map/ppermute | solution.py:421
  6.6 1.4 %near.1.soot = f32[24,16,1024]{2,1,0:T(8,128)S(1)} custom-call(f32[24,16,1024]{2,1,0:T(8,128)} %given.1, f32[4,24,8,128]{3,2,1,0:T(8,128)S(1)} %get-tuple-element.29.after), custom_call_target="tpu_custom_call" | custom-call | tf_op jit(solution)/shard_map/near/pallas_call | solution.py:276
  8.4 0.8 %collective-permute-start.4 = (f32[3,24,8,128]{3,2,1,0:T(8,128)S(1)}, f32[3,24,8,128]{3,2,1,0:T(8,128)S(1)}, u32[]{:S(2)}, u32[]{:S(2)}) collective-permute-start(f32[3,24,8,128]{3,2,1,0:T(8,128)S(1)} %get-tuple-element.42), channel_id=1, source_target_pairs={{0,24},{8,16},{16,8},{24,0},{1,25},{9,17},{17,9},{25,1},{2,26},{10... | collective-permute-start | bytes 884744 | tf_op jit(solution)/shard_map/ppermute | solution.py:421
  9.2 0.7 %collective-permute-start.1 = (f32[64,1024]{1,0:T(8,128)S(1)}, f32[64,1024]{1,0:T(8,128)S(1)}, u32[]{:S(2)}, u32[]{:S(2)}) collective-permute-start(f32[64,1024]{1,0:T(8,128)S(1)} %get-tuple-element.31), channel_id=1, source_target_pairs={{1,2},{2,1},{3,4},{4,3},{5,6},{6,5},{9,10},{10,9},{11,12},{12,11},... | collective-permute-start | bytes 786440 | tf_op jit(solution)/shard_map/ppermute | solution.py:431
  9.9 2.2 %collective-permute-start.5 = (f32[1,24,8,128]{3,2,1,0:T(8,128)S(1)}, f32[1,24,8,128]{3,2,1,0:T(8,128)S(1)}, u32[]{:S(2)}, u32[]{:S(2)}) collective-permute-start(f32[1,24,8,128]{3,2,1,0:T(8,128)S(1)} %get-tuple-element.43), channel_id=1, source_target_pairs={{0,24},{8,16},{16,8},{24,0},{1,25},{9,17},{17,9},{25,1},{2,26},{10... | collective-permute-start | bytes 294920 | tf_op jit(solution)/shard_map/ppermute | solution.py:421
  12.1 0.6 %weights.1 = (bf16[320,240]{1,0:T(8,128)(2,1)S(1)}, bf16[176,288]{1,0:T(8,128)(2,1)S(1)}, f32[96,256]{1,0:T(8,128)S(1)}, f32[96,256]{1,0:T(8,128)S(1)}, bf16[320,960]{1,0:T(8,128)(2,1)S(1)}) custom-call(f32[96,96]{1,0:T(8,128)S(1)} %copy-done.1, f32[96,96]{1,0:T(8,128)S(1)} %copy-done.2, s32[96,96]{1,0:T(8,128)S(1)} %copy-done.3, f32[1,96]{1,0:T(1,128)S(1)} %bitcast.1, ...), custom_call_target="tpu_custom_call" | custom-call | tf_op jit(solution)/shard_map/weights/pallas_call | solution.py:159
  12.8 3.7 %bases.1 = (f32[24,16,1024]{2,1,0:T(8,128)S(1)}, f32[40,16,1024]{2,1,0:T(8,128)S(1)}) custom-call(f32[40]{0:T(128)S(1)} %copy-done.6, bf16[320,960]{1,0:T(8,128)(2,1)S(1)} %get-tuple-element.32.kinetics, f32[24,16,1024]{2,1,0:T(8,128)S(1)} %near.1.soot, f32[40,16,1024]{2,1,0:T(8,128)S(1)} %copy-done), custom_call_target="tpu_custom_call" | custom-call | tf_op jit(solution)/shard_map/bases/pallas_call | solution.py:334
  16.5 0.8 %rim.1 = (f32[24,16,1024]{2,1,0:T(8,128)S(1)}, f32[40,16,1024]{2,1,0:T(8,128)S(1)}) custom-call(f32[64,1024]{1,0:T(8,128)S(1)} %collective-permute-done.inner, f32[64,1024]{1,0:T(8,128)S(1)} %collective-permute-done.1.outer, f32[40]{0:T(128)S(1)} %copy-done.6, ...), custom_call_target="tpu_custom_call", output_to_operand_aliasing={{0}: (3, {}), {1}: (4, {})} | custom-call | tf_op jit(solution)/shard_map/rim/pallas_call | solution.py:356
  17.2 5.7 %collective-permute-done.4.refs_2_ = f32[3,24,8,128]{3,2,1,0:T(8,128)S(1)} collective-permute-done((f32[3,24,8,128]{3,2,1,0:T(8,128)S(1)}, f32[3,24,8,128]{3,2,1,0:T(8,128)S(1)}, u32[]{:S(2)}, u32[]{:S(2)}) %collective-permute-start.4) | collective-permute-done | bytes 294944 | tf_op jit(solution)/shard_map/ppermute | solution.py:421
  22.9 1.2 %collective-permute-done.2.refs_0_ = f32[4,24,8,128]{3,2,1,0:T(8,128)S(1)} collective-permute-done((f32[4,24,8,128]{3,2,1,0:T(8,128)S(1)}, f32[4,24,8,128]{3,2,1,0:T(8,128)S(1)}, u32[]{:S(2)}, u32[]{:S(2)}) %collective-permute-start.2) | collective-permute-done | bytes 393248 | tf_op jit(solution)/shard_map/ppermute | solution.py:421
  24.1 1.5 %rates.3 = (f32[2,25,8,128]{3,2,1,0:T(8,128)S(1)}, f32[2,25,8,128]{3,2,1,0:T(8,128)S(1)}, f32[2,25,8,128]{3,2,1,0:T(8,128)S(1)}, f32[2,25,8,128]{3,2,1,0:T(8,128)S(1)}) custom-call(bf16[320,240]{1,0:T(8,128)(2,1)S(1)} %get-tuple-element.37.lower, bf16[176,288]{1,0:T(8,128)(2,1)S(1)} %get-tuple-element.38.upper, f32[96,256]{1,0:T(8,128)S(1)} %get-tuple-element.39.rate, ...), custom_call_target="tpu_custom_call" | custom-call | tf_op jit(solution)/shard_map/rates/pallas_call | solution.py:253
  25.7 1.6 %collective-permute-start.11 = (f32[2,25,8,128]{3,2,1,0:T(8,128)S(1)}, f32[2,25,8,128]{3,2,1,0:T(8,128)S(1)}, u32[]{:S(2)}, u32[]{:S(2)}) collective-permute-start(f32[2,25,8,128]{3,2,1,0:T(8,128)S(1)} %gate.1), channel_id=1, source_target_pairs={{0,24},{8,16},{16,8},{24,0},{1,25},{9,17},{17,9},{25,1},{2,26},{10... | collective-permute-start | bytes 614408 | tf_op jit(solution)/shard_map/ppermute | solution.py:421
  27.3 1.5 %collective-permute-start.9 = (f32[2,25,8,128]{3,2,1,0:T(8,128)S(1)}, f32[2,25,8,128]{3,2,1,0:T(8,128)S(1)}, u32[]{:S(2)}, u32[]{:S(2)}) collective-permute-start(f32[2,25,8,128]{3,2,1,0:T(8,128)S(1)} %get-tuple-element.49), channel_id=1, source_target_pairs={{0,8},{8,0},{16,24},{24,16},{1,9},{9,1},{17,25},{25,17},{2,10},{10... | collective-permute-start | bytes 614408 | tf_op jit(solution)/shard_map/ppermute | solution.py:421
  29.3 1.5 %rates.2 = (f32[2,25,8,128]{3,2,1,0:T(8,128)S(1)}, f32[2,25,8,128]{3,2,1,0:T(8,128)S(1)}, f32[2,25,8,128]{3,2,1,0:T(8,128)S(1)}, f32[2,25,8,128]{3,2,1,0:T(8,128)S(1)}) custom-call(bf16[320,240]{1,0:T(8,128)(2,1)S(1)} %get-tuple-element.37.lower, bf16[176,288]{1,0:T(8,128)(2,1)S(1)} %get-tuple-element.38.upper, f32[96,256]{1,0:T(8,128)S(1)} %get-tuple-element.39.rate, ...), custom_call_target="tpu_custom_call" | custom-call | tf_op jit(solution)/shard_map/rates/pallas_call | solution.py:253
  31.1 1.9 %collective-permute-start.6 = (f32[2,25,8,128]{3,2,1,0:T(8,128)S(1)}, f32[2,25,8,128]{3,2,1,0:T(8,128)S(1)}, u32[]{:S(2)}, u32[]{:S(2)}) collective-permute-start(f32[2,25,8,128]{3,2,1,0:T(8,128)S(1)} %get-tuple-element.44), channel_id=1, source_target_pairs={{0,16},{8,24},{16,0},{24,8},{1,17},{9,25},{17,1},{25,9},{2,18},{10... | collective-permute-start | bytes 614408 | tf_op jit(solution)/shard_map/ppermute | solution.py:421
  32.9 1.7 %collective-permute-done.11.refs_3_ = f32[2,25,8,128]{3,2,1,0:T(8,128)S(1)} collective-permute-done((f32[2,25,8,128]{3,2,1,0:T(8,128)S(1)}, f32[2,25,8,128]{3,2,1,0:T(8,128)S(1)}, u32[]{:S(2)}, u32[]{:S(2)}) %collective-permute-start.11) | collective-permute-done | bytes 204832 | tf_op jit(solution)/shard_map/ppermute | solution.py:421
  34.7 1.5 %collective-permute-start.7 = (f32[2,25,8,128]{3,2,1,0:T(8,128)S(1)}, f32[2,25,8,128]{3,2,1,0:T(8,128)S(1)}, u32[]{:S(2)}, u32[]{:S(2)}) collective-permute-start(f32[2,25,8,128]{3,2,1,0:T(8,128)S(1)} %get-tuple-element.45), channel_id=1, source_target_pairs={{0,24},{8,16},{16,8},{24,0},{1,25},{9,17},{17,9},{25,1},{2,26},{10... | collective-permute-start | bytes 614408 | tf_op jit(solution)/shard_map/ppermute | solution.py:421
  36.2 2.5 %collective-permute-done.9.refs_1_ = f32[2,25,8,128]{3,2,1,0:T(8,128)S(1)} collective-permute-done((f32[2,25,8,128]{3,2,1,0:T(8,128)S(1)}, f32[2,25,8,128]{3,2,1,0:T(8,128)S(1)}, u32[]{:S(2)}, u32[]{:S(2)}) %collective-permute-start.9) | collective-permute-done | bytes 204832 | tf_op jit(solution)/shard_map/ppermute | solution.py:421
  39.0 2.1 %last.3 = (f32[24,16,1024]{2,1,0:T(8,128)}, f32[40,16,1024]{2,1,0:T(8,128)}) custom-call(f32[40]{0:T(128)S(1)} %copy-done.5, f32[24,16,1024]{2,1,0:T(8,128)S(1)} %get-tuple-element.35.after.soot_base, f32[40,16,1024]{2,1,0:T(8,128)S(1)} %get-tuple-element.36.species_base, f32[2,25,8,128]{3,2,1,0:T(8,128)S(1)} %get-tuple-element.48.refs_0_, ...), custom_call_target="tpu_custom_call" | custom-call | tf_op jit(solution)/shard_map/last/pallas_call | solution.py:399
  41.1 1.6 %last.4 = (f32[24,16,1024]{2,1,0:T(8,128)}, f32[40,16,1024]{2,1,0:T(8,128)}) custom-call(f32[40]{0:T(128)S(1)} %copy-done.5, f32[24,16,1024]{2,1,0:T(8,128)S(1)} %get-tuple-element.35.after.soot_base, f32[40,16,1024]{2,1,0:T(8,128)S(1)} %get-tuple-element.36.species_base, ...), custom_call_target="tpu_custom_call", output_to_operand_aliasing={{0}: (5, {}), {1}: (6, {})} | custom-call | tf_op jit(solution)/shard_map/last/pallas_call | solution.py:399
  42.8 1.2 %collective-permute-done.7.refs_1_ = f32[2,25,8,128]{3,2,1,0:T(8,128)S(1)} collective-permute-done((f32[2,25,8,128]{3,2,1,0:T(8,128)S(1)}, f32[2,25,8,128]{3,2,1,0:T(8,128)S(1)}, u32[]{:S(2)}, u32[]{:S(2)}) %collective-permute-start.7) | collective-permute-done | bytes 204832 | tf_op jit(solution)/shard_map/ppermute | solution.py:421
  43.9 1.6 %last.5 = (f32[24,16,1024]{2,1,0:T(8,128)}, f32[40,16,1024]{2,1,0:T(8,128)}) custom-call(f32[40]{0:T(128)S(1)} %copy-done.5, f32[24,16,1024]{2,1,0:T(8,128)S(1)} %get-tuple-element.35.after.soot_base, f32[40,16,1024]{2,1,0:T(8,128)S(1)} %get-tuple-element.36.species_base, ...), custom_call_target="tpu_custom_call", output_to_operand_aliasing={{0}: (5, {}), {1}: (6, {})} | custom-call | tf_op jit(solution)/shard_map/last/pallas_call | solution.py:399
  (28 shorter events, 1.5 us)
Async XLA Ops:
  2.1 20.8 %collective-permute-start.3 = (f32[4,24,8,128]{3,2,1,0:T(8,128)S(1)}, f32[4,24,8,128]{3,2,1,0:T(8,128)S(1)}, u32[]{:S(2)}, u32[]{:S(2)}) collective-permute-start(f32[4,24,8,128]{3,2,1,0:T(8,128)S(1)} %get-tuple-element.41), channel_id=1, source_target_pairs={{0,8},{8,0},{16,24},{24,16},{1,9},{9,1},{17,25},{25,17},{2,10},{10... | collective-permute-start | bytes 1179656 | tf_op jit(solution)/shard_map/ppermute | solution.py:421
  5.1 2.9 %copy-start = (f32[40,16,1024]{2,1,0:T(8,128)S(1)}, f32[40,16,1024]{2,1,0:T(8,128)}, u32[]{:S(2)}) copy-start(f32[40,16,1024]{2,1,0:T(8,128)} %acet.3) | copy-start | bytes 7864324
  5.1 19.0 %collective-permute-start.2 = (f32[4,24,8,128]{3,2,1,0:T(8,128)S(1)}, f32[4,24,8,128]{3,2,1,0:T(8,128)S(1)}, u32[]{:S(2)}, u32[]{:S(2)}) collective-permute-start(f32[4,24,8,128]{3,2,1,0:T(8,128)S(1)} %get-tuple-element.29.after), channel_id=1, source_target_pairs={{0,16},{8,24},{16,0},{24,8},{1,17},{9,25},{17,1},{25,9},{2,18},{10... | collective-permute-start | bytes 1179656 | tf_op jit(solution)/shard_map/ppermute | solution.py:421
  8.1 4.1 %copy-start.1 = (f32[96,96]{1,0:T(8,128)S(1)}, f32[96,96]{1,0:T(8,128)}, u32[]{:S(2)}) copy-start(f32[96,96]{1,0:T(8,128)} %kernel.1) | copy-start | bytes 110596
  8.1 4.0 %copy-start.2 = (f32[96,96]{1,0:T(8,128)S(1)}, f32[96,96]{1,0:T(8,128)}, u32[]{:S(2)}) copy-start(f32[96,96]{1,0:T(8,128)} %split.1) | copy-start | bytes 110596
  8.1 4.0 %copy-start.3 = (s32[96,96]{1,0:T(8,128)S(1)}, s32[96,96]{1,0:T(8,128)}, u32[]{:S(2)}) copy-start(s32[96,96]{1,0:T(8,128)} %target.1) | copy-start | bytes 110596
  8.1 4.0 %copy-start.4 = (f32[40,40]{1,0:T(8,128)S(1)}, f32[40,40]{1,0:T(8,128)}, u32[]{:S(2)}) copy-start(f32[40,40]{1,0:T(8,128)} %reaction.1) | copy-start | bytes 19204
  8.1 4.0 %copy-start.7 = (f32[96]{0:T(128)S(1)}, f32[96]{0:T(128)}, u32[]{:S(2)}) copy-start(f32[96]{0:T(128)} %param.14) | copy-start | bytes 1156
  8.1 4.7 %copy-start.6 = (f32[40]{0:T(128)S(1)}, f32[40]{0:T(128)}, u32[]{:S(2)}) copy-start(f32[40]{0:T(128)} %diffusivity.3) | copy-start | bytes 484
  8.3 1.6 %collective-permute-start = (f32[64,1024]{1,0:T(8,128)S(1)}, f32[64,1024]{1,0:T(8,128)S(1)}, u32[]{:S(2)}, u32[]{:S(2)}) collective-permute-start(f32[64,1024]{1,0:T(8,128)S(1)} %get-tuple-element.30), channel_id=1, source_target_pairs={{0,1},{1,0},{2,3},{3,2},{4,5},{5,4},{6,7},{7,6},{8,9},{9,8},{10,11... | collective-permute-start | bytes 786440 | tf_op jit(solution)/shard_map/ppermute | solution.py:431
  8.4 14.5 %collective-permute-start.4 = (f32[3,24,8,128]{3,2,1,0:T(8,128)S(1)}, f32[3,24,8,128]{3,2,1,0:T(8,128)S(1)}, u32[]{:S(2)}, u32[]{:S(2)}) collective-permute-start(f32[3,24,8,128]{3,2,1,0:T(8,128)S(1)} %get-tuple-element.42), channel_id=1, source_target_pairs={{0,24},{8,16},{16,8},{24,0},{1,25},{9,17},{17,9},{25,1},{2,26},{10... | collective-permute-start | bytes 884744 | tf_op jit(solution)/shard_map/ppermute | solution.py:421
  9.2 7.3 %collective-permute-start.1 = (f32[64,1024]{1,0:T(8,128)S(1)}, f32[64,1024]{1,0:T(8,128)S(1)}, u32[]{:S(2)}, u32[]{:S(2)}) collective-permute-start(f32[64,1024]{1,0:T(8,128)S(1)} %get-tuple-element.31), channel_id=1, source_target_pairs={{1,2},{2,1},{3,4},{4,3},{5,6},{6,5},{9,10},{10,9},{11,12},{12,11},... | collective-permute-start | bytes 786440 | tf_op jit(solution)/shard_map/ppermute | solution.py:431
  9.9 15.8 %collective-permute-start.5 = (f32[1,24,8,128]{3,2,1,0:T(8,128)S(1)}, f32[1,24,8,128]{3,2,1,0:T(8,128)S(1)}, u32[]{:S(2)}, u32[]{:S(2)}) collective-permute-start(f32[1,24,8,128]{3,2,1,0:T(8,128)S(1)} %get-tuple-element.43), channel_id=1, source_target_pairs={{0,24},{8,16},{16,8},{24,0},{1,25},{9,17},{17,9},{25,1},{2,26},{10... | collective-permute-start | bytes 294920 | tf_op jit(solution)/shard_map/ppermute | solution.py:421
  24.1 5.1 %copy-start.5 = (f32[40]{0:T(128)S(1)}, f32[40]{0:T(128)}, u32[]{:S(2)}) copy-start(f32[40]{0:T(128)} %stoich.5) | copy-start | bytes 484
  25.7 9.0 %collective-permute-start.11 = (f32[2,25,8,128]{3,2,1,0:T(8,128)S(1)}, f32[2,25,8,128]{3,2,1,0:T(8,128)S(1)}, u32[]{:S(2)}, u32[]{:S(2)}) collective-permute-start(f32[2,25,8,128]{3,2,1,0:T(8,128)S(1)} %gate.1), channel_id=1, source_target_pairs={{0,24},{8,16},{16,8},{24,0},{1,25},{9,17},{17,9},{25,1},{2,26},{10... | collective-permute-start | bytes 614408 | tf_op jit(solution)/shard_map/ppermute | solution.py:421
  27.3 11.4 %collective-permute-start.9 = (f32[2,25,8,128]{3,2,1,0:T(8,128)S(1)}, f32[2,25,8,128]{3,2,1,0:T(8,128)S(1)}, u32[]{:S(2)}, u32[]{:S(2)}) collective-permute-start(f32[2,25,8,128]{3,2,1,0:T(8,128)S(1)} %get-tuple-element.49), channel_id=1, source_target_pairs={{0,8},{8,0},{16,24},{24,16},{1,9},{9,1},{17,25},{25,17},{2,10},{10... | collective-permute-start | bytes 614408 | tf_op jit(solution)/shard_map/ppermute | solution.py:421
  28.7 10.3 %collective-permute-start.10 = (f32[2,25,8,128]{3,2,1,0:T(8,128)S(1)}, f32[2,25,8,128]{3,2,1,0:T(8,128)S(1)}, u32[]{:S(2)}, u32[]{:S(2)}) collective-permute-start(f32[2,25,8,128]{3,2,1,0:T(8,128)S(1)} %get-tuple-element.50), channel_id=1, source_target_pairs={{0,16},{8,24},{16,0},{24,8},{1,17},{9,25},{17,1},{25,9},{2,18},{10... | collective-permute-start | bytes 614408 | tf_op jit(solution)/shard_map/ppermute | solution.py:421
  30.8 10.3 %collective-permute-start.8 = (f32[2,25,8,128]{3,2,1,0:T(8,128)S(1)}, f32[2,25,8,128]{3,2,1,0:T(8,128)S(1)}, u32[]{:S(2)}, u32[]{:S(2)}) collective-permute-start(f32[2,25,8,128]{3,2,1,0:T(8,128)S(1)} %get-tuple-element.47), channel_id=1, source_target_pairs={{0,8},{8,0},{16,24},{24,16},{1,9},{9,1},{17,25},{25,17},{2,10},{10... | collective-permute-start | bytes 614408 | tf_op jit(solution)/shard_map/ppermute | solution.py:421
  31.1 11.7 %collective-permute-start.6 = (f32[2,25,8,128]{3,2,1,0:T(8,128)S(1)}, f32[2,25,8,128]{3,2,1,0:T(8,128)S(1)}, u32[]{:S(2)}, u32[]{:S(2)}) collective-permute-start(f32[2,25,8,128]{3,2,1,0:T(8,128)S(1)} %get-tuple-element.44), channel_id=1, source_target_pairs={{0,16},{8,24},{16,0},{24,8},{1,17},{9,25},{17,1},{25,9},{2,18},{10... | collective-permute-start | bytes 614408 | tf_op jit(solution)/shard_map/ppermute | solution.py:421
  34.7 9.3 %collective-permute-start.7 = (f32[2,25,8,128]{3,2,1,0:T(8,128)S(1)}, f32[2,25,8,128]{3,2,1,0:T(8,128)S(1)}, u32[]{:S(2)}, u32[]{:S(2)}) collective-permute-start(f32[2,25,8,128]{3,2,1,0:T(8,128)S(1)} %get-tuple-element.45), channel_id=1, source_target_pairs={{0,24},{8,16},{16,8},{24,0},{1,25},{9,17},{17,9},{25,1},{2,26},{10... | collective-permute-start | bytes 614408 | tf_op jit(solution)/shard_map/ppermute | solution.py:421

commit v6 on v5

--- a/solution.py
+++ b/solution.py
@@ -442,7 +442,8 @@
     result = ()
     for i, (part, moved) in enumerate(back):
         early = 2 if i == len(back) - 1 else n
-        for peers in (range(early), range(early, n)):
+        groups = (range(early), range(early, n)) if early == n or n < 4 else ([0, 2], [1, *range(3, n)])
+        for peers in groups:
             if peers:
                 result = last(plan, part, peers, stoich, *base, [moved[k] for k in peers], result)
     return tuple(result)

time: 45.7 us -> 45.7 us (level)
  transfers between devices with their start and end apart: 12 -> 12, of which waited for: 7 -> 8; matrix products, arithmetic and copies ran while one was open for 0% -> 0% of each run, Pallas kernels for 29% -> 29%
where the time goes in v6:
time: 45.7 us; the launch traced here: 45.6 us
  Pallas kernels  16.5 us (36%)
  starting transfers between devices  15.4 us (34%)
  waiting for transfers between devices  12.8 us (28%)
  between operations  0.84 us (2%)
    ppermute x10, starting transfers between devices, swap(): return lax.ppermute(x, 'sec', [(i, i ^ k) for i in range(n)])  14.7 us
    ppermute x10, waiting for transfers between devices, swap(): return lax.ppermute(x, 'sec', [(i, i ^ k) for i in range(n)])  12.7 us
    pallas_call x3, Pallas kernels, last(): pl.pallas_call(functools.partial(last_kernel, plan, part, peers), out_sha...  5.29 us
    pallas_call x1, Pallas kernels, bases(): pl.pallas_call(base_kernel, out_shape=[jax.ShapeDtypeStruct(soot.shape, F...  3.65 us
    pallas_call x2, Pallas kernels, rates(): pl.pallas_call(functools.partial(rate_kernel, plan, sources, len(used), p...  3.1 us
    pallas_call x1, Pallas kernels, cut(): pl.pallas_call(functools.partial(cut_kernel, plan, pieces), out_shape=sha...  1.48 us
    pallas_call x1, Pallas kernels, near(): pl.pallas_call(near_kernel, out_shape=jax.ShapeDtypeStruct(soot.shape, F3...  1.42 us
  transfers between devices with their start and end apart: 12, of which 8 were waited for; matrix products, arithmetic and copies ran while one was open for 0% of the time, Pallas kernels for 29%

profile of v6, /device:TPU:0, one launch (start us, length us, event | category | flops | bytes accessed | tf_op | source)
XLA Modules:
  0.0 45.6 jit_solution(6117618111140004892)
XLA Ops:
  0.6 1.5 %cut.1 = (f32[4,24,8,128]{3,2,1,0:T(8,128)S(1)}, f32[4,24,8,128]{3,2,1,0:T(8,128)S(1)}, f32[3,24,8,128]{3,2,1,0:T(8,128)S(1)}, f32[1,24,8,128]{3,2,1,0:T(8,128)S(1)}) custom-call(f32[24,16,1024]{2,1,0:T(8,128)} %given.1), custom_call_target="tpu_custom_call" | custom-call | tf_op jit(solution)/shard_map/cut/pallas_call | solution.py:66
  2.1 3.0 %collective-permute-start.3 = (f32[4,24,8,128]{3,2,1,0:T(8,128)S(1)}, f32[4,24,8,128]{3,2,1,0:T(8,128)S(1)}, u32[]{:S(2)}, u32[]{:S(2)}) collective-permute-start(f32[4,24,8,128]{3,2,1,0:T(8,128)S(1)} %get-tuple-element.41), channel_id=1, source_target_pairs={{0,8},{8,0},{16,24},{24,16},{1,9},{9,1},{17,25},{25,17},{2,10},{10... | collective-permute-start | bytes 1179656 | tf_op jit(solution)/shard_map/ppermute | solution.py:421
  5.1 1.5 %collective-permute-start.2 = (f32[4,24,8,128]{3,2,1,0:T(8,128)S(1)}, f32[4,24,8,128]{3,2,1,0:T(8,128)S(1)}, u32[]{:S(2)}, u32[]{:S(2)}) collective-permute-start(f32[4,24,8,128]{3,2,1,0:T(8,128)S(1)} %get-tuple-element.29.after), channel_id=1, source_target_pairs={{0,16},{8,24},{16,0},{24,8},{1,17},{9,25},{17,1},{25,9},{2,18},{10... | collective-permute-start | bytes 1179656 | tf_op jit(solution)/shard_map/ppermute | solution.py:421
  6.6 1.4 %near.1.soot = f32[24,16,1024]{2,1,0:T(8,128)S(1)} custom-call(f32[24,16,1024]{2,1,0:T(8,128)} %given.1, f32[4,24,8,128]{3,2,1,0:T(8,128)S(1)} %get-tuple-element.29.after), custom_call_target="tpu_custom_call" | custom-call | tf_op jit(solution)/shard_map/near/pallas_call | solution.py:276
  8.4 0.8 %collective-permute-start.4 = (f32[3,24,8,128]{3,2,1,0:T(8,128)S(1)}, f32[3,24,8,128]{3,2,1,0:T(8,128)S(1)}, u32[]{:S(2)}, u32[]{:S(2)}) collective-permute-start(f32[3,24,8,128]{3,2,1,0:T(8,128)S(1)} %get-tuple-element.42), channel_id=1, source_target_pairs={{0,24},{8,16},{16,8},{24,0},{1,25},{9,17},{17,9},{25,1},{2,26},{10... | collective-permute-start | bytes 884744 | tf_op jit(solution)/shard_map/ppermute | solution.py:421
  9.2 0.7 %collective-permute-start.1 = (f32[64,1024]{1,0:T(8,128)S(1)}, f32[64,1024]{1,0:T(8,128)S(1)}, u32[]{:S(2)}, u32[]{:S(2)}) collective-permute-start(f32[64,1024]{1,0:T(8,128)S(1)} %get-tuple-element.31), channel_id=1, source_target_pairs={{1,2},{2,1},{3,4},{4,3},{5,6},{6,5},{9,10},{10,9},{11,12},{12,11},... | collective-permute-start | bytes 786440 | tf_op jit(solution)/shard_map/ppermute | solution.py:431
  9.9 2.2 %collective-permute-start.5 = (f32[1,24,8,128]{3,2,1,0:T(8,128)S(1)}, f32[1,24,8,128]{3,2,1,0:T(8,128)S(1)}, u32[]{:S(2)}, u32[]{:S(2)}) collective-permute-start(f32[1,24,8,128]{3,2,1,0:T(8,128)S(1)} %get-tuple-element.43), channel_id=1, source_target_pairs={{0,24},{8,16},{16,8},{24,0},{1,25},{9,17},{17,9},{25,1},{2,26},{10... | collective-permute-start | bytes 294920 | tf_op jit(solution)/shard_map/ppermute | solution.py:421
  12.1 0.6 %weights.1 = (bf16[320,240]{1,0:T(8,128)(2,1)S(1)}, bf16[176,288]{1,0:T(8,128)(2,1)S(1)}, f32[96,256]{1,0:T(8,128)S(1)}, f32[96,256]{1,0:T(8,128)S(1)}, bf16[320,960]{1,0:T(8,128)(2,1)S(1)}) custom-call(f32[96,96]{1,0:T(8,128)S(1)} %copy-done.1, f32[96,96]{1,0:T(8,128)S(1)} %copy-done.2, s32[96,96]{1,0:T(8,128)S(1)} %copy-done.3, f32[1,96]{1,0:T(1,128)S(1)} %bitcast.1, ...), custom_call_target="tpu_custom_call" | custom-call | tf_op jit(solution)/shard_map/weights/pallas_call | solution.py:159
  12.8 3.7 %bases.1 = (f32[24,16,1024]{2,1,0:T(8,128)S(1)}, f32[40,16,1024]{2,1,0:T(8,128)S(1)}) custom-call(f32[40]{0:T(128)S(1)} %copy-done.6, bf16[320,960]{1,0:T(8,128)(2,1)S(1)} %get-tuple-element.32.kinetics, f32[24,16,1024]{2,1,0:T(8,128)S(1)} %near.1.soot, f32[40,16,1024]{2,1,0:T(8,128)S(1)} %copy-done), custom_call_target="tpu_custom_call" | custom-call | tf_op jit(solution)/shard_map/bases/pallas_call | solution.py:334
  16.5 0.8 %rim.1 = (f32[24,16,1024]{2,1,0:T(8,128)S(1)}, f32[40,16,1024]{2,1,0:T(8,128)S(1)}) custom-call(f32[64,1024]{1,0:T(8,128)S(1)} %collective-permute-done.inner, f32[64,1024]{1,0:T(8,128)S(1)} %collective-permute-done.1.outer, f32[40]{0:T(128)S(1)} %copy-done.6, ...), custom_call_target="tpu_custom_call", output_to_operand_aliasing={{0}: (3, {}), {1}: (4, {})} | custom-call | tf_op jit(solution)/shard_map/rim/pallas_call | solution.py:356
  17.2 5.7 %collective-permute-done.4.refs_2_ = f32[3,24,8,128]{3,2,1,0:T(8,128)S(1)} collective-permute-done((f32[3,24,8,128]{3,2,1,0:T(8,128)S(1)}, f32[3,24,8,128]{3,2,1,0:T(8,128)S(1)}, u32[]{:S(2)}, u32[]{:S(2)}) %collective-permute-start.4) | collective-permute-done | bytes 294944 | tf_op jit(solution)/shard_map/ppermute | solution.py:421
  22.9 1.2 %collective-permute-done.2.refs_0_ = f32[4,24,8,128]{3,2,1,0:T(8,128)S(1)} collective-permute-done((f32[4,24,8,128]{3,2,1,0:T(8,128)S(1)}, f32[4,24,8,128]{3,2,1,0:T(8,128)S(1)}, u32[]{:S(2)}, u32[]{:S(2)}) %collective-permute-start.2) | collective-permute-done | bytes 393248 | tf_op jit(solution)/shard_map/ppermute | solution.py:421
  24.1 1.5 %rates.3 = (f32[2,25,8,128]{3,2,1,0:T(8,128)S(1)}, f32[2,25,8,128]{3,2,1,0:T(8,128)S(1)}, f32[2,25,8,128]{3,2,1,0:T(8,128)S(1)}, f32[2,25,8,128]{3,2,1,0:T(8,128)S(1)}) custom-call(bf16[320,240]{1,0:T(8,128)(2,1)S(1)} %get-tuple-element.37.lower, bf16[176,288]{1,0:T(8,128)(2,1)S(1)} %get-tuple-element.38.upper, f32[96,256]{1,0:T(8,128)S(1)} %get-tuple-element.39.rate, ...), custom_call_target="tpu_custom_call" | custom-call | tf_op jit(solution)/shard_map/rates/pallas_call | solution.py:253
  25.7 1.6 %collective-permute-start.11 = (f32[2,25,8,128]{3,2,1,0:T(8,128)S(1)}, f32[2,25,8,128]{3,2,1,0:T(8,128)S(1)}, u32[]{:S(2)}, u32[]{:S(2)}) collective-permute-start(f32[2,25,8,128]{3,2,1,0:T(8,128)S(1)} %gate.1), channel_id=1, source_target_pairs={{0,24},{8,16},{16,8},{24,0},{1,25},{9,17},{17,9},{25,1},{2,26},{10... | collective-permute-start | bytes 614408 | tf_op jit(solution)/shard_map/ppermute | solution.py:421
  27.3 1.5 %collective-permute-start.9 = (f32[2,25,8,128]{3,2,1,0:T(8,128)S(1)}, f32[2,25,8,128]{3,2,1,0:T(8,128)S(1)}, u32[]{:S(2)}, u32[]{:S(2)}) collective-permute-start(f32[2,25,8,128]{3,2,1,0:T(8,128)S(1)} %get-tuple-element.49), channel_id=1, source_target_pairs={{0,8},{8,0},{16,24},{24,16},{1,9},{9,1},{17,25},{25,17},{2,10},{10... | collective-permute-start | bytes 614408 | tf_op jit(solution)/shard_map/ppermute | solution.py:421
  29.3 1.5 %rates.2 = (f32[2,25,8,128]{3,2,1,0:T(8,128)S(1)}, f32[2,25,8,128]{3,2,1,0:T(8,128)S(1)}, f32[2,25,8,128]{3,2,1,0:T(8,128)S(1)}, f32[2,25,8,128]{3,2,1,0:T(8,128)S(1)}) custom-call(bf16[320,240]{1,0:T(8,128)(2,1)S(1)} %get-tuple-element.37.lower, bf16[176,288]{1,0:T(8,128)(2,1)S(1)} %get-tuple-element.38.upper, f32[96,256]{1,0:T(8,128)S(1)} %get-tuple-element.39.rate, ...), custom_call_target="tpu_custom_call" | custom-call | tf_op jit(solution)/shard_map/rates/pallas_call | solution.py:253
  30.8 1.6 %collective-permute-start.8 = (f32[2,25,8,128]{3,2,1,0:T(8,128)S(1)}, f32[2,25,8,128]{3,2,1,0:T(8,128)S(1)}, u32[]{:S(2)}, u32[]{:S(2)}) collective-permute-start(f32[2,25,8,128]{3,2,1,0:T(8,128)S(1)} %get-tuple-element.47), channel_id=1, source_target_pairs={{0,16},{8,24},{16,0},{24,8},{1,17},{9,25},{17,1},{25,9},{2,18},{10... | collective-permute-start | bytes 614408 | tf_op jit(solution)/shard_map/ppermute | solution.py:421
  32.9 1.7 %collective-permute-done.11.refs_3_ = f32[2,25,8,128]{3,2,1,0:T(8,128)S(1)} collective-permute-done((f32[2,25,8,128]{3,2,1,0:T(8,128)S(1)}, f32[2,25,8,128]{3,2,1,0:T(8,128)S(1)}, u32[]{:S(2)}, u32[]{:S(2)}) %collective-permute-start.11) | collective-permute-done | bytes 204832 | tf_op jit(solution)/shard_map/ppermute | solution.py:421
  34.7 1.5 %collective-permute-start.7 = (f32[2,25,8,128]{3,2,1,0:T(8,128)S(1)}, f32[2,25,8,128]{3,2,1,0:T(8,128)S(1)}, u32[]{:S(2)}, u32[]{:S(2)}) collective-permute-start(f32[2,25,8,128]{3,2,1,0:T(8,128)S(1)} %get-tuple-element.45), channel_id=1, source_target_pairs={{0,24},{8,16},{16,8},{24,0},{1,25},{9,17},{17,9},{25,1},{2,26},{10... | collective-permute-start | bytes 614408 | tf_op jit(solution)/shard_map/ppermute | solution.py:421
  36.2 2.6 %collective-permute-done.9.refs_1_ = f32[2,25,8,128]{3,2,1,0:T(8,128)S(1)} collective-permute-done((f32[2,25,8,128]{3,2,1,0:T(8,128)S(1)}, f32[2,25,8,128]{3,2,1,0:T(8,128)S(1)}, u32[]{:S(2)}, u32[]{:S(2)}) %collective-permute-start.9) | collective-permute-done | bytes 204832 | tf_op jit(solution)/shard_map/ppermute | solution.py:421
  39.0 2.1 %last.3 = (f32[24,16,1024]{2,1,0:T(8,128)}, f32[40,16,1024]{2,1,0:T(8,128)}) custom-call(f32[40]{0:T(128)S(1)} %copy-done.5, f32[24,16,1024]{2,1,0:T(8,128)S(1)} %get-tuple-element.35.after.soot_base, f32[40,16,1024]{2,1,0:T(8,128)S(1)} %get-tuple-element.36.species_base, f32[2,25,8,128]{3,2,1,0:T(8,128)S(1)} %get-tuple-element.48.refs_0_, ...), custom_call_target="tpu_custom_call" | custom-call | tf_op jit(solution)/shard_map/last/pallas_call | solution.py:399
  41.1 0.6 %collective-permute-done.8.refs_1_ = f32[2,25,8,128]{3,2,1,0:T(8,128)S(1)} collective-permute-done((f32[2,25,8,128]{3,2,1,0:T(8,128)S(1)}, f32[2,25,8,128]{3,2,1,0:T(8,128)S(1)}, u32[]{:S(2)}, u32[]{:S(2)}) %collective-permute-start.8) | collective-permute-done | bytes 204832 | tf_op jit(solution)/shard_map/ppermute | solution.py:421
  41.7 1.6 %last.4 = (f32[24,16,1024]{2,1,0:T(8,128)}, f32[40,16,1024]{2,1,0:T(8,128)}) custom-call(f32[40]{0:T(128)S(1)} %copy-done.5, f32[24,16,1024]{2,1,0:T(8,128)S(1)} %get-tuple-element.35.after.soot_base, f32[40,16,1024]{2,1,0:T(8,128)S(1)} %get-tuple-element.36.species_base, ...), custom_call_target="tpu_custom_call", output_to_operand_aliasing={{0}: (5, {}), {1}: (6, {})} | custom-call | tf_op jit(solution)/shard_map/last/pallas_call | solution.py:399
  43.9 1.6 %last.5 = (f32[24,16,1024]{2,1,0:T(8,128)}, f32[40,16,1024]{2,1,0:T(8,128)}) custom-call(f32[40]{0:T(128)S(1)} %copy-done.5, f32[24,16,1024]{2,1,0:T(8,128)S(1)} %get-tuple-element.35.after.soot_base, f32[40,16,1024]{2,1,0:T(8,128)S(1)} %get-tuple-element.36.species_base, ...), custom_call_target="tpu_custom_call", output_to_operand_aliasing={{0}: (5, {}), {1}: (6, {})} | custom-call | tf_op jit(solution)/shard_map/last/pallas_call | solution.py:399
  (28 shorter events, 2.2 us)
Async XLA Ops:
  2.1 20.8 %collective-permute-start.3 = (f32[4,24,8,128]{3,2,1,0:T(8,128)S(1)}, f32[4,24,8,128]{3,2,1,0:T(8,128)S(1)}, u32[]{:S(2)}, u32[]{:S(2)}) collective-permute-start(f32[4,24,8,128]{3,2,1,0:T(8,128)S(1)} %get-tuple-element.41), channel_id=1, source_target_pairs={{0,8},{8,0},{16,24},{24,16},{1,9},{9,1},{17,25},{25,17},{2,10},{10... | collective-permute-start | bytes 1179656 | tf_op jit(solution)/shard_map/ppermute | solution.py:421
  5.1 2.9 %copy-start = (f32[40,16,1024]{2,1,0:T(8,128)S(1)}, f32[40,16,1024]{2,1,0:T(8,128)}, u32[]{:S(2)}) copy-start(f32[40,16,1024]{2,1,0:T(8,128)} %acet.3) | copy-start | bytes 7864324
  5.1 19.0 %collective-permute-start.2 = (f32[4,24,8,128]{3,2,1,0:T(8,128)S(1)}, f32[4,24,8,128]{3,2,1,0:T(8,128)S(1)}, u32[]{:S(2)}, u32[]{:S(2)}) collective-permute-start(f32[4,24,8,128]{3,2,1,0:T(8,128)S(1)} %get-tuple-element.29.after), channel_id=1, source_target_pairs={{0,16},{8,24},{16,0},{24,8},{1,17},{9,25},{17,1},{25,9},{2,18},{10... | collective-permute-start | bytes 1179656 | tf_op jit(solution)/shard_map/ppermute | solution.py:421
  8.1 4.1 %copy-start.1 = (f32[96,96]{1,0:T(8,128)S(1)}, f32[96,96]{1,0:T(8,128)}, u32[]{:S(2)}) copy-start(f32[96,96]{1,0:T(8,128)} %kernel.1) | copy-start | bytes 110596
  8.1 4.0 %copy-start.2 = (f32[96,96]{1,0:T(8,128)S(1)}, f32[96,96]{1,0:T(8,128)}, u32[]{:S(2)}) copy-start(f32[96,96]{1,0:T(8,128)} %split.1) | copy-start | bytes 110596
  8.1 4.0 %copy-start.3 = (s32[96,96]{1,0:T(8,128)S(1)}, s32[96,96]{1,0:T(8,128)}, u32[]{:S(2)}) copy-start(s32[96,96]{1,0:T(8,128)} %target.1) | copy-start | bytes 110596
  8.1 4.0 %copy-start.4 = (f32[40,40]{1,0:T(8,128)S(1)}, f32[40,40]{1,0:T(8,128)}, u32[]{:S(2)}) copy-start(f32[40,40]{1,0:T(8,128)} %reaction.1) | copy-start | bytes 19204
  8.1 4.0 %copy-start.7 = (f32[96]{0:T(128)S(1)}, f32[96]{0:T(128)}, u32[]{:S(2)}) copy-start(f32[96]{0:T(128)} %param.14) | copy-start | bytes 1156
  8.1 4.7 %copy-start.6 = (f32[40]{0:T(128)S(1)}, f32[40]{0:T(128)}, u32[]{:S(2)}) copy-start(f32[40]{0:T(128)} %diffusivity.3) | copy-start | bytes 484
  8.3 1.6 %collective-permute-start = (f32[64,1024]{1,0:T(8,128)S(1)}, f32[64,1024]{1,0:T(8,128)S(1)}, u32[]{:S(2)}, u32[]{:S(2)}) collective-permute-start(f32[64,1024]{1,0:T(8,128)S(1)} %get-tuple-element.30), channel_id=1, source_target_pairs={{0,1},{1,0},{2,3},{3,2},{4,5},{5,4},{6,7},{7,6},{8,9},{9,8},{10,11... | collective-permute-start | bytes 786440 | tf_op jit(solution)/shard_map/ppermute | solution.py:431
  8.4 14.5 %collective-permute-start.4 = (f32[3,24,8,128]{3,2,1,0:T(8,128)S(1)}, f32[3,24,8,128]{3,2,1,0:T(8,128)S(1)}, u32[]{:S(2)}, u32[]{:S(2)}) collective-permute-start(f32[3,24,8,128]{3,2,1,0:T(8,128)S(1)} %get-tuple-element.42), channel_id=1, source_target_pairs={{0,24},{8,16},{16,8},{24,0},{1,25},{9,17},{17,9},{25,1},{2,26},{10... | collective-permute-start | bytes 884744 | tf_op jit(solution)/shard_map/ppermute | solution.py:421
  9.2 7.3 %collective-permute-start.1 = (f32[64,1024]{1,0:T(8,128)S(1)}, f32[64,1024]{1,0:T(8,128)S(1)}, u32[]{:S(2)}, u32[]{:S(2)}) collective-permute-start(f32[64,1024]{1,0:T(8,128)S(1)} %get-tuple-element.31), channel_id=1, source_target_pairs={{1,2},{2,1},{3,4},{4,3},{5,6},{6,5},{9,10},{10,9},{11,12},{12,11},... | collective-permute-start | bytes 786440 | tf_op jit(solution)/shard_map/ppermute | solution.py:431
  9.9 15.8 %collective-permute-start.5 = (f32[1,24,8,128]{3,2,1,0:T(8,128)S(1)}, f32[1,24,8,128]{3,2,1,0:T(8,128)S(1)}, u32[]{:S(2)}, u32[]{:S(2)}) collective-permute-start(f32[1,24,8,128]{3,2,1,0:T(8,128)S(1)} %get-tuple-element.43), channel_id=1, source_target_pairs={{0,24},{8,16},{16,8},{24,0},{1,25},{9,17},{17,9},{25,1},{2,26},{10... | collective-permute-start | bytes 294920 | tf_op jit(solution)/shard_map/ppermute | solution.py:421
  24.1 5.1 %copy-start.5 = (f32[40]{0:T(128)S(1)}, f32[40]{0:T(128)}, u32[]{:S(2)}) copy-start(f32[40]{0:T(128)} %stoich.5) | copy-start | bytes 484
  25.7 9.0 %collective-permute-start.11 = (f32[2,25,8,128]{3,2,1,0:T(8,128)S(1)}, f32[2,25,8,128]{3,2,1,0:T(8,128)S(1)}, u32[]{:S(2)}, u32[]{:S(2)}) collective-permute-start(f32[2,25,8,128]{3,2,1,0:T(8,128)S(1)} %gate.1), channel_id=1, source_target_pairs={{0,24},{8,16},{16,8},{24,0},{1,25},{9,17},{17,9},{25,1},{2,26},{10... | collective-permute-start | bytes 614408 | tf_op jit(solution)/shard_map/ppermute | solution.py:421
  27.3 11.6 %collective-permute-start.9 = (f32[2,25,8,128]{3,2,1,0:T(8,128)S(1)}, f32[2,25,8,128]{3,2,1,0:T(8,128)S(1)}, u32[]{:S(2)}, u32[]{:S(2)}) collective-permute-start(f32[2,25,8,128]{3,2,1,0:T(8,128)S(1)} %get-tuple-element.49), channel_id=1, source_target_pairs={{0,8},{8,0},{16,24},{24,16},{1,9},{9,1},{17,25},{25,17},{2,10},{10... | collective-permute-start | bytes 614408 | tf_op jit(solution)/shard_map/ppermute | solution.py:421
  28.7 10.3 %collective-permute-start.10 = (f32[2,25,8,128]{3,2,1,0:T(8,128)S(1)}, f32[2,25,8,128]{3,2,1,0:T(8,128)S(1)}, u32[]{:S(2)}, u32[]{:S(2)}) collective-permute-start(f32[2,25,8,128]{3,2,1,0:T(8,128)S(1)} %get-tuple-element.50), channel_id=1, source_target_pairs={{0,16},{8,24},{16,0},{24,8},{1,17},{9,25},{17,1},{25,9},{2,18},{10... | collective-permute-start | bytes 614408 | tf_op jit(solution)/shard_map/ppermute | solution.py:421
  30.8 10.9 %collective-permute-start.8 = (f32[2,25,8,128]{3,2,1,0:T(8,128)S(1)}, f32[2,25,8,128]{3,2,1,0:T(8,128)S(1)}, u32[]{:S(2)}, u32[]{:S(2)}) collective-permute-start(f32[2,25,8,128]{3,2,1,0:T(8,128)S(1)} %get-tuple-element.47), channel_id=1, source_target_pairs={{0,16},{8,24},{16,0},{24,8},{1,17},{9,25},{17,1},{25,9},{2,18},{10... | collective-permute-start | bytes 614408 | tf_op jit(solution)/shard_map/ppermute | solution.py:421
  32.4 11.0 %collective-permute-start.6 = (f32[2,25,8,128]{3,2,1,0:T(8,128)S(1)}, f32[2,25,8,128]{3,2,1,0:T(8,128)S(1)}, u32[]{:S(2)}, u32[]{:S(2)}) collective-permute-start(f32[2,25,8,128]{3,2,1,0:T(8,128)S(1)} %get-tuple-element.44), channel_id=1, source_target_pairs={{0,8},{8,0},{16,24},{24,16},{1,9},{9,1},{17,25},{25,17},{2,10},{10... | collective-permute-start | bytes 614408 | tf_op jit(solution)/shard_map/ppermute | solution.py:421
  34.7 9.3 %collective-permute-start.7 = (f32[2,25,8,128]{3,2,1,0:T(8,128)S(1)}, f32[2,25,8,128]{3,2,1,0:T(8,128)S(1)}, u32[]{:S(2)}, u32[]{:S(2)}) collective-permute-start(f32[2,25,8,128]{3,2,1,0:T(8,128)S(1)} %get-tuple-element.45), channel_id=1, source_target_pairs={{0,24},{8,16},{16,8},{24,0},{1,25},{9,17},{17,9},{25,1},{2,26},{10... | collective-permute-start | bytes 614408 | tf_op jit(solution)/shard_map/ppermute | solution.py:421
